TPU v7x, 128 devices: a whole 4x4x4 slice. The times are simulated.
128 devices in a mesh: section: 2 (over z_lo), dp: 16 (over y, z_hi, core), fsdp: 4 (over x).
Axes of the slice: x: 4, y: 4, z: 4 (z_hi: 2, z_lo: 2; z = z_hi * 2 + z_lo), core: 2. Of those that a mesh axis runs over, the one named last changes fastest.
Arguments:
- inputs: bfloat16 [2, 8192, 1024], P(None, ('dp', 'fsdp')), may hold values from -6 to 6
- cotangent: bfloat16 [2, 8192, 1024], P(None, ('dp', 'fsdp')), may hold values from -6 to 6
- lengths: int32 [2, 64, 4], P(None, ('dp', 'fsdp')), may hold values from 1 to 64, 128 in all within a row
- expert_ids: int32 [2, 2, 8192, 4], P('section', None, ('dp', 'fsdp')), may hold values from 0 to 7, all different within a row; in each aligned block of 128 rows (0 to 127, 128 to 255, ..., all dimensions but the last counted through in order) at most 80 rows name the same one
- gain_attn: bfloat16 [2, 1024], P('section', 'fsdp'), may hold values from 0.5 to 1.5
- w_query: bfloat16 [2, 1024, 1024], P('section', 'fsdp'), may hold values from -0.1875 to 0.1875
- w_key: bfloat16 [2, 1024, 512], P('section', 'fsdp'), may hold values from -0.1875 to 0.1875
- w_value: bfloat16 [2, 1024, 512], P('section', 'fsdp'), may hold values from -0.1875 to 0.1875
- w_out: bfloat16 [2, 1024, 1024], P('section', 'fsdp'), may hold values from -0.75 to 0.75
- gain_ffn: bfloat16 [2, 1024], P('section', 'fsdp'), may hold values from 0.5 to 1.5
- w_router: bfloat16 [2, 1024, 8], P('section', 'fsdp'), may hold values from -0.09375 to 0.09375
- w_gate: bfloat16 [2, 1024, 8, 512], P('section', 'fsdp'), may hold values from -0.1875 to 0.1875
- w_up: bfloat16 [2, 1024, 8, 512], P('section', 'fsdp'), may hold values from -0.1875 to 0.1875
- w_down: bfloat16 [2, 8, 512, 1024], P('section', None, None, 'fsdp'), may hold values from -1 to 1
Outputs:
- layer_outputs: bfloat16 [2, 2, 8192, 1024], P('section', None, ('dp', 'fsdp'))
- input_grads: bfloat16 [2, 2, 8192, 1024], P('section', None, ('dp', 'fsdp'))
- grad_gain_attn: float32 [2, 1024], P('section', 'fsdp')
- grad_query: float32 [2, 1024, 1024], P('section', 'fsdp')
- grad_key: float32 [2, 1024, 512], P('section', 'fsdp')
- grad_value: float32 [2, 1024, 512], P('section', 'fsdp')
- grad_out: float32 [2, 1024, 1024], P('section', 'fsdp')
- grad_gain_ffn: float32 [2, 1024], P('section', 'fsdp')
- grad_router: float32 [2, 1024, 8], P('section', 'fsdp')
- grad_gate: float32 [2, 1024, 8, 512], P('section', 'fsdp')
- grad_up: float32 [2, 1024, 8, 512], P('section', 'fsdp')
- grad_down: float32 [2, 8, 512, 1024], P('section', None, None, 'fsdp')
Inputs may be any that keep to these rules, and one draw needn't show every extreme that they name: In each row the 4 lengths sum to 128, and the longest is exactly 64. `expert_ids`: each token names 4 different experts. Among the 128 tokens of one row for one layer (aligned blocks of 128 rows), no expert is named by more than 80 tokens, and in every draw some block has an expert named by exactly 80.
All inputs are finite; a program needn't handle non-finite values.
Results may differ from a plain program's by a relative error of at most 0.03.
Values may be sent and summed in bfloat16 or wider, within the bound.
No kernel may reach another device: no remote copies, remote signals or barrier semaphores. Data moves between devices by JAX's collectives and lax.ppermute only.
A program may use at most 256 MiB of HBM per device.

v0:
```python
import jax
import jax.numpy as jnp
from jax import lax
from jax.sharding import PartitionSpec as P

D = 1024
HEADS = 16
KV_HEADS = 8
HEAD_DIM = 64
EXPERTS = 8
TOP = 4
CAP = 80


epsilon = 1e-05
rope_base = 10000.0


def from_behind(value, axis, steps):
    count = lax.axis_size(axis)
    first, last = (max(0, -steps), min(count, count - steps))
    return lax.ppermute(value, axis, [(source, source + steps) for source in range(first, last)])


def layout(lengths, width):
    ends = jnp.cumsum(lengths, -1)
    places = jnp.arange(width, dtype=jnp.int32)
    segment = jnp.sum((places[None, :, None] >= ends[:, None, :]).astype(jnp.int32), -1)
    starts = ends - lengths
    member = segment[:, :, None] == jnp.arange(lengths.shape[-1], dtype=jnp.int32)[None, None, :]
    position = places[None, :] - jnp.sum(jnp.where(member, starts[:, None, :], 0), -1)
    allowed = (segment[:, :, None] == segment[:, None, :]) & (
        places[None, :, None] >= places[None, None, :]
    )
    return (position, allowed)


def turning(position):
    freqs = rope_base ** (-jnp.arange(HEAD_DIM // 2, dtype=jnp.float32) * 2.0 / HEAD_DIM)
    turned = position.astype(jnp.float32)[..., None] * freqs
    return (jnp.cos(turned)[..., None, :], jnp.sin(turned)[..., None, :])


def rotate(values, cosine, sine):
    half = values.shape[-1] // 2
    first = values[..., :half]
    second = values[..., half:]
    return jnp.concatenate([first * cosine - second * sine, second * cosine + first * sine], -1)


def unrotate(grads, cosine, sine):
    half = grads.shape[-1] // 2
    first = grads[..., :half]
    second = grads[..., half:]
    return jnp.concatenate([first * cosine + second * sine, second * cosine - first * sine], -1)


def routing(routes):
    width, top = routes.shape
    flat = routes.reshape(width * top)
    table = (flat[:, None] == jnp.arange(EXPERTS, dtype=jnp.int32)[None, :]).astype(jnp.int32)
    rank = jnp.sum((jnp.cumsum(table, 0) - table) * table, -1)
    slot = flat * CAP + rank
    match = (slot[:, None] == jnp.arange(EXPERTS * CAP, dtype=jnp.int32)[None, :]).astype(jnp.int32)
    filled = jnp.sum(match, 0)
    source = jnp.sum(match * jnp.arange(width * top, dtype=jnp.int32)[:, None], 0)
    owner = source // top
    picker = table.reshape(width, top, EXPERTS).astype(jnp.float32)
    return (slot, owner, filled, source, picker)


def layer_forward(incoming, cosine, sine, allowed, routes, shards):
    gain_one, query_w, key_w, value_w, out_w, gain_two, router_w, gate_w, up_w, down_w = shards
    source = incoming.astype(jnp.float32)
    width = source.shape[0]
    scale_one = lax.rsqrt(jnp.mean(source * source, -1, keepdims=True) + epsilon)
    gain = lax.all_gather(gain_one, "fsdp", axis=0, tiled=True)
    query_piece = lax.all_gather(query_w, "fsdp", axis=0, tiled=True)
    key_piece = lax.all_gather(key_w, "fsdp", axis=0, tiled=True)
    value_piece = lax.all_gather(value_w, "fsdp", axis=0, tiled=True)
    part = (source * scale_one * gain).astype(jnp.bfloat16)
    normed = part
    query = jnp.dot(part, query_piece, preferred_element_type=jnp.float32)
    keys = jnp.dot(part, key_piece, preferred_element_type=jnp.float32)
    values = jnp.dot(part, value_piece, preferred_element_type=jnp.float32)
    normed, query, keys, values = (normed, query, keys, values)
    query = rotate(query.reshape(width, HEADS, HEAD_DIM), cosine, sine).astype(jnp.bfloat16)
    keys = rotate(keys.reshape(width, KV_HEADS, HEAD_DIM), cosine, sine).astype(jnp.bfloat16)
    values = values.astype(jnp.bfloat16).reshape(width, KV_HEADS, HEAD_DIM)
    grouped = query.reshape(width, KV_HEADS, HEADS // KV_HEADS, HEAD_DIM)
    scores = jnp.einsum(
        "qgjd,kgd->gjqk", grouped, keys, preferred_element_type=jnp.float32
    ) * HEAD_DIM ** (-0.5)
    scores = jnp.where(allowed[None, None], scores, -1e30)
    peak = jnp.max(scores, -1, keepdims=True)
    expo = jnp.exp(scores - peak)
    total = jnp.sum(expo, -1, keepdims=True)
    attend = (expo / total).astype(jnp.bfloat16)
    log_total = peak + jnp.log(total)
    mixed = jnp.einsum("gjqk,kgd->qgjd", attend, values, preferred_element_type=jnp.float32)
    mixed = mixed.reshape(width, HEADS * HEAD_DIM).astype(jnp.bfloat16)
    attended = jnp.dot(
        mixed, lax.all_gather(out_w, "fsdp", axis=0, tiled=True), preferred_element_type=jnp.float32
    )
    hidden = source + attended
    slot, owner, filled, slot_source, picker = routing(routes)
    scale_two = lax.rsqrt(jnp.mean(hidden * hidden, -1, keepdims=True) + epsilon)
    gain = lax.all_gather(gain_two, "fsdp", axis=0, tiled=True)
    router_piece = lax.all_gather(router_w, "fsdp", axis=0, tiled=True)
    gate_piece = lax.all_gather(gate_w, "fsdp", axis=0, tiled=True)
    up_piece = lax.all_gather(up_w, "fsdp", axis=0, tiled=True)
    count = gain.shape[0]
    part = (hidden * scale_two * gain).astype(jnp.bfloat16)
    routed = jnp.where(filled[:, None] > 0, jnp.take(part, owner, axis=0), 0)
    normed_two = part
    routed_all = routed
    logits = jnp.dot(part, router_piece, preferred_element_type=jnp.float32)
    shaped = routed.reshape(EXPERTS, CAP, count)
    gate_acc = jnp.einsum("ecd,def->ecf", shaped, gate_piece, preferred_element_type=jnp.float32)
    up_acc = jnp.einsum("ecd,def->ecf", shaped, up_piece, preferred_element_type=jnp.float32)
    normed_two, routed_all, logits, gate_acc, up_acc = (
        normed_two,
        routed_all,
        logits,
        gate_acc,
        up_acc,
    )
    picked = jnp.sum(logits[:, None, :] * picker, -1)
    top_logit = jnp.max(picked, -1, keepdims=True)
    raised = jnp.exp(picked - top_logit)
    gates = raised / jnp.sum(raised, -1, keepdims=True)
    act = (gate_acc * lax.logistic(gate_acc) * up_acc).astype(jnp.bfloat16)
    expert_out = jnp.einsum(
        "ecf,efd->ecd",
        act,
        lax.all_gather(down_w, "fsdp", axis=2, tiled=True),
        preferred_element_type=jnp.float32,
    )
    expert_low = expert_out.astype(jnp.bfloat16)
    spread = jnp.take(expert_low.reshape(EXPERTS * CAP, D), slot, axis=0).reshape(width, TOP, D)
    result = hidden + jnp.sum(gates[:, :, None] * spread, 1)
    record = (
        incoming,
        normed,
        query,
        keys,
        values,
        log_total,
        mixed,
        hidden,
        normed_two,
        routed_all,
        gates,
        gate_acc,
        up_acc,
        expert_low,
    )
    return (result, record)


def layer_backward(grad_out, record, cosine, sine, allowed, routes, shards):
    gain_one, query_w, key_w, value_w, out_w, gain_two, router_w, gate_w, up_w, down_w = shards
    (
        incoming,
        normed,
        query,
        keys,
        values,
        log_total,
        mixed,
        hidden,
        normed_two,
        routed_all,
        gates,
        gate_acc,
        up_acc,
        expert_low,
    ) = record
    source = incoming.astype(jnp.float32)
    width = source.shape[0]
    slot, owner, filled, slot_source, picker = routing(routes)
    spread = jnp.take(expert_low.reshape(EXPERTS * CAP, D), slot, axis=0).reshape(width, TOP, D)
    grad_gates = jnp.sum(grad_out[:, None, :] * spread, -1)
    grad_picked = gates * (grad_gates - jnp.sum(gates * grad_gates, -1, keepdims=True))
    grad_logits = jnp.sum(grad_picked[:, :, None] * picker, 1).astype(jnp.bfloat16)
    weighted = (gates[:, :, None] * grad_out[:, None, :]).reshape(width * TOP, D)
    grad_expert = jnp.where(filled[:, None] > 0, jnp.take(weighted, slot_source, axis=0), 0.0)
    grad_expert = grad_expert.astype(jnp.bfloat16).reshape(EXPERTS, CAP, D)
    grad_act = jnp.einsum(
        "ecd,efd->ecf",
        grad_expert,
        lax.all_gather(down_w, "fsdp", axis=2, tiled=True),
        preferred_element_type=jnp.float32,
    )
    sigma = lax.logistic(gate_acc)
    act = (gate_acc * sigma * up_acc).astype(jnp.bfloat16)
    grad_gate = (grad_act * up_acc * sigma * (1.0 + gate_acc * (1.0 - sigma))).astype(jnp.bfloat16)
    grad_up = (grad_act * gate_acc * sigma).astype(jnp.bfloat16)
    gain = lax.all_gather(gain_two, "fsdp", axis=0, tiled=True)
    router_piece = lax.all_gather(router_w, "fsdp", axis=0, tiled=True)
    gate_piece = lax.all_gather(gate_w, "fsdp", axis=0, tiled=True)
    up_piece = lax.all_gather(up_w, "fsdp", axis=0, tiled=True)
    count = gain.shape[0]
    back = jnp.einsum("ecf,def->ecd", grad_gate, gate_piece, preferred_element_type=jnp.float32)
    back = back + jnp.einsum("ecf,def->ecd", grad_up, up_piece, preferred_element_type=jnp.float32)
    gathered = jnp.take(back.reshape(EXPERTS * CAP, count), slot, axis=0).reshape(width, TOP, count)
    column = jnp.sum(gathered, 1) + jnp.einsum(
        "le,ce->lc", grad_logits, router_piece, preferred_element_type=jnp.float32
    )
    grad_normed = column
    gain_full = gain.astype(jnp.float32)
    grad_normed_two = grad_normed
    gain_two_full = gain_full
    scale_two = lax.rsqrt(jnp.mean(hidden * hidden, -1, keepdims=True) + epsilon)
    scaled_two = grad_normed_two * gain_two_full
    grad_gain_two = jnp.sum(grad_normed_two * hidden * scale_two, 0)
    grad_hidden = (
        grad_out
        + scale_two * scaled_two
        - hidden * scale_two**3 * jnp.mean(hidden * scaled_two, -1, keepdims=True)
    )
    grad_attn = grad_hidden.astype(jnp.bfloat16)
    grad_mixed = jnp.einsum(
        "ld,cd->lc",
        grad_attn,
        lax.all_gather(out_w, "fsdp", axis=0, tiled=True),
        preferred_element_type=jnp.float32,
    )
    grad_mixed = grad_mixed.astype(jnp.bfloat16).reshape(
        width, KV_HEADS, HEADS // KV_HEADS, HEAD_DIM
    )
    grouped = query.reshape(width, KV_HEADS, HEADS // KV_HEADS, HEAD_DIM)
    scores = jnp.einsum(
        "qgjd,kgd->gjqk", grouped, keys, preferred_element_type=jnp.float32
    ) * HEAD_DIM ** (-0.5)
    scores = jnp.where(allowed[None, None], scores, -1e30)
    attend_full = jnp.exp(scores - log_total)
    attend = attend_full.astype(jnp.bfloat16)
    grad_attend = jnp.einsum(
        "qgjd,kgd->gjqk", grad_mixed, values, preferred_element_type=jnp.float32
    )
    grad_values = jnp.einsum(
        "gjqk,qgjd->kgd", attend, grad_mixed, preferred_element_type=jnp.float32
    )
    grad_values = grad_values.reshape(width, KV_HEADS * HEAD_DIM).astype(jnp.bfloat16)
    inner = jnp.sum(attend_full * grad_attend, -1, keepdims=True)
    grad_scores = (attend_full * (grad_attend - inner)).astype(jnp.bfloat16)
    grad_query = jnp.einsum(
        "gjqk,kgd->qgjd", grad_scores, keys, preferred_element_type=jnp.float32
    ) * HEAD_DIM ** (-0.5)
    grad_keys = jnp.einsum(
        "gjqk,qgjd->kgd", grad_scores, grouped, preferred_element_type=jnp.float32
    ) * HEAD_DIM ** (-0.5)
    grad_query = unrotate(grad_query.reshape(width, HEADS, HEAD_DIM), cosine, sine)
    grad_query = grad_query.reshape(width, HEADS * HEAD_DIM).astype(jnp.bfloat16)
    grad_keys = (
        unrotate(grad_keys, cosine, sine).reshape(width, KV_HEADS * HEAD_DIM).astype(jnp.bfloat16)
    )
    gain = lax.all_gather(gain_one, "fsdp", axis=0, tiled=True)
    query_piece = lax.all_gather(query_w, "fsdp", axis=0, tiled=True)
    key_piece = lax.all_gather(key_w, "fsdp", axis=0, tiled=True)
    value_piece = lax.all_gather(value_w, "fsdp", axis=0, tiled=True)
    column = jnp.einsum("le,ce->lc", grad_query, query_piece, preferred_element_type=jnp.float32)
    column = column + jnp.einsum(
        "le,ce->lc", grad_keys, key_piece, preferred_element_type=jnp.float32
    )
    column = column + jnp.einsum(
        "le,ce->lc", grad_values, value_piece, preferred_element_type=jnp.float32
    )
    grad_normed = column
    gain_full = gain.astype(jnp.float32)
    scale_one = lax.rsqrt(jnp.mean(source * source, -1, keepdims=True) + epsilon)
    scaled_one = grad_normed * gain_full
    grad_gain_one = jnp.sum(grad_normed * source * scale_one, 0)
    grad_input = (
        grad_hidden
        + scale_one * scaled_one
        - source * scale_one**3 * jnp.mean(source * scaled_one, -1, keepdims=True)
    )
    terms = (
        normed,
        grad_query,
        grad_keys,
        grad_values,
        mixed,
        grad_attn,
        normed_two,
        grad_logits,
        routed_all,
        grad_gate,
        grad_up,
        act,
        grad_expert,
        grad_gain_one,
        grad_gain_two,
    )
    return (grad_input, terms)


def cross(left, right):
    return jnp.einsum("std,ste->de", left, right, preferred_element_type=jnp.float32)


def local(
    inputs,
    cotangent,
    lengths,
    expert_ids,
    gain_attn,
    w_query,
    w_key,
    w_value,
    w_out,
    gain_ffn,
    w_router,
    w_gate,
    w_up,
    w_down,
):
    shards = (
        gain_attn[0],
        w_query[0],
        w_key[0],
        w_value[0],
        w_out[0],
        gain_ffn[0],
        w_router[0],
        w_gate[0],
        w_up[0],
        w_down[0],
    )
    section = lax.axis_index("section")
    sections = lax.axis_size("section")
    micro = inputs.shape[0]
    width = inputs.shape[1]
    steps = micro + sections - 1
    received = jnp.zeros(inputs.shape[1:], jnp.bfloat16)
    outputs = jnp.zeros(inputs.shape, jnp.bfloat16)
    records = []
    for step in range(steps):
        index = step - section
        valid = (index >= 0) & (index < micro)
        chosen = jnp.clip(index, 0, micro - 1)
        own = lax.dynamic_index_in_dim(inputs, chosen, 0, keepdims=False)
        incoming = jnp.where(section == 0, own, received)
        spans = lax.dynamic_index_in_dim(lengths, chosen, 0, keepdims=False)
        position, allowed = layout(spans, width)
        cosine, sine = turning(position[0])
        routes = lax.dynamic_index_in_dim(expert_ids[0], chosen, 0, keepdims=False)
        result, record = layer_forward(incoming, cosine, sine, allowed[0], routes, shards)
        result = result.astype(jnp.bfloat16)
        outputs = jnp.where(
            valid, lax.dynamic_update_index_in_dim(outputs, result, chosen, 0), outputs
        )
        records.append(record)
        received = from_behind(result, "section", 1)
    stacked = [jnp.stack(items) for items in zip(*records)]
    returned = jnp.zeros(inputs.shape[1:], jnp.bfloat16)
    input_grads = jnp.zeros(inputs.shape, jnp.bfloat16)
    collected = []
    for step in range(steps):
        index = step - (sections - 1 - section)
        valid = (index >= 0) & (index < micro)
        chosen = jnp.clip(index, 0, micro - 1)
        own = lax.dynamic_index_in_dim(cotangent, chosen, 0, keepdims=False).astype(jnp.float32)
        grad_out = jnp.where(section == sections - 1, own, returned.astype(jnp.float32))
        grad_out = jnp.where(valid, grad_out, 0.0)
        record = tuple(
            (
                lax.dynamic_index_in_dim(item, chosen + section, 0, keepdims=False)
                for item in stacked
            )
        )
        spans = lax.dynamic_index_in_dim(lengths, chosen, 0, keepdims=False)
        position, allowed = layout(spans, width)
        cosine, sine = turning(position[0])
        routes = lax.dynamic_index_in_dim(expert_ids[0], chosen, 0, keepdims=False)
        grad_input, terms = layer_backward(
            grad_out, record, cosine, sine, allowed[0], routes, shards
        )
        rounded = grad_input.astype(jnp.bfloat16)
        input_grads = jnp.where(
            valid, lax.dynamic_update_index_in_dim(input_grads, rounded, chosen, 0), input_grads
        )
        collected.append(terms)
        returned = from_behind(rounded, "section", -1)
    (
        normed_all,
        query_grads,
        key_grads,
        value_grads,
        mixed_all,
        attn_grads,
        normed_two_all,
        logit_grads,
        routed_all,
        gate_grads,
        up_grads,
        act_all,
        expert_grads,
        gain_one_grads,
        gain_two_grads,
    ) = [jnp.stack(items) for items in zip(*collected)]
    routed_shaped = routed_all.reshape(steps, EXPERTS, CAP, D)
    local_gain_one = jnp.sum(gain_one_grads, 0)
    local_query = cross(normed_all, query_grads)
    local_key = cross(normed_all, key_grads)
    local_value = cross(normed_all, value_grads)
    local_out = cross(mixed_all, attn_grads)
    local_gain_two = jnp.sum(gain_two_grads, 0)
    local_router = cross(normed_two_all, logit_grads)
    local_gate = jnp.einsum(
        "secd,secf->def", routed_shaped, gate_grads, preferred_element_type=jnp.float32
    )
    local_up = jnp.einsum(
        "secd,secf->def", routed_shaped, up_grads, preferred_element_type=jnp.float32
    )
    local_down = jnp.einsum(
        "secf,secd->efd", act_all, expert_grads, preferred_element_type=jnp.float32
    )
    shares = (
        lax.psum_scatter(
            local_gain_one.astype(jnp.bfloat16), "fsdp", scatter_dimension=0, tiled=True
        ).astype(jnp.float32),
        lax.psum_scatter(
            local_query.astype(jnp.bfloat16), "fsdp", scatter_dimension=0, tiled=True
        ).astype(jnp.float32),
        lax.psum_scatter(
            local_key.astype(jnp.bfloat16), "fsdp", scatter_dimension=0, tiled=True
        ).astype(jnp.float32),
        lax.psum_scatter(
            local_value.astype(jnp.bfloat16), "fsdp", scatter_dimension=0, tiled=True
        ).astype(jnp.float32),
        lax.psum_scatter(
            local_out.astype(jnp.bfloat16), "fsdp", scatter_dimension=0, tiled=True
        ).astype(jnp.float32),
        lax.psum_scatter(
            local_gain_two.astype(jnp.bfloat16), "fsdp", scatter_dimension=0, tiled=True
        ).astype(jnp.float32),
        lax.psum_scatter(
            local_router.astype(jnp.bfloat16), "fsdp", scatter_dimension=0, tiled=True
        ).astype(jnp.float32),
        lax.psum_scatter(
            local_gate.astype(jnp.bfloat16), "fsdp", scatter_dimension=0, tiled=True
        ).astype(jnp.float32),
        lax.psum_scatter(
            local_up.astype(jnp.bfloat16), "fsdp", scatter_dimension=0, tiled=True
        ).astype(jnp.float32),
        lax.psum_scatter(
            local_down.astype(jnp.bfloat16), "fsdp", scatter_dimension=2, tiled=True
        ).astype(jnp.float32),
    )
    totals = (
        lax.psum(shares[0].astype(jnp.bfloat16), "dp").astype(jnp.float32),
        lax.psum(shares[1].astype(jnp.bfloat16), "dp").astype(jnp.float32),
        lax.psum(shares[2].astype(jnp.bfloat16), "dp").astype(jnp.float32),
        lax.psum(shares[3].astype(jnp.bfloat16), "dp").astype(jnp.float32),
        lax.psum(shares[4].astype(jnp.bfloat16), "dp").astype(jnp.float32),
        lax.psum(shares[5].astype(jnp.bfloat16), "dp").astype(jnp.float32),
        lax.psum(shares[6].astype(jnp.bfloat16), "dp").astype(jnp.float32),
        lax.psum(shares[7].astype(jnp.bfloat16), "dp").astype(jnp.float32),
        lax.psum(shares[8].astype(jnp.bfloat16), "dp").astype(jnp.float32),
        lax.psum(shares[9].astype(jnp.bfloat16), "dp").astype(jnp.float32),
    )
    return (
        outputs[None],
        input_grads[None],
        totals[0][None],
        totals[1][None],
        totals[2][None],
        totals[3][None],
        totals[4][None],
        totals[5][None],
        totals[6][None],
        totals[7][None],
        totals[8][None],
        totals[9][None],
    )


def solution(mesh):
    return jax.shard_map(
        local,
        mesh=mesh,
        in_specs=(
            P(None, ("dp", "fsdp"), None),
            P(None, ("dp", "fsdp"), None),
            P(None, ("dp", "fsdp"), None),
            P("section", None, ("dp", "fsdp"), None),
            P("section", "fsdp"),
            P("section", "fsdp", None),
            P("section", "fsdp", None),
            P("section", "fsdp", None),
            P("section", "fsdp", None),
            P("section", "fsdp"),
            P("section", "fsdp", None),
            P("section", "fsdp", None, None),
            P("section", "fsdp", None, None),
            P("section", None, None, "fsdp"),
        ),
        out_specs=(
            P("section", None, ("dp", "fsdp"), None),
            P("section", None, ("dp", "fsdp"), None),
            P("section", "fsdp"),
            P("section", "fsdp", None),
            P("section", "fsdp", None),
            P("section", "fsdp", None),
            P("section", "fsdp", None),
            P("section", "fsdp"),
            P("section", "fsdp", None),
            P("section", "fsdp", None, None),
            P("section", "fsdp", None, None),
            P("section", None, None, "fsdp"),
        ),
        check_vma=False,
    )
```

profile of v0, /device:TPU:1, one launch (start us, length us, event | category | flops | bytes accessed | tf_op | source)
XLA Modules:
  0.0 1288.5 jit_solution(15532662000158451063)
XLA Ops:
  31.5 8.5 all-gather
  41.2 5.3 all-gather.5
  46.5 9.5 all-gather.6
  81.2 15.0 %all-gather.22.cloned.1.call-done = bf16[1,1024,1024]{2,1,0:T(8,128)(2,1)} async-done(((bf16[1,256,1024]{2,1,0:T(8,128)(2,1)}), bf16[1,1024,1024]{2,1,0:T(8,128)(2,1)}) %all-gather.22.cloned.1.call-update) | async-done | bytes 2097168 | tf_op jit(solution)/shard_map/all_gather | solution.py:78
  100.8 27.7 %all-gather.24.cloned.1.call-done = bf16[1,1024,1024]{2,1,0:T(8,128)(2,1)} async-done(((bf16[1,256,1024]{2,1,0:T(8,128)(2,1)}), bf16[1,1024,1024]{2,1,0:T(8,128)(2,1)}) %all-gather.24.cloned.1.call-update) | async-done | bytes 2097168 | tf_op jit(solution)/shard_map/all_gather | solution.py:103
  134.3 79.4 %all-gather.28.cloned.1.call-done = bf16[1,1024,8,512]{3,1,2,0:T(8,128)(2,1)} async-done(((bf16[1,256,8,512]{3,1,2,0:T(8,128)(2,1)}), bf16[1,1024,8,512]{3,1,2,0:T(8,128)(2,1)}) %all-gather.28.cloned.1.call-update) | async-done | bytes 8388624 | tf_op jit(solution)/shard_map/all_gather | solution.py:111
  213.7 6.0 fusion.22
  219.7 80.2 %all-gather.26.cloned.1.call-done = bf16[1,1024,8,512]{3,1,2,0:T(8,128)(2,1)} async-done(((bf16[1,256,8,512]{3,1,2,0:T(8,128)(2,1)}), bf16[1,1024,8,512]{3,1,2,0:T(8,128)(2,1)}) %all-gather.26.cloned.1.call-update) | async-done | bytes 8388624 | tf_op jit(solution)/shard_map/all_gather | solution.py:110
  299.9 6.1 fusion.34
  306.0 83.1 %all-gather.30.cloned.1.call-done = bf16[1,8,512,1024]{3,2,1,0:T(8,128)(2,1)} async-done(((bf16[1,8,512,256]{3,2,1,0:T(8,128)(2,1)}), bf16[1,8,512,1024]{3,2,1,0:T(8,128)(2,1)}) %all-gather.30.cloned.1.call-update) | async-done | bytes 8388624 | tf_op jit(solution)/shard_map/all_gather | solution.py:136
  389.1 5.4 fusion.92
  424.3 5.1 fusion.20
  470.7 5.1 fusion.18
  498.1 9.0 fusion.142
  507.1 5.3 fusion.16
  566.2 7.4 fusion.133
  573.6 6.5 fusion.14
  580.1 6.1 fusion.86
  629.4 7.4 fusion.124
  636.8 6.5 fusion.12
  643.4 6.1 fusion.89
  694.2 5.7 fusion.36
  701.2 8.0 fusion.37
  721.9 6.1 reduce-scatter.13.cloned.1.call-done
  728.0 33.0 %reduce-scatter.9.cloned.1.call-done = bf16[256,1024]{1,0:T(8,128)(2,1)} async-done(((bf16[1024,1024]{1,0:T(8,128)(2,1)}), bf16[256,1024]{1,0:T(8,128)(2,1)}) %reduce-scatter.9.cloned.1.call-update) | async-done | bytes 524304 | tf_op jit(solution)/shard_map/reduce_scatter | solution.py:425
  761.0 31.9 %reduce-scatter.15.cloned.1.call-done = bf16[256,1024]{1,0:T(8,128)(2,1)} async-done(((bf16[1024,1024]{1,0:T(8,128)(2,1)}), bf16[256,1024]{1,0:T(8,128)(2,1)}) %reduce-scatter.15.cloned.1.call-update) | async-done | bytes 524304 | tf_op jit(solution)/shard_map/reduce_scatter | solution.py:434
  793.0 82.6 %reduce-scatter.19.cloned.1.call-done = bf16[256,8,512]{0,2,1:T(8,128)(2,1)} async-done(((bf16[1024,8,512]{0,2,1:T(8,128)(2,1)}), bf16[256,8,512]{0,2,1:T(8,128)(2,1)}) %reduce-scatter.19.cloned.1.call-update) | async-done | bytes 2097168 | tf_op jit(solution)/shard_map/reduce_scatter | solution.py:443
  875.6 82.7 %reduce-scatter.21.cloned.1.call-done = bf16[256,8,512]{0,2,1:T(8,128)(2,1)} async-done(((bf16[1024,8,512]{0,2,1:T(8,128)(2,1)}), bf16[256,8,512]{0,2,1:T(8,128)(2,1)}) %reduce-scatter.21.cloned.1.call-update) | async-done | bytes 2097168 | tf_op jit(solution)/shard_map/reduce_scatter | solution.py:446
  958.3 82.6 %reduce-scatter.23.cloned.1.call-done = bf16[8,512,256]{2,1,0:T(8,128)(2,1)} async-done(((bf16[8,512,1024]{2,1,0:T(8,128)(2,1)}), bf16[8,512,256]{2,1,0:T(8,128)(2,1)}) %reduce-scatter.23.cloned.1.call-update) | async-done | bytes 2097168 | tf_op jit(solution)/shard_map/reduce_scatter | solution.py:449
  1057.5 6.9 all-reduce.4
  1065.9 36.1 %all-reduce.2 = (bf16[1,256]{1,0:T(2,128)(2,1)S(1)}, bf16[1,256]{1,0:T(2,128)(2,1)S(1)}, bf16[1,256,8]{1,2,0:T(8,128)(2,1)S(1)}) all-reduce(bf16[1,256]{1,0:T(2,128)(2,1)S(1)} %broadcast_in_dim.485, bf16[1,256]{1,0:T(2,128)(2,1)S(1)} %broadcast_in_dim.495, ...), channel_id=1, replica_groups=mesh['section'=2,'dp'=16,'fsdp'=4] {'dp'}, use_global_device_ids=true, to_apply=%region_103.108 | all-reduce | flops 2560 | bytes 10240 | tf_op jit(solution)/shard_map/psum | solution.py:454
  1103.8 162.0 %all-reduce.7.cloned.1.call-done = (bf16[1,256,8,512]{1,3,2,0:T(8,128)(2,1)}, bf16[1,256,8,512]{1,3,2,0:T(8,128)(2,1)}, bf16[1,256,1024]{2,1,0:T(8,128)(2,1)}, b...) async-done(((bf16[1,256,8,512]{1,3,2,0:T(8,128)(2,1)}, ...) | async-done | bytes 7864336 | tf_op jit(solution)/shard_map/psum | solution.py:461
  (1048 shorter events, 340.8 us)
Async XLA Ops:
  7.2 70.1 %all-gather.18.cloned.1.call-start = ((), (), s32[]{:S(2)}) async-start(), calls=%async_computation.16 | async-start | bytes 1310720 | tf_op jit(solution)/shard_map/all_gather | solution.py:80
  7.9 71.2 %all-gather.20.cloned.1.call-start = ((), (), s32[]{:S(2)}) async-start(), calls=%async_computation.17 | async-start | bytes 1310720 | tf_op jit(solution)/shard_map/all_gather | solution.py:79
  8.7 87.5 %all-gather.22.cloned.1.call-start = ((), (), s32[]{:S(2)}) async-start(), calls=%async_computation.18 | async-start | bytes 2621440 | tf_op jit(solution)/shard_map/all_gather | solution.py:78
  9.4 119.1 %all-gather.24.cloned.1.call-start = ((), (), s32[]{:S(2)}) async-start(), calls=%async_computation.19 | async-start | bytes 2621440 | tf_op jit(solution)/shard_map/all_gather | solution.py:103
  10.0 203.7 %all-gather.28.cloned.1.call-start = ((), (), s32[]{:S(2)}) async-start(), calls=%async_computation.21 | async-start | bytes 10485760 | tf_op jit(solution)/shard_map/all_gather | solution.py:111
  13.6 286.3 %all-gather.26.cloned.1.call-start = ((), (), s32[]{:S(2)}) async-start(), calls=%async_computation.20 | async-start | bytes 10485760 | tf_op jit(solution)/shard_map/all_gather | solution.py:110
  17.3 371.8 %all-gather.30.cloned.1.call-start = ((), (), s32[]{:S(2)}) async-start(), calls=%async_computation.22 | async-start | bytes 10485760 | tf_op jit(solution)/shard_map/all_gather | solution.py:136
  18.0 42.0 %copy-start.97 = (bf16[2,128,1024]{2,1,0:T(8,128)(2,1)S(1)}, bf16[2,128,1024]{2,1,0:T(8,128)(2,1)}, u32[]{:S(2)}) copy-start(bf16[2,128,1024]{2,1,0:T(8,128)(2,1)} %param.23) | copy-start | bytes 1572868
  18.0 703.8 %reduce-scatter.11.cloned.1.call-start = ((), (), s32[]{:S(2)}) async-start(), calls=%async_computation.9 | async-start | bytes 1310720 | tf_op jit(solution)/shard_map/reduce_scatter | solution.py:428
  18.2 41.8 %copy-start.197 = (s32[1,1,128,4]{2,3,1,0:T(4,128)}, s32[1,1,128,4]{2,3,1,0:T(4,128)S(1)}, u32[]{:S(2)}) copy-start(s32[1,1,128,4]{2,3,1,0:T(4,128)S(1)} %get-tuple-element.204) | copy-start | bytes 6148
  18.2 42.5 %copy-start.195 = (s32[1,1,128,4]{2,3,1,0:T(4,128)}, s32[1,1,128,4]{2,3,1,0:T(4,128)S(1)}, u32[]{:S(2)}) copy-start(s32[1,1,128,4]{2,3,1,0:T(4,128)S(1)} %get-tuple-element.208) | copy-start | bytes 6148
  46.4 87.6 %copy-start.220 = (pred[640]{0:T(1024)(128)(4,1)}, pred[640]{0:T(1024)(128)(4,1)S(1)}, u32[]{:S(2)}) copy-start(pred[640]{0:T(1024)(128)(4,1)S(1)} %get-tuple-element.138) | copy-start | bytes 1924
  56.0 471.7 %copy-start.124 = (bf16[1,1024,8]{1,2,0:T(8,128)(2,1)}, bf16[1,1024,8]{1,2,0:T(8,128)(2,1)S(1)}, u32[]{:S(2)}) copy-start(bf16[1,1024,8]{1,2,0:T(8,128)(2,1)S(1)} %all-gather.6) | copy-start | bytes 49156
  65.1 63.4 %copy-start.65 = (bf16[1,128,1024]{2,1,0:T(8,128)(2,1)}, bf16[1,128,1024]{2,1,0:T(8,128)(2,1)S(1)}, u32[]{:S(2)}) copy-start(bf16[1,128,1024]{2,1,0:T(8,128)(2,1)S(1)} %get-tuple-element.141) | copy-start | bytes 786436
  69.8 64.2 %copy-start.230 = (pred[640]{0:T(1024)(128)(4,1)}, pred[640]{0:T(1024)(128)(4,1)S(1)}, u32[]{:S(2)}) copy-start(pred[640]{0:T(1024)(128)(4,1)S(1)} %broadcast_compare_fusion.5) | copy-start | bytes 1924
  77.1 336.9 %copy-start.179 = (f32[128,32]{0,1:T(8,128)}, f32[128,32]{0,1:T(8,128)S(1)}, u32[]{:S(2)}) copy-start(f32[128,32]{0,1:T(8,128)S(1)} %get-tuple-element.236) | copy-start | bytes 49156
  130.6 273.5 %copy-start.37 = (f32[128,1024]{1,0:T(8,128)}, f32[128,1024]{1,0:T(8,128)S(1)}, u32[]{:S(2)}) copy-start(f32[128,1024]{1,0:T(8,128)S(1)} %get-tuple-element.264) | copy-start | bytes 1572868
  133.6 86.1 %copy-start.51 = (bf16[640,1024]{1,0:T(8,128)(2,1)}, bf16[640,1024]{1,0:T(8,128)(2,1)S(1)}, u32[]{:S(2)}) copy-start(bf16[640,1024]{1,0:T(8,128)(2,1)S(1)} %gather_fusion) | copy-start | bytes 3932164
  299.9 89.2 %copy-start.56 = (f32[8,80,512]{2,1,0:T(8,128)S(1)}, f32[8,80,512]{2,1,0:T(8,128)}, u32[]{:S(2)}) copy-start(f32[8,80,512]{2,1,0:T(8,128)} %fusion.22) | copy-start | bytes 3932164
  404.3 7.4 collective-permute-start
  446.8 7.5 collective-permute-start.1
  542.2 11.7 collective-permute-start.2
  610.0 7.8 collective-permute-start.3
  675.3 52.7 %reduce-scatter.13.cloned.1.call-start = ((), (), s32[]{:S(2)}) async-start(), calls=%async_computation.10 | async-start | bytes 1310720 | tf_op jit(solution)/shard_map/reduce_scatter | solution.py:431
  677.5 83.5 %reduce-scatter.9.cloned.1.call-start = ((), (), s32[]{:S(2)}) async-start(), calls=%async_computation.8 | async-start | bytes 2621440 | tf_op jit(solution)/shard_map/reduce_scatter | solution.py:425
  681.4 111.6 %reduce-scatter.15.cloned.1.call-start = ((), (), s32[]{:S(2)}) async-start(), calls=%async_computation.11 | async-start | bytes 2621440 | tf_op jit(solution)/shard_map/reduce_scatter | solution.py:434
  686.3 189.3 %reduce-scatter.19.cloned.1.call-start = ((), (), s32[]{:S(2)}) async-start(), calls=%async_computation.13 | async-start | bytes 10485760 | tf_op jit(solution)/shard_map/reduce_scatter | solution.py:443
  700.0 258.3 %reduce-scatter.21.cloned.1.call-start = ((), (), s32[]{:S(2)}) async-start(), calls=%async_computation.14 | async-start | bytes 10485760 | tf_op jit(solution)/shard_map/reduce_scatter | solution.py:446
  709.3 331.6 %reduce-scatter.23.cloned.1.call-start = ((), (), s32[]{:S(2)}) async-start(), calls=%async_computation.15 | async-start | bytes 10485760 | tf_op jit(solution)/shard_map/reduce_scatter | solution.py:449
  718.8 347.1 %reduce-scatter.17.cloned.1.call-start = ((), (), s32[]{:S(2)}) async-start(), calls=%async_computation.12 | async-start | bytes 20480 | tf_op jit(solution)/shard_map/reduce_scatter | solution.py:440
  721.8 544.0 %all-reduce.7.cloned.1.call-start = ((), (), s32[]{:S(2)}) async-start(), calls=%async_computation.23 | async-start | bytes 15728640 | tf_op jit(solution)/shard_map/psum | solution.py:461
  1065.9 202.2 %copy-start.149 = (bf16[1,2,128,1024]{3,2,1,0:T(8,128)(2,1)}, bf16[1,2,128,1024]{3,2,1,0:T(8,128)(2,1)S(1)}, u32[]{:S(2)}) copy-start(bf16[1,2,128,1024]{3,2,1,0:T(8,128)(2,1)S(1)} %bitcast_dynamic-update-slice_fusion) | copy-start | bytes 1572868
  (279 other events, 961.3 us)
Sparse Core Ops, SparseCore 0:
  9.7 26.1 all-gather.17
  37.6 24.4 all-gather.19
  63.7 32.3 all-gather.21
  97.7 30.7 all-gather.23
  130.5 83.0 all-gather.27
  215.8 84.0 all-gather.25
  301.5 87.4 all-gather.29
  675.5 26.1 reduce-scatter.10
  704.8 23.2 reduce-scatter.12
  730.3 30.7 reduce-scatter.8
  763.6 29.3 reduce-scatter.14
  795.3 80.2 reduce-scatter.18
  878.0 80.2 reduce-scatter.20
  960.6 80.1 reduce-scatter.22
  1043.6 17.6 reduce-scatter.16
  1064.5 201.2 all-reduce.6
where the time goes:
time: 1300 us; the launch traced here: 1290 us
  waiting for transfers between devices  780 us (60%)
  matrix products  154 us (12%)
  local copies, waits for them, and re-layouts  148 us (11%)
  other arithmetic  110 us (8%)
  blocking collectives  66.4 us (5%)
  between operations  19.4 us (1%)
    psum x1, waiting for transfers between devices, local(): lax.psum(shares[7].astype(jnp.bfloat16), 'dp').astype(jnp.float32)  162 us
    all_gather x1, waiting for transfers between devices, layer_forward(): lax.all_gather(down_w, 'fsdp', axis=2, tiled=True)  83.1 us
    reduce_scatter x1, waiting for transfers between devices, local(): lax.psum_scatter(local_up.astype(jnp.bfloat16), 'fsdp', scatter_dimension...  82.7 us
    reduce_scatter x1, waiting for transfers between devices, local(): lax.psum_scatter(local_gate.astype(jnp.bfloat16), 'fsdp', scatter_dimensi...  82.6 us
    reduce_scatter x1, waiting for transfers between devices, local(): lax.psum_scatter(local_down.astype(jnp.bfloat16), 'fsdp', scatter_dimensi...  82.6 us
    all_gather x1, waiting for transfers between devices, layer_forward(): gate_piece = lax.all_gather(gate_w, 'fsdp', axis=0, tiled=True)  80.2 us
    all_gather x1, waiting for transfers between devices, layer_forward(): up_piece = lax.all_gather(up_w, 'fsdp', axis=0, tiled=True)  79.4 us
    unnamed x591, local copies, waits for them, and re-layouts  55.7 us
  transfers between devices with their start and end apart: 20, of which 15 were waited for; matrix products, arithmetic and copies ran while one was open for 10% of the time, Pallas kernels for 0%

commit v1 on v0

v1 whole, which is shorter than its diff:
```python
import jax
import jax.numpy as jnp
from jax import lax
from jax.sharding import Mesh, PartitionSpec as P

D = 1024
HEAD_DIM = 64
GROUPS = 4
FF = 512
OWN = 4
ROW = 128
epsilon = 1e-05
rope_base = 10000.0
bf16 = jnp.bfloat16
f32 = jnp.float32


def pp(value, axis, step):
    count = lax.axis_size(axis)
    return lax.ppermute(value, axis, [(i, (i + step) % count) for i in range(count)])


def involute(value, dim, index):
    size = value.shape[dim] // 4
    blocks = [lax.slice_in_dim(value, i * size, (i + 1) * size, axis=dim) for i in (3, 2, 1, 0)]
    double = jnp.concatenate(blocks + blocks[:3], dim)
    return lax.dynamic_slice_in_dim(double, (3 - index) * size, 4 * size, dim)


def gather4(value, axis):
    half = value.shape[0] // 2
    left = pp(value, axis, 1)
    right = pp(value, axis, -1)
    far = jnp.concatenate([pp(left[:half], axis, 1), pp(right[half:], axis, -1)], 0)
    return [value, left, far, right]


def plus(first, second):
    return (first.astype(f32) + second.astype(f32)).astype(bf16)


def scatter4(blocks, axis):
    here, behind, far, ahead = blocks
    half = here.shape[0] // 2
    far_up = pp(far[:half], axis, 1)
    far_down = pp(far[half:], axis, -1)
    up_late = pp(ahead[half:], axis, 1)
    down_early = pp(behind[:half], axis, -1)
    up_early = pp(plus(ahead[:half], far_up), axis, 1)
    down_late = pp(plus(behind[half:], far_down), axis, -1)
    first = (here[:half].astype(f32) + up_early.astype(f32) + down_early.astype(f32)).astype(bf16)
    second = (here[half:].astype(f32) + up_late.astype(f32) + down_late.astype(f32)).astype(bf16)
    return jnp.concatenate([first, second], 0)


def other(value):
    return pp(value, "core", 1)


def both(value):
    return jnp.concatenate([value, other(value)], 0)


def flip(value):
    half = value.shape[0] // 2
    return jnp.concatenate([value[half:], value[:half]], 0)


def dot(left, right):
    return jnp.dot(left, right, preferred_element_type=f32)


def dot_t(left, right):
    return lax.dot_general(left, right, (((1,), (1,)), ((), ())), preferred_element_type=f32)


def t_dot(left, right):
    return lax.dot_general(left, right, (((0,), (0,)), ((), ())), preferred_element_type=f32)


def inverse_root(value):
    return lax.rsqrt(jnp.mean(value * value, -1, keepdims=True) + epsilon)


def layout(lengths):
    ends = jnp.cumsum(lengths, -1)
    places = jnp.arange(ROW, dtype=jnp.int32)
    segment = jnp.sum((places[None, :, None] >= ends[:, None, :]).astype(jnp.int32), -1)
    starts = ends - lengths
    member = segment[:, :, None] == jnp.arange(lengths.shape[-1], dtype=jnp.int32)
    position = places[None, :] - jnp.sum(jnp.where(member, starts[:, None, :], 0), -1)
    allowed = (segment[:, :, None] == segment[:, None, :]) & (
        places[None, :, None] >= places[None, None, :]
    )
    freqs = rope_base ** (-jnp.arange(HEAD_DIM // 2, dtype=f32) * 2.0 / HEAD_DIM)
    turned = position.reshape(-1).astype(f32)[:, None] * freqs
    return allowed, jnp.cos(turned)[:, None, :], jnp.sin(turned)[:, None, :]


def rotate(values, cosine, sine):
    shaped = values.reshape(values.shape[0], -1, HEAD_DIM)
    first, second = shaped[..., : HEAD_DIM // 2], shaped[..., HEAD_DIM // 2 :]
    turned = jnp.concatenate([first * cosine - second * sine, second * cosine + first * sine], -1)
    return turned.reshape(values.shape)


def attention_scores(query, keys, allowed):
    rows = query.shape[0] // ROW
    grouped = query.reshape(rows, ROW, GROUPS, 2, HEAD_DIM)
    shaped = keys.reshape(rows, ROW, GROUPS, HEAD_DIM)
    scores = jnp.einsum("rqgjd,rkgd->rgjqk", grouped, shaped, preferred_element_type=f32)
    scores = jnp.where(allowed[:, None, None], scores * HEAD_DIM**-0.5, -1e30)
    expo = jnp.exp(scores - jnp.max(scores, -1, keepdims=True))
    return grouped, shaped, expo / jnp.sum(expo, -1, keepdims=True)


def attention_forward(x, gain, w_qkv, w_out, place):
    allowed, cosine, sine = place
    source = x.astype(f32)
    normed = (source * inverse_root(source) * gain).astype(bf16)
    qkv = dot(normed, w_qkv)
    query = rotate(qkv[:, :512], cosine, sine).astype(bf16)
    keys = rotate(qkv[:, 512:768], cosine, sine).astype(bf16)
    values = qkv[:, 768:].astype(bf16)
    _, _, attend = attention_scores(query, keys, allowed)
    rows = x.shape[0] // ROW
    mixed = jnp.einsum(
        "rgjqk,rkgd->rqgjd",
        attend.astype(bf16),
        values.reshape(rows, ROW, GROUPS, HEAD_DIM),
        preferred_element_type=f32,
    )
    mixed = mixed.reshape(x.shape[0], 512).astype(bf16)
    return normed, query, keys, values, mixed, dot(mixed, w_out).astype(bf16)


def expert_forward(x, part, gain, w_router, w_gate, w_up, w_down, chosen):
    hidden = x.astype(f32) + part[0].astype(f32) + flip(part[1]).astype(f32)
    normed = (hidden * inverse_root(hidden) * gain).astype(bf16)
    logits = dot(normed, w_router)
    masked = jnp.where(chosen > 0, logits, -1e30)
    raised = jnp.where(chosen > 0, jnp.exp(masked - jnp.max(masked, -1, keepdims=True)), 0.0)
    gates = (raised / jnp.sum(raised, -1, keepdims=True))[:, :OWN]
    gate_in = [dot(normed, w_gate[e]) for e in range(OWN)]
    up_in = [dot(normed, w_up[e]) for e in range(OWN)]
    acted = [
        (gates[:, e, None] * gate_in[e] * lax.logistic(gate_in[e]) * up_in[e]).astype(bf16)
        for e in range(OWN)
    ]
    total = sum(dot(acted[e], w_down[e]) for e in range(OWN)).astype(bf16)
    gate_in = [v.astype(bf16) for v in gate_in]
    up_in = [v.astype(bf16) for v in up_in]
    return hidden, normed, gates, gate_in, up_in, acted, total


def expert_backward(grad, moe, record, w_router, w_gate, w_up, w_down, weights):
    hidden, normed, gates, gate_in, up_in, acted = record
    inner = jnp.sum(grad.astype(f32) * moe, -1, keepdims=True)
    total = 0.0
    logit_grads, gate_grads, up_grads = [], [], []
    for e in range(OWN):
        a, b = gate_in[e].astype(f32), up_in[e].astype(f32)
        sigma = lax.logistic(a)
        wide = dot_t(grad, w_down[e])
        slope = jnp.sum(wide * a * sigma * b, -1, keepdims=True)
        logit_grads.append(gates[:, e, None] * (slope - inner))
        wide = wide * gates[:, e, None]
        gate_grads.append((wide * b * sigma * (1.0 + a * (1.0 - sigma))).astype(bf16))
        up_grads.append((wide * a * sigma).astype(bf16))
        total = total + dot_t(gate_grads[e], w_gate[e]) + dot_t(up_grads[e], w_up[e])
    logit_grads = jnp.concatenate(logit_grads, -1).astype(bf16)
    total = (total + dot_t(logit_grads, w_router[:, :OWN])).astype(bf16)
    if not weights:
        return total, None
    grads = (
        t_dot(normed, logit_grads),
        [t_dot(normed, gate_grads[e]).astype(bf16) for e in range(OWN)],
        [t_dot(normed, up_grads[e]).astype(bf16) for e in range(OWN)],
        [t_dot(acted[e], grad).astype(bf16) for e in range(OWN)],
    )
    return total, grads


def norm_backward(grad_normed, value, gain):
    scale = inverse_root(value)
    scaled = grad_normed * gain
    gain_grad = jnp.sum((grad_normed * value * scale)[:256], 0)
    return scale * scaled - value * scale**3 * jnp.mean(value * scaled, -1, keepdims=True), gain_grad


def attention_backward(grad_hidden, record, w_qkv, w_out, place, weights):
    allowed, cosine, sine = place
    normed, query, keys, values, mixed = record
    width = query.shape[0]
    rows = width // ROW
    grad_attn = grad_hidden.astype(bf16)
    grad_mixed = dot_t(grad_attn, w_out).astype(bf16).reshape(rows, ROW, GROUPS, 2, HEAD_DIM)
    grouped, shaped, attend = attention_scores(query, keys, allowed)
    shaped_values = values.reshape(rows, ROW, GROUPS, HEAD_DIM)
    grad_attend = jnp.einsum("rqgjd,rkgd->rgjqk", grad_mixed, shaped_values, preferred_element_type=f32)
    grad_values = jnp.einsum("rgjqk,rqgjd->rkgd", attend.astype(bf16), grad_mixed, preferred_element_type=f32)
    inner = jnp.sum(attend * grad_attend, -1, keepdims=True)
    grad_scores = (attend * (grad_attend - inner) * HEAD_DIM**-0.5).astype(bf16)
    grad_query = jnp.einsum("rgjqk,rkgd->rqgjd", grad_scores, shaped, preferred_element_type=f32)
    grad_keys = jnp.einsum("rgjqk,rqgjd->rkgd", grad_scores, grouped, preferred_element_type=f32)
    grad_query = rotate(grad_query.reshape(width, 512), cosine, -sine)
    grad_keys = rotate(grad_keys.reshape(width, 256), cosine, -sine)
    grad_qkv = jnp.concatenate([grad_query, grad_keys, grad_values.reshape(width, 256)], -1).astype(bf16)
    total = dot_t(grad_qkv, w_qkv).astype(bf16)
    if not weights:
        return total, None
    return total, (t_dot(normed, grad_qkv).astype(bf16), t_dot(mixed, grad_attn).astype(bf16))


def local(
    inputs, cotangent, lengths, expert_ids, gain_attn, w_query, w_key, w_value, w_out,
    gain_ffn, w_router, w_gate, w_up, w_down,
):
    section = lax.axis_index("section")
    x_at, y_at, core = lax.axis_index("x"), lax.axis_index("y"), lax.axis_index("core")

    q_own = lax.dynamic_index_in_dim(w_query[0].reshape(256, 4, 2, 128), core, 2, False).reshape(256, 512)
    k_own = lax.dynamic_index_in_dim(w_key[0].reshape(256, 4, 2, 64), core, 2, False).reshape(256, 256)
    v_own = lax.dynamic_index_in_dim(w_value[0].reshape(256, 4, 2, 64), core, 2, False).reshape(256, 256)
    out_own = lax.dynamic_slice_in_dim(w_out[0], core * 128, 128, 0)
    small = jnp.concatenate([gain_attn[0][None], gain_ffn[0][None], w_router[0].T], 0)
    small = jnp.concatenate([small, jnp.zeros((6, 256), bf16)], 0)
    small_all = jnp.concatenate(gather4(small, "x"), -1)
    qkv_all = jnp.concatenate(gather4(jnp.concatenate([q_own, k_own, v_own], -1), "x"), 0)
    out_all = involute(jnp.concatenate(gather4(out_own, "x"), 0), 0, x_at)
    out_all = involute(out_all, 1, x_at)
    gate_own = involute(
        jnp.swapaxes(lax.dynamic_slice_in_dim(w_gate[0], core * OWN, OWN, 1), 0, 1), 0, y_at
    )
    up_own = involute(
        jnp.swapaxes(lax.dynamic_slice_in_dim(w_up[0], core * OWN, OWN, 1), 0, 1), 0, y_at
    )
    down_own = involute(lax.dynamic_slice_in_dim(w_down[0], core * OWN, OWN, 0), 0, y_at)
    pair = jnp.stack([gate_own[0], up_own[0]], 0)
    pair = jnp.concatenate(gather4(pair, "x"), 1)
    pairs = gather4(pair, "y")
    gate_all = [v[0] for v in pairs]
    up_all = [v[1] for v in pairs]
    down_pieces = gather4(down_own, "x")
    down_all = [jnp.concatenate([v[e] for v in down_pieces], -1) for e in range(OWN)]
    gain_one = small_all[0].astype(f32)
    gain_two = small_all[1].astype(f32)

    marks = jnp.concatenate(
        [expert_ids[0].reshape(256, 4), jnp.broadcast_to(lengths, (2, 128, 4)).reshape(256, 4)], -1
    )
    marks = both(marks)
    ids = marks[:, :4]
    place = layout(marks[:, 4:].reshape(4, 128, 4)[:, 0])
    near = core * OWN + (y_at - jnp.arange(OWN)) % OWN
    slots = jnp.concatenate([near, (near + OWN) % 8])
    chosen = jnp.sum((ids[:, :, None] == slots).astype(jnp.int32), 1)
    router = jnp.take(small_all[2:10].T, slots, axis=1)

    own_x = involute(inputs.reshape(256, D), 1, x_at)
    start = both(own_x)
    x = start
    own_out = None
    for phase in range(2):
        normed, query, keys, values, mixed, part = attention_forward(x, gain_one, qkv_all, out_all, place)
        hidden, normed_two, gates, gate_in, up_in, acted, total = expert_forward(
            x, (part, other(part)), gain_two, router, gate_all, up_all, down_all, chosen
        )
        moe = total.astype(f32) + flip(other(total)).astype(f32)
        own_out = (hidden + moe)[:256].astype(bf16)
        if phase == 0:
            received = lax.ppermute(own_out, "section", [(0, 1)])
            x = jnp.where(section == 0, start, both(received))

    grad = both(involute(cotangent.reshape(256, D), 1, x_at))
    first = grad
    expert_record = (hidden, normed_two, gates, gate_in, up_in, acted)
    attn_record = (normed, query, keys, values, mixed)
    source = x.astype(f32)
    for phase in range(2):
        last = phase == 1
        part, expert_grads = expert_backward(
            grad, moe, expert_record, router, gate_all, up_all, down_all, last
        )
        grad_normed = part.astype(f32) + flip(other(part)).astype(f32)
        change, gain_two_grad = norm_backward(grad_normed, hidden, gain_two)
        grad_hidden = grad.astype(f32) + change
        part, attn_grads = attention_backward(grad_hidden, attn_record, qkv_all, out_all, place, last)
        grad_normed = part.astype(f32) + flip(other(part)).astype(f32)
        change, gain_one_grad = norm_backward(grad_normed, source, gain_one)
        own_grad = (grad_hidden + change)[:256].astype(bf16)
        if not last:
            received = lax.ppermute(own_grad, "section", [(1, 0)])
            grad = jnp.where(section == 1, first, both(received))

    router_grad, gate_grads, up_grads, down_grads = expert_grads
    qkv_grad, out_grad = attn_grads

    pair_blocks = [jnp.stack([gate_grads[e], up_grads[e]], 0) for e in range(OWN)]
    pair_sum = scatter4(pair_blocks, "y")
    pair_sum = scatter4([pair_sum[:, 256 * s : 256 * (s + 1)] for s in range(4)], "x")
    down_blocks = [
        jnp.stack([down_grads[e][:, 256 * s : 256 * (s + 1)] for e in range(OWN)], 0) for s in range(4)
    ]
    down_sum = scatter4(down_blocks, "x")
    down_sum = scatter4([down_sum[e] for e in range(OWN)], "y")
    out_grad = involute(involute(out_grad, 0, x_at), 1, x_at)
    attn_blocks = [
        jnp.concatenate([qkv_grad[256 * s : 256 * (s + 1)], out_grad[128 * s : 128 * (s + 1)]], 0)
        for s in range(4)
    ]
    attn_sum = scatter4(attn_blocks, "x")
    attn_sum = involute(attn_sum, 0, y_at)
    attn_sum = scatter4([attn_sum[96 * s : 96 * (s + 1)] for s in range(4)], "y")

    def finish(value):
        value = plus(value, pp(value, "zh", 1))
        return gather4(value, "y")

    def experts(parts):
        mine = involute(jnp.stack(parts, 0), 0, y_at)
        theirs = other(mine)
        low = jnp.where(core == 0, mine, theirs)
        high = jnp.where(core == 0, theirs, mine)
        return jnp.concatenate([low, high], 0).astype(f32)

    pairs = finish(pair_sum)
    grad_gate = jnp.swapaxes(experts([v[0] for v in pairs]), 0, 1)
    grad_up = jnp.swapaxes(experts([v[1] for v in pairs]), 0, 1)
    grad_down = experts(finish(down_sum))
    attn_own = involute(jnp.concatenate(finish(attn_sum), 0), 0, y_at)
    attn_far = other(attn_own)
    attn_low = jnp.where(core == 0, attn_own, attn_far).astype(f32)
    attn_high = jnp.where(core == 0, attn_far, attn_own).astype(f32)

    def mingle(start_at, size):
        low = attn_low[:256, start_at : start_at + 4 * size].reshape(256, 4, size)
        high = attn_high[:256, start_at : start_at + 4 * size].reshape(256, 4, size)
        return jnp.stack([low, high], 2).reshape(256, 8 * size)

    grad_query = mingle(0, 128)
    grad_key = mingle(512, 64)
    grad_value = mingle(768, 64)
    grad_out = jnp.concatenate([attn_low[256:], attn_high[256:]], 0)

    spread = jnp.zeros((8, D), f32)
    spread = lax.dynamic_update_slice_in_dim(spread, involute(router_grad.T, 0, y_at), core * OWN, 0)
    small_grads = jnp.concatenate(
        [gain_one_grad[None], gain_two_grad[None], spread, jnp.zeros((6, D), f32)], 0
    ).astype(bf16)
    small_sum = scatter4([small_grads[:, 256 * s : 256 * (s + 1)] for s in range(4)], "x")
    small_sum = plus(small_sum, other(small_sum))
    small_sum = plus(small_sum, pp(small_sum, "zh", 1))
    small_sum = sum(v.astype(f32) for v in gather4(small_sum, "y"))

    outputs = involute(own_out, 1, x_at).reshape(2, ROW, D)
    input_grads = involute(own_grad, 1, x_at).reshape(2, ROW, D)
    return (
        outputs[None],
        input_grads[None],
        small_sum[0][None],
        grad_query[None],
        grad_key[None],
        grad_value[None],
        grad_out[None],
        small_sum[1][None],
        small_sum[2:10].T[None],
        grad_gate[None],
        grad_up[None],
        grad_down[None],
    )


def solution(mesh):
    fine = Mesh(mesh.devices.reshape(2, 4, 2, 2, 4), ("section", "y", "zh", "core", "x"))
    rows = ("y", "zh", "core", "x")
    return jax.shard_map(
        local,
        mesh=fine,
        in_specs=(
            P(None, rows, None),
            P(None, rows, None),
            P(None, rows, None),
            P("section", None, rows, None),
            P("section", "x"),
            P("section", "x", None),
            P("section", "x", None),
            P("section", "x", None),
            P("section", "x", None),
            P("section", "x"),
            P("section", "x", None),
            P("section", "x", None, None),
            P("section", "x", None, None),
            P("section", None, None, "x"),
        ),
        out_specs=(
            P("section", None, rows, None),
            P("section", None, rows, None),
            P("section", "x"),
            P("section", "x", None),
            P("section", "x", None),
            P("section", "x", None),
            P("section", "x", None),
            P("section", "x"),
            P("section", "x", None),
            P("section", "x", None, None),
            P("section", "x", None, None),
            P("section", None, None, "x"),
        ),
        check_vma=False,
    )
```

time: 1300 us -> 769 us (0.59)
  waiting for transfers between devices: 780 us -> 204 us
  starting transfers between devices: 10.9 us -> 160 us
  blocking collectives: 66.4 us -> 0 us
  other arithmetic: 110 us -> 67.5 us
  matrix products: 154 us -> 174 us
  between operations: 19.4 us -> 5.4 us
    reduce_scatter x8 -> x0, waiting for transfers between devices: 319 us -> none  [the longest x1 82.7 us: local(): lax.psum_scatter(local_up.astype(jnp.bfloat16), 'fsdp', scatter_dimension...]
    all_gather x7 -> x0, waiting for transfers between devices: 285 us -> none  [the longest x1 83.1 us: layer_forward(): lax.all_gather(down_w, 'fsdp', axis=2, tiled=True)]
    ppermute x4 -> x106, waiting for transfers between devices: 10 us -> 204 us  [the longest x104 179 us: pp(): lax.ppermute(value, axis, [(i, (i + step) % count) for i in range(count)])]
    psum x1 -> x0, waiting for transfers between devices: 162 us -> none  [local(): lax.psum(shares[7].astype(jnp.bfloat16), 'dp').astype(jnp.float32)]
    ppermute x4 -> x106, starting transfers between devices: 10.3 us -> 160 us  [the longest x104 155 us: pp(): lax.ppermute(value, axis, [(i, (i + step) % count) for i in range(count)])]
    gather x15 -> x1, local copies, waits for them, and re-layouts: 45.7 us -> 0.69 us  [local(): router = jnp.take(small_all[2:10].T, slots, axis=1)]
    psum x1 -> x0, blocking collectives: 36.1 us -> none  [local(): lax.psum(shares[0].astype(jnp.bfloat16), 'dp').astype(jnp.float32)]
    slice x0 -> x68, local copies, waits for them, and re-layouts: none -> 24.3 us  [the longest x9 4.17 us: gather4(): right[half:]]
  transfers between devices with their start and end apart: 20 -> 106, of which waited for: 15 -> 48; matrix products, arithmetic and copies ran while one was open for 10% -> 33% of each run, Pallas kernels for 0% -> 0%
where the time goes in v1:
time: 769 us; the launch traced here: 754 us
  waiting for transfers between devices  204 us (27%)
  matrix products  174 us (23%)
  starting transfers between devices  160 us (21%)
  local copies, waits for them, and re-layouts  143 us (19%)
  other arithmetic  67.5 us (9%)
    ppermute x104, waiting for transfers between devices, pp(): lax.ppermute(value, axis, [(i, (i + step) % count) for i in range(count)])  179 us
    ppermute x104, starting transfers between devices, pp(): lax.ppermute(value, axis, [(i, (i + step) % count) for i in range(count)])  155 us
    dot_general x26, matrix products, dot(): return jnp.dot(left, right, preferred_element_type=f32)  56.6 us
    dot_general x30, matrix products, dot_t(): lax.dot_general(left, right, (((1,), (1,)), ((), ())), preferred_element_...  52.3 us
    unnamed x522, local copies, waits for them, and re-layouts  50.3 us
    dot_general x15, matrix products, t_dot(): lax.dot_general(left, right, (((0,), (0,)), ((), ())), preferred_element_...  22.9 us
  transfers between devices with their start and end apart: 106, of which 48 were waited for; matrix products, arithmetic and copies ran while one was open for 33% of the time, Pallas kernels for 0%

profile of v1, /device:TPU:1, one launch (start us, length us, event | category | flops | bytes accessed | tf_op | source)
XLA Modules:
  0.0 754.1 jit_solution(10981022009879896454)
XLA Ops:
  50.4 5.8 collective-permute-done.2
  63.4 11.9 %collective-permute-done.13 = bf16[64,1024]{1,0:T(8,128)(2,1)S(1)} collective-permute-done((bf16[64,1024]{1,0:T(8,128)(2,1)S(1)}, bf16[64,1024]{1,0:T(8,128)(2,1)S(1)}, u32[]{:S(2)}, u32[]{:S(2)}) %collective-permute-start.13) | collective-permute-done | bytes 131104 | tf_op jit(solution)/shard_map/ppermute | solution.py:20
  92.7 19.4 %collective-permute-done.8 = bf16[128,1024]{0,1:T(8,128)(2,1)S(1)} collective-permute-done((bf16[128,1024]{0,1:T(8,128)(2,1)S(1)}, bf16[128,1024]{0,1:T(8,128)(2,1)S(1)}, u32[]{:S(2)}, u32[]{:S(2)}) %collective-permute-start.8) | collective-permute-done | bytes 262176 | tf_op jit(solution)/shard_map/ppermute | solution.py:20
  118.4 4.0 fusion.414
  130.3 4.0 pad_maximum_fusion
  146.9 5.7 collective-permute-done.26
  158.7 4.5 fusion.39
  163.2 19.1 %collective-permute-done.24 = bf16[2,1024,512]{2,1,0:T(8,128)(2,1)} collective-permute-done((bf16[2,1024,512]{2,1,0:T(8,128)(2,1)}, bf16[2,1024,512]{2,1,0:T(8,128)(2,1)}, u32[]{:S(2)}, u32[]{:S(2)}) %collective-permute-start.24) | collective-permute-done | bytes 2097184 | tf_op jit(solution)/shard_map/ppermute | solution.py:20
  196.4 4.4 fusion.196
  200.8 9.4 %collective-permute-done.25 = bf16[1,1024,512]{2,1,0:T(8,128)(2,1)} collective-permute-done((bf16[1,1024,512]{2,1,0:T(8,128)(2,1)}, bf16[1,1024,512]{2,1,0:T(8,128)(2,1)}, u32[]{:S(2)}, u32[]{:S(2)}) %collective-permute-start.25) | collective-permute-done | bytes 1048608 | tf_op jit(solution)/shard_map/ppermute | solution.py:20
  215.6 4.6 fusion.205
  220.2 6.1 add_convert_fusion.5
  235.0 10.8 %collective-permute-done.28 = bf16[256,1024]{1,0:T(8,128)(2,1)S(1)} collective-permute-done((bf16[256,1024]{1,0:T(8,128)(2,1)S(1)}, bf16[256,1024]{1,0:T(8,128)(2,1)S(1)}, u32[]{:S(2)}, u32[]{:S(2)}) %collective-permute-start.28) | collective-permute-done | bytes 524320 | tf_op jit(solution)/shard_map/ppermute | solution.py:272
  338.6 5.2 convolution_bitcast_fusion.5
  343.9 5.3 convolution_bitcast_fusion.1
  367.3 14.1 %collective-permute-done.35 = bf16[256,1024]{1,0:T(8,128)(2,1)} collective-permute-done((bf16[256,1024]{1,0:T(8,128)(2,1)S(1)}, bf16[256,1024]{1,0:T(8,128)(2,1)}, u32[]{:S(2)}, u32[]{:S(2)}) %collective-permute-start.35) | collective-permute-done | bytes 524320 | tf_op jit(solution)/shard_map/ppermute | solution.py:293
  453.8 4.5 convert_add_fusion.9
  473.3 5.5 convolution_bitcast_fusion.3
  478.8 5.5 convolution_bitcast_fusion
  506.8 4.3 collective-permute-start.38
  535.7 4.6 collective-permute-done.54
  543.4 6.1 collective-permute-done.53
  569.4 13.9 %collective-permute-done.75 = bf16[1,1024,512]{2,1,0:T(8,128)(2,1)S(1)} collective-permute-done((bf16[1,1024,512]{2,1,0:T(8,128)(2,1)S(1)}, bf16[1,1024,512]{2,1,0:T(8,128)(2,1)S(1)}, u32[]{:S(2)}, u32[]{:S(2)}) %collective-permute-start.75) | collective-permute-done | bytes 1048608 | tf_op jit(solution)/shard_map/ppermute | solution.py:20
  583.4 15.9 %collective-permute-done.77 = bf16[1,1024,512]{2,1,0:T(8,128)(2,1)S(1)} collective-permute-done((bf16[1,1024,512]{2,1,0:T(8,128)(2,1)S(1)}, bf16[1,1024,512]{2,1,0:T(8,128)(2,1)S(1)}, u32[]{:S(2)}, u32[]{:S(2)}) %collective-permute-start.77) | collective-permute-done | bytes 1048608 | tf_op jit(solution)/shard_map/ppermute | solution.py:20
  619.1 16.1 %collective-permute-start.45 = (bf16[16,256]{1,0:T(8,128)(2,1)S(1)}, bf16[16,256]{1,0:T(8,128)(2,1)S(1)}, u32[]{:S(2)}, u32[]{:S(2)}) collective-permute-start(bf16[16,256]{1,0:T(8,128)(2,1)S(1)} %pad_maximum_fusion.44), channel_id=1, source_target_pairs={{0,4},{4,0},{1,5},{5,1},{2,6},{6,2},{3,7},{7,3},{8,12},{12,8},{9,1... | collective-permute-start | bytes 24584 | tf_op jit(solution)/shard_map/ppermute | solution.py:20
  665.0 6.5 collective-permute-start.105
  678.0 8.1 %collective-permute-done.81 = bf16[2,256,512]{2,1,0:T(8,128)(2,1)S(1)} collective-permute-done((bf16[2,256,512]{2,1,0:T(8,128)(2,1)S(1)}, bf16[2,256,512]{2,1,0:T(8,128)(2,1)S(1)}, u32[]{:S(2)}, u32[]{:S(2)}) %collective-permute-start.81) | collective-permute-done | bytes 524320 | tf_op jit(solution)/shard_map/ppermute | solution.py:20
  686.9 4.5 collective-permute-start.68
  706.6 6.1 collective-permute-done.84
  714.0 4.4 collective-permute-start.85
  743.1 4.4 copy.364
  749.2 4.4 copy.365
  (1056 shorter events, 499.3 us)
Async XLA Ops:
  2.5 58.2 %collective-permute-start.10 = (bf16[128,1024]{1,0:T(8,128)(2,1)}, bf16[128,1024]{1,0:T(8,128)(2,1)S(1)}, u32[]{:S(2)}, u32[]{:S(2)}) collective-permute-start(bf16[128,1024]{1,0:T(8,128)(2,1)} %dynamic-slice_bitcast_fusion.8), channel_id=1, source_target_pairs={{0,3},{1,0},{2,1},{3,2},{4,7},{5,4},{6,5},{7,6},{8,11},{9,8},{10,9... | collective-permute-start | bytes 786440 | tf_op jit(solution)/shard_map/ppermute | solution.py:20
  5.8 52.5 %collective-permute-start.11 = (bf16[128,1024]{1,0:T(8,128)(2,1)}, bf16[128,1024]{1,0:T(8,128)(2,1)S(1)}, u32[]{:S(2)}, u32[]{:S(2)}) collective-permute-start(bf16[128,1024]{1,0:T(8,128)(2,1)} %dynamic-slice_bitcast_fusion.8), channel_id=1, source_target_pairs={{0,1},{1,2},{2,3},{3,0},{4,5},{5,6},{6,7},{7,4},{8,9},{9,10},{10,1... | collective-permute-start | bytes 786440 | tf_op jit(solution)/shard_map/ppermute | solution.py:20
  6.5 34.1 %collective-permute-start.3 = (bf16[16,256]{1,0:T(8,128)(2,1)S(1)}, bf16[16,256]{1,0:T(8,128)(2,1)S(1)}, u32[]{:S(2)}, u32[]{:S(2)}) collective-permute-start(bf16[16,256]{1,0:T(8,128)(2,1)S(1)} %pad_maximum_fusion.43), channel_id=1, source_target_pairs={{0,3},{1,0},{2,1},{3,2},{4,7},{5,4},{6,5},{7,6},{8,11},{9,8},{10,9... | collective-permute-start | bytes 24584 | tf_op jit(solution)/shard_map/ppermute | solution.py:20
  9.3 31.4 %collective-permute-start.1 = (bf16[16,256]{1,0:T(8,128)(2,1)S(1)}, bf16[16,256]{1,0:T(8,128)(2,1)S(1)}, u32[]{:S(2)}, u32[]{:S(2)}) collective-permute-start(bf16[16,256]{1,0:T(8,128)(2,1)S(1)} %pad_maximum_fusion.43), channel_id=1, source_target_pairs={{0,1},{1,2},{2,3},{3,0},{4,5},{5,6},{6,7},{7,4},{8,9},{9,10},{10,1... | collective-permute-start | bytes 24584 | tf_op jit(solution)/shard_map/ppermute | solution.py:20
  10.8 32.9 %collective-permute-start.9 = (s32[256,8]{0,1:T(8,128)S(1)}, s32[256,8]{0,1:T(8,128)S(1)}, u32[]{:S(2)}, u32[]{:S(2)}) collective-permute-start(s32[256,8]{0,1:T(8,128)S(1)} %pad_add_fusion.1), channel_id=1, source_target_pairs={{0,4},{4,0},{1,5},{5,1},{2,6},{6,2},{3,7},{7,3},{8,12},{12,8},{9,1... | collective-permute-start | bytes 24584 | tf_op jit(solution)/shard_map/ppermute | solution.py:20
  40.6 39.6 %collective-permute-start.5 = (bf16[256,1024]{0,1:T(8,128)(2,1)}, bf16[256,1024]{0,1:T(8,128)(2,1)S(1)}, u32[]{:S(2)}, u32[]{:S(2)}) collective-permute-start(bf16[256,1024]{0,1:T(8,128)(2,1)} %get-tuple-element.213), channel_id=1, source_target_pairs={{0,1},{1,2},{2,3},{3,0},{4,5},{5,6},{6,7},{7,4},{8,9},{9,10},{10,1... | collective-permute-start | bytes 1572872 | tf_op jit(solution)/shard_map/ppermute | solution.py:20
  47.8 36.0 %collective-permute-start.7 = (bf16[256,1024]{0,1:T(8,128)(2,1)}, bf16[256,1024]{0,1:T(8,128)(2,1)S(1)}, u32[]{:S(2)}, u32[]{:S(2)}) collective-permute-start(bf16[256,1024]{0,1:T(8,128)(2,1)} %get-tuple-element.213), channel_id=1, source_target_pairs={{0,3},{1,0},{2,1},{3,2},{4,7},{5,4},{6,5},{7,6},{8,11},{9,8},{10,9... | collective-permute-start | bytes 1572872 | tf_op jit(solution)/shard_map/ppermute | solution.py:20
  56.2 30.6 %collective-permute-start.17 = (bf16[2,256,512]{2,1,0:T(8,128)(2,1)}, bf16[2,256,512]{2,1,0:T(8,128)(2,1)S(1)}, u32[]{:S(2)}, u32[]{:S(2)}) collective-permute-start(bf16[2,256,512]{2,1,0:T(8,128)(2,1)} %pad_maximum_fusion.14), channel_id=1, source_target_pairs={{0,3},{1,0},{2,1},{3,2},{4,7},{5,4},{6,5},{7,6},{8,11},{9,8},{10,9... | collective-permute-start | bytes 1572872 | tf_op jit(solution)/shard_map/ppermute | solution.py:20
  80.2 56.8 %collective-permute-start.21 = (bf16[4,512,256]{2,1,0:T(8,128)(2,1)}, bf16[4,512,256]{2,1,0:T(8,128)(2,1)}, u32[]{:S(2)}, u32[]{:S(2)}) collective-permute-start(bf16[4,512,256]{2,1,0:T(8,128)(2,1)} %constant_dynamic-slice_fusion.12), channel_id=1, source_target_pairs={{0,3},{1,0},{2,1},{3,2},{4,7},{5,4},{6,5},{7,6},{8,11},{9,8},{10,9... | collective-permute-start | bytes 3145736 | tf_op jit(solution)/shard_map/ppermute | solution.py:20
  83.9 28.2 %collective-permute-start.8 = (bf16[128,1024]{0,1:T(8,128)(2,1)S(1)}, bf16[128,1024]{0,1:T(8,128)(2,1)S(1)}, u32[]{:S(2)}, u32[]{:S(2)}) collective-permute-start(bf16[128,1024]{0,1:T(8,128)(2,1)S(1)} %slice.1080), channel_id=1, source_target_pairs={{0,3},{1,0},{2,1},{3,2},{4,7},{5,4},{6,5},{7,6},{8,11},{9,8},{10,9... | collective-permute-start | bytes 786440 | tf_op jit(solution)/shard_map/ppermute | solution.py:20
  86.9 42.2 %collective-permute-start.19 = (bf16[4,512,256]{2,1,0:T(8,128)(2,1)}, bf16[4,512,256]{2,1,0:T(8,128)(2,1)}, u32[]{:S(2)}, u32[]{:S(2)}) collective-permute-start(bf16[4,512,256]{2,1,0:T(8,128)(2,1)} %constant_dynamic-slice_fusion.12), channel_id=1, source_target_pairs={{0,1},{1,2},{2,3},{3,0},{4,5},{5,6},{6,7},{7,4},{8,9},{9,10},{10,1... | collective-permute-start | bytes 3145736 | tf_op jit(solution)/shard_map/ppermute | solution.py:20
  87.8 42.5 %collective-permute-start.18 = (bf16[1,256,512]{2,1,0:T(8,128)(2,1)}, bf16[1,256,512]{2,1,0:T(8,128)(2,1)}, u32[]{:S(2)}, u32[]{:S(2)}) collective-permute-start(bf16[1,256,512]{2,1,0:T(8,128)(2,1)} %slice.1105), channel_id=1, source_target_pairs={{0,3},{1,0},{2,1},{3,2},{4,7},{5,4},{6,5},{7,6},{8,11},{9,8},{10,9... | collective-permute-start | bytes 786440 | tf_op jit(solution)/shard_map/ppermute | solution.py:20
  92.6 37.7 %collective-permute-start.16 = (bf16[1,256,512]{2,1,0:T(8,128)(2,1)}, bf16[1,256,512]{2,1,0:T(8,128)(2,1)}, u32[]{:S(2)}, u32[]{:S(2)}) collective-permute-start(bf16[1,256,512]{2,1,0:T(8,128)(2,1)} %slice.1104), channel_id=1, source_target_pairs={{0,1},{1,2},{2,3},{3,0},{4,5},{5,6},{6,7},{7,4},{8,9},{9,10},{10,1... | collective-permute-start | bytes 786440 | tf_op jit(solution)/shard_map/ppermute | solution.py:20
  134.3 48.1 %collective-permute-start.24 = (bf16[2,1024,512]{2,1,0:T(8,128)(2,1)}, bf16[2,1024,512]{2,1,0:T(8,128)(2,1)}, u32[]{:S(2)}, u32[]{:S(2)}) collective-permute-start(bf16[2,1024,512]{2,1,0:T(8,128)(2,1)} %pad_maximum_fusion), channel_id=1, source_target_pairs={{0,48},{16,0},{32,16},{48,32},{1,49},{17,1},{33,17},{49,33},{2,50}... | collective-permute-start | bytes 6291464 | tf_op jit(solution)/shard_map/ppermute | solution.py:20
  137.0 51.2 %collective-permute-start.22 = (bf16[2,1024,512]{2,1,0:T(8,128)(2,1)}, bf16[2,1024,512]{2,1,0:T(8,128)(2,1)}, u32[]{:S(2)}, u32[]{:S(2)}) collective-permute-start(bf16[2,1024,512]{2,1,0:T(8,128)(2,1)} %pad_maximum_fusion), channel_id=1, source_target_pairs={{0,16},{16,32},{32,48},{48,0},{1,17},{17,33},{33,49},{49,1},{2,18}... | collective-permute-start | bytes 6291464 | tf_op jit(solution)/shard_map/ppermute | solution.py:20
  425.0 81.8 %collective-permute-start.76 = (bf16[1,1024,512]{2,1,0:T(8,128)(2,1)}, bf16[1,1024,512]{2,1,0:T(8,128)(2,1)}, u32[]{:S(2)}, u32[]{:S(2)}) collective-permute-start(bf16[1,1024,512]{2,1,0:T(8,128)(2,1)} %fusion.37), channel_id=1, source_target_pairs={{0,48},{16,0},{32,16},{48,32},{1,49},{17,1},{33,17},{49,33},{2,50}... | collective-permute-start | bytes 3145736 | tf_op jit(solution)/shard_map/ppermute | solution.py:20
  425.6 74.3 %collective-permute-start.69 = (bf16[1,1024,512]{2,1,0:T(8,128)(2,1)}, bf16[1,1024,512]{2,1,0:T(8,128)(2,1)}, u32[]{:S(2)}, u32[]{:S(2)}) collective-permute-start(bf16[1,1024,512]{2,1,0:T(8,128)(2,1)} %fusion.32), channel_id=1, source_target_pairs={{0,16},{16,32},{32,48},{48,0},{1,17},{17,33},{33,49},{49,1},{2,18}... | collective-permute-start | bytes 3145736 | tf_op jit(solution)/shard_map/ppermute | solution.py:20
  443.7 71.1 %collective-permute-start.90 = (bf16[2,512,256]{2,1,0:T(8,128)(2,1)}, bf16[2,512,256]{2,1,0:T(8,128)(2,1)}, u32[]{:S(2)}, u32[]{:S(2)}) collective-permute-start(bf16[2,512,256]{2,1,0:T(8,128)(2,1)} %pad_maximum_fusion.22), channel_id=1, source_target_pairs={{0,3},{1,0},{2,1},{3,2},{4,7},{5,4},{6,5},{7,6},{8,11},{9,8},{10,9... | collective-permute-start | bytes 1572872 | tf_op jit(solution)/shard_map/ppermute | solution.py:20
  446.8 66.5 %collective-permute-start.91 = (bf16[2,512,256]{2,1,0:T(8,128)(2,1)}, bf16[2,512,256]{2,1,0:T(8,128)(2,1)}, u32[]{:S(2)}, u32[]{:S(2)}) collective-permute-start(bf16[2,512,256]{2,1,0:T(8,128)(2,1)} %pad_maximum_fusion.23), channel_id=1, source_target_pairs={{0,1},{1,2},{2,3},{3,0},{4,5},{5,6},{6,7},{7,4},{8,9},{9,10},{10,1... | collective-permute-start | bytes 1572872 | tf_op jit(solution)/shard_map/ppermute | solution.py:20
  449.8 65.0 %collective-permute-start.89 = (bf16[2,512,256]{2,1,0:T(8,128)(2,1)}, bf16[2,512,256]{2,1,0:T(8,128)(2,1)}, u32[]{:S(2)}, u32[]{:S(2)}) collective-permute-start(bf16[2,512,256]{2,1,0:T(8,128)(2,1)} %add_convert_fusion.9), channel_id=1, source_target_pairs={{0,1},{1,2},{2,3},{3,0},{4,5},{5,6},{6,7},{7,4},{8,9},{9,10},{10,1... | collective-permute-start | bytes 1572872 | tf_op jit(solution)/shard_map/ppermute | solution.py:20
  506.8 58.9 %collective-permute-start.38 = (bf16[512,1024]{1,0:T(8,128)(2,1)S(1)}, bf16[512,1024]{1,0:T(8,128)(2,1)S(1)}, u32[]{:S(2)}, u32[]{:S(2)}) collective-permute-start(bf16[512,1024]{1,0:T(8,128)(2,1)S(1)} %convolution_convert_fusion.1), channel_id=1, source_target_pairs={{0,4},{4,0},{1,5},{5,1},{2,6},{6,2},{3,7},{7,3},{8,12},{12,8},{9,1... | collective-permute-start | bytes 3145736 | tf_op jit(solution)/shard_map/ppermute | solution.py:20
  561.4 39.0 %collective-permute-start.71 = (bf16[1,1024,512]{2,1,0:T(8,128)(2,1)S(1)}, bf16[1,1024,512]{2,1,0:T(8,128)(2,1)S(1)}, u32[]{:S(2)}, u32[]{:S(2)}) collective-permute-start(bf16[1,1024,512]{2,1,0:T(8,128)(2,1)S(1)} %copy-done.177), channel_id=1, source_target_pairs={{0,48},{16,0},{32,16},{48,32},{1,49},{17,1},{33,17},{49,33},{2,50}... | collective-permute-start | bytes 3145736 | tf_op jit(solution)/shard_map/ppermute | solution.py:20
  564.1 35.2 %collective-permute-start.77 = (bf16[1,1024,512]{2,1,0:T(8,128)(2,1)S(1)}, bf16[1,1024,512]{2,1,0:T(8,128)(2,1)S(1)}, u32[]{:S(2)}, u32[]{:S(2)}) collective-permute-start(bf16[1,1024,512]{2,1,0:T(8,128)(2,1)S(1)} %fusion.16), channel_id=1, source_target_pairs={{0,48},{16,0},{32,16},{48,32},{1,49},{17,1},{33,17},{49,33},{2,50}... | collective-permute-start | bytes 3145736 | tf_op jit(solution)/shard_map/ppermute | solution.py:20
  564.2 41.6 %collective-permute-start.70 = (bf16[1,1024,512]{2,1,0:T(8,128)(2,1)S(1)}, bf16[1,1024,512]{2,1,0:T(8,128)(2,1)S(1)}, u32[]{:S(2)}, u32[]{:S(2)}) collective-permute-start(bf16[1,1024,512]{2,1,0:T(8,128)(2,1)S(1)} %fusion.19), channel_id=1, source_target_pairs={{0,16},{16,32},{32,48},{48,0},{1,17},{17,33},{33,49},{49,1},{2,18}... | collective-permute-start | bytes 3145736 | tf_op jit(solution)/shard_map/ppermute | solution.py:20
  565.7 77.5 %collective-permute-start.60 = (bf16[48,1024]{1,0:T(8,128)(2,1)S(1)}, bf16[48,1024]{1,0:T(8,128)(2,1)S(1)}, u32[]{:S(2)}, u32[]{:S(2)}) collective-permute-start(bf16[48,1024]{1,0:T(8,128)(2,1)S(1)} %get-tuple-element.132), channel_id=1, source_target_pairs={{0,16},{16,32},{32,48},{48,0},{1,17},{17,33},{33,49},{49,1},{2,18}... | collective-permute-start | bytes 294920 | tf_op jit(solution)/shard_map/ppermute | solution.py:20
  600.4 44.5 %collective-permute-start.62 = (bf16[48,1024]{1,0:T(8,128)(2,1)S(1)}, bf16[48,1024]{1,0:T(8,128)(2,1)S(1)}, u32[]{:S(2)}, u32[]{:S(2)}) collective-permute-start(bf16[48,1024]{1,0:T(8,128)(2,1)S(1)} %get-tuple-element.130), channel_id=1, source_target_pairs={{0,48},{16,0},{32,16},{48,32},{1,49},{17,1},{33,17},{49,33},{2,50}... | collective-permute-start | bytes 294920 | tf_op jit(solution)/shard_map/ppermute | solution.py:20
  613.5 45.1 %collective-permute-start.79 = (bf16[1,256,512]{2,1,0:T(8,128)(2,1)S(1)}, bf16[1,256,512]{2,1,0:T(8,128)(2,1)S(1)}, u32[]{:S(2)}, u32[]{:S(2)}) collective-permute-start(bf16[1,256,512]{2,1,0:T(8,128)(2,1)S(1)} %get-tuple-element.162), channel_id=1, source_target_pairs={{0,3},{1,0},{2,1},{3,2},{4,7},{5,4},{6,5},{7,6},{8,11},{9,8},{10,9... | collective-permute-start | bytes 786440 | tf_op jit(solution)/shard_map/ppermute | solution.py:20
  616.5 54.9 %collective-permute-start.78 = (bf16[1,256,512]{2,1,0:T(8,128)(2,1)S(1)}, bf16[1,256,512]{2,1,0:T(8,128)(2,1)S(1)}, u32[]{:S(2)}, u32[]{:S(2)}) collective-permute-start(bf16[1,256,512]{2,1,0:T(8,128)(2,1)S(1)} %get-tuple-element.161), channel_id=1, source_target_pairs={{0,1},{1,2},{2,3},{3,0},{4,5},{5,6},{6,7},{7,4},{8,9},{9,10},{10,1... | collective-permute-start | bytes 786440 | tf_op jit(solution)/shard_map/ppermute | solution.py:20
  640.4 33.9 %collective-permute-start.74 = (bf16[1,256,512]{2,1,0:T(8,128)(2,1)S(1)}, bf16[1,256,512]{2,1,0:T(8,128)(2,1)S(1)}, u32[]{:S(2)}, u32[]{:S(2)}) collective-permute-start(bf16[1,256,512]{2,1,0:T(8,128)(2,1)S(1)} %get-tuple-element.160), channel_id=1, source_target_pairs={{0,3},{1,0},{2,1},{3,2},{4,7},{5,4},{6,5},{7,6},{8,11},{9,8},{10,9... | collective-permute-start | bytes 786440 | tf_op jit(solution)/shard_map/ppermute | solution.py:20
  665.0 32.3 %collective-permute-start.105 = (bf16[4,512,256]{2,1,0:T(8,128)(2,1)S(1)}, bf16[4,512,256]{2,1,0:T(8,128)(2,1)S(1)}, u32[]{:S(2)}, u32[]{:S(2)}) collective-permute-start(bf16[4,512,256]{2,1,0:T(8,128)(2,1)S(1)} %constant_dynamic-slice_fusion.3), channel_id=1, source_target_pairs={{0,4},{4,0},{1,5},{5,1},{2,6},{6,2},{3,7},{7,3},{8,12},{12,8},{9,1... | collective-permute-start | bytes 3145736 | tf_op jit(solution)/shard_map/ppermute | solution.py:20
  686.9 31.6 %collective-permute-start.68 = (bf16[384,1024]{1,0:T(8,128)(2,1)S(1)}, bf16[384,1024]{1,0:T(8,128)(2,1)S(1)}, u32[]{:S(2)}, u32[]{:S(2)}) collective-permute-start(bf16[384,1024]{1,0:T(8,128)(2,1)S(1)} %constant_dynamic-slice_fusion.6), channel_id=1, source_target_pairs={{0,4},{4,0},{1,5},{5,1},{2,6},{6,2},{3,7},{7,3},{8,12},{12,8},{9,1... | collective-permute-start | bytes 2359304 | tf_op jit(solution)/shard_map/ppermute | solution.py:20
  714.0 27.4 %collective-permute-start.85 = (bf16[4,256,512]{2,1,0:T(8,128)(2,1)}, bf16[4,256,512]{2,1,0:T(8,128)(2,1)}, u32[]{:S(2)}, u32[]{:S(2)}) collective-permute-start(bf16[4,256,512]{2,1,0:T(8,128)(2,1)} %constant_dynamic-slice_fusion.5), channel_id=1, source_target_pairs={{0,4},{4,0},{1,5},{5,1},{2,6},{6,2},{3,7},{7,3},{8,12},{12,8},{9,1... | collective-permute-start | bytes 3145736 | tf_op jit(solution)/shard_map/ppermute | solution.py:20
  (282 other events, 2355.3 us)

commit v2 on v1

v2 whole, which is shorter than its diff:
```python
import functools

import jax
import jax.numpy as jnp
from jax import lax
from jax.experimental import pallas as pl
from jax.experimental.pallas import tpu as pltpu
from jax.sharding import Mesh, PartitionSpec as P

D = 1024
HEAD_DIM = 64
GROUPS = 4
FF = 512
OWN = 4
ROW = 128
epsilon = 1e-05
rope_base = 10000.0
bf16 = jnp.bfloat16
f32 = jnp.float32


def pp(value, axis, step):
    count = lax.axis_size(axis)
    return lax.ppermute(value, axis, [(i, (i + step) % count) for i in range(count)])


def involute(value, dim, index):
    size = value.shape[dim] // 4
    blocks = [lax.slice_in_dim(value, i * size, (i + 1) * size, axis=dim) for i in (3, 2, 1, 0)]
    double = jnp.concatenate(blocks + blocks[:3], dim)
    return lax.dynamic_slice_in_dim(double, (3 - index) * size, 4 * size, dim)


def plus(first, second):
    return (first.astype(f32) + second.astype(f32)).astype(bf16)


def ring3(value, axis):
    return [value, pp(value, axis, 1), pp(value, axis, 2), pp(value, axis, -1)]


def scatter3(blocks, axis):
    here, behind, far, ahead = blocks
    total = here.astype(f32) + pp(ahead, axis, 1).astype(f32)
    total = total + pp(behind, axis, -1).astype(f32) + pp(far, axis, 2).astype(f32)
    return total.astype(bf16)


def other(value):
    return pp(value, "core", 1)


def both(value):
    return jnp.concatenate([value, other(value)], 0)


def flip(value):
    half = value.shape[0] // 2
    return jnp.concatenate([value[half:], value[:half]], 0)


def dot(left, right):
    return jnp.dot(left, right, preferred_element_type=f32)


def dot_t(left, right):
    return lax.dot_general(left, right, (((1,), (1,)), ((), ())), preferred_element_type=f32)


def t_dot(left, right):
    return lax.dot_general(left, right, (((0,), (0,)), ((), ())), preferred_element_type=f32)


def inverse_root(value):
    return lax.rsqrt(jnp.mean(value * value, -1, keepdims=True) + epsilon)


def layout(lengths):
    ends = jnp.cumsum(lengths, -1)
    places = jnp.arange(ROW, dtype=jnp.int32)
    segment = jnp.sum((places[None, :, None] >= ends[:, None, :]).astype(jnp.int32), -1)
    starts = ends - lengths
    member = segment[:, :, None] == jnp.arange(lengths.shape[-1], dtype=jnp.int32)
    position = places[None, :] - jnp.sum(jnp.where(member, starts[:, None, :], 0), -1)
    allowed = (segment[:, :, None] == segment[:, None, :]) & (
        places[None, :, None] >= places[None, None, :]
    )
    freqs = rope_base ** (-jnp.arange(HEAD_DIM // 2, dtype=f32) * 2.0 / HEAD_DIM)
    turned = position.reshape(-1).astype(f32)[:, None] * jnp.tile(freqs, 4)
    sign = jnp.where(jnp.arange(ROW) % HEAD_DIM < HEAD_DIM // 2, -1.0, 1.0).astype(f32)
    return jnp.where(allowed, 0.0, -1e30).astype(f32), jnp.cos(turned), jnp.sin(turned) * sign


def lanes(rows):
    return lax.broadcasted_iota(jnp.int32, (rows, ROW), 1)


def turn(value, cosine, sine):
    lane = lanes(value.shape[0])
    swapped = jnp.where(lane % HEAD_DIM < HEAD_DIM // 2, pltpu.roll(value, 96, 1), pltpu.roll(value, 32, 1))
    return value * cosine + swapped * sine


def doubled(value):
    low = lanes(value.shape[0]) < HEAD_DIM
    rolled = pltpu.roll(value, HEAD_DIM, 1)
    return jnp.where(low, value, rolled), jnp.where(low, rolled, value)


def split_heads(value):
    low = (lanes(1) < HEAD_DIM).astype(f32).astype(bf16)
    return jnp.concatenate([value * low, value * (1 - low)], 0)


def join_heads(value):
    half = value.shape[0] // 2
    return jnp.where(lanes(half) < HEAD_DIM, value[:half], value[half:])


def attend(query, keys, bias):
    scores = dot_t(query, keys) * HEAD_DIM**-0.5 + bias
    expo = jnp.exp(scores - jnp.max(scores, -1, keepdims=True))
    return expo / jnp.sum(expo, -1, keepdims=True)


def attention_forward_kernel(
    x_ref, gain_ref, *refs
):
    cos_ref, sin_ref, bias_ref, n_ref, q_ref, k_ref, v_ref, o_ref, part_ref, w_qkv, w_out, sems = refs[4:]
    bring_attention(refs[:4], w_qkv, w_out, sems)
    source = x_ref[...].astype(f32)
    n_ref[...] = (source * inverse_root(source) * gain_ref[...]).astype(bf16)
    cosine, sine = cos_ref[...], sin_ref[...]
    for c in range(4):
        wide = dot(n_ref[...], w_qkv[:, 256 * c : 256 * (c + 1)])
        for h in range(2):
            value = wide[:, ROW * h : ROW * (h + 1)]
            if c < 2:
                at = ROW * (2 * c + h)
                q_ref[:, at : at + ROW] = turn(value, cosine, sine).astype(bf16)
                continue
            to = k_ref
            if c == 2:
                value = turn(value, cosine, sine)
            else:
                to = v_ref
            first, second = doubled(value)
            to[:, 256 * h : 256 * h + ROW] = first.astype(bf16)
            to[:, 256 * h + ROW : 256 * (h + 1)] = second.astype(bf16)
    for r in range(2):
        rows = slice(ROW * r, ROW * (r + 1))
        bias = jnp.concatenate([bias_ref[r], bias_ref[r]], 0)
        for g in range(GROUPS):
            cols = slice(ROW * g, ROW * (g + 1))
            prob = attend(split_heads(q_ref[rows, cols]), k_ref[rows, cols], bias).astype(bf16)
            o_ref[rows, cols] = join_heads(dot(prob, v_ref[rows, cols])).astype(bf16)
    part_ref[...] = dot(o_ref[...], w_out[...]).astype(bf16)


def spec(shape, index):
    return pl.BlockSpec(shape, index)


def fixed(shape):
    return pl.BlockSpec(shape, lambda i: (0,) * len(shape))


def shape_of(shape, dtype):
    return jax.ShapeDtypeStruct(shape, dtype)


def params():
    return pltpu.CompilerParams(vmem_limit_bytes=56 * 2**20)


def rows_spec(width):
    return pl.BlockSpec((256, width), lambda i: (i, 0))


def ring_place(s):
    return lax.rem(lax.axis_index("x") - s + 4, 4)


def bring_attention(pieces, w_qkv, w_out, sems):
    @pl.when(pl.program_id(0) == 0)
    def _():
        copies = []
        for s in range(4):
            at = ring_place(s)
            to = w_qkv.at[pl.ds(pl.multiple_of(at * 256, 256), 256)]
            copies.append(pltpu.make_async_copy(pieces[s].at[pl.ds(0, 256)], to, sems.at[2 * s]))
            to = w_out.at[pl.ds(pl.multiple_of(at * ROW, ROW), ROW)]
            copies.append(pltpu.make_async_copy(pieces[s].at[pl.ds(256, ROW)], to, sems.at[2 * s + 1]))
        for copy in copies:
            copy.start()
        for copy in copies:
            copy.wait()


def attention_buffers():
    return [pltpu.VMEM((D, D), bf16), pltpu.VMEM((512, D), bf16), pltpu.SemaphoreType.DMA((8,))]


def attention_forward(x, gain, w_attn, place):
    bias, cosine, sine = place
    return pl.pallas_call(
        attention_forward_kernel,
        grid=(2,),
        in_specs=[
            rows_spec(D), fixed((1, D)), *[afar()] * 4, rows_spec(ROW), rows_spec(ROW),
            spec((2, ROW, ROW), lambda i: (i, 0, 0)),
        ],
        out_specs=[rows_spec(w) for w in (D, 512, 512, 512, 512, D)],
        out_shape=[shape_of((512, w), bf16) for w in (D, 512, 512, 512, 512, D)],
        scratch_shapes=attention_buffers(),
        compiler_params=params(),
        cost_estimate=pl.CostEstimate(flops=6 * 10**9, bytes_accessed=10 * 2**20, transcendentals=10**6),
        name="attention_forward",
    )(x, gain, *w_attn, cosine, sine, bias)


def weight_copies(weights, buffers, sems):
    own, left, far_gate, far_up, right, down, down_left, down_far, down_far_too, down_right = weights
    gate, up, low = buffers
    sources = [(own.at[0], own.at[1]), (left.at[0], left.at[1]), (far_gate.at[0], far_up.at[0]), (right.at[0], right.at[1])]
    copies = []
    for e in range(OWN):
        low_from = [down.at[e], down_left.at[e], (down_far, down_far_too)[e // 2].at[e % 2], down_right.at[e]]
        group = []
        for s in range(4):
            at = pl.ds(pl.multiple_of(ring_place(s) * 256, 256), 256)
            group.append((sources[e][0].at[s], gate.at[e, at]))
            group.append((sources[e][1].at[s], up.at[e, at]))
            group.append((low_from[s], low.at[e, :, at]))
        copies.append([pltpu.make_async_copy(*pair, sems.at[12 * e + i]) for i, pair in enumerate(group)])
    return copies


def weight_buffers():
    return [
        pltpu.VMEM((OWN, D, FF), bf16),
        pltpu.VMEM((OWN, D, FF), bf16),
        pltpu.VMEM((OWN, FF, D), bf16),
        pltpu.SemaphoreType.DMA((12 * OWN,)),
    ]


def expert_forward_kernel(save, *refs):
    x_ref, part_ref, far_ref, gain_ref, router_ref, chosen_ref = refs[:6]
    weights, refs = refs[6:16], refs[16:]
    if save:
        h_ref, total_ref, n_ref, gates_ref, *stores = refs[:7]
        refs = refs[7:]
    else:
        h_ref, total_ref = refs[:2]
        n_ref, gates_ref = refs[-2:]
        refs = refs[2:-2]
    gate_ref, up_ref, down_ref, sems, acc_ref = refs[:5]
    if save:
        held, out_sems = refs[5:8], refs[8]
    copies = weight_copies(weights, (gate_ref, up_ref, down_ref), sems)
    for group in copies:
        for copy in group:
            copy.start()
    for i in range(4):
        rows = slice(ROW * i, ROW * (i + 1))
        away = slice(ROW * ((i + 2) % 4), ROW * ((i + 2) % 4 + 1))
        hidden = x_ref[rows].astype(f32) + part_ref[rows].astype(f32) + far_ref[away].astype(f32)
        h_ref[rows] = hidden
        normed = (hidden * inverse_root(hidden) * gain_ref[...]).astype(bf16)
        n_ref[rows] = normed
        on = chosen_ref[rows] > 0
        masked = jnp.where(on, dot(normed, router_ref[...]), -1e30)
        raised = jnp.where(on, jnp.exp(masked - jnp.max(masked, -1, keepdims=True)), 0.0)
        gates_ref[rows] = raised / jnp.sum(raised, -1, keepdims=True)
    sent = []
    for e in range(OWN):
        for copy in copies[e]:
            copy.wait()
        cols = slice(FF * e, FF * (e + 1))
        for i in range(2):
            rows = slice(256 * i, 256 * (i + 1))
            gate = jnp.sum(jnp.where(lanes(256) == e, gates_ref[rows], 0.0), -1, keepdims=True)
            a = dot(n_ref[rows], gate_ref[e])
            b = dot(n_ref[rows], up_ref[e])
            acted = (gate * a * lax.logistic(a) * b).astype(bf16)
            if save:
                held[0][rows, cols] = a.astype(bf16)
                held[1][rows, cols] = b.astype(bf16)
                held[2][rows, cols] = acted
            added = dot(acted, down_ref[e])
            if e == 0:
                acc_ref[rows] = added
            elif e < OWN - 1:
                acc_ref[rows] += added
            else:
                total_ref[rows] = (acc_ref[rows] + added).astype(bf16)
        if save:
            for i in range(3):
                copy = pltpu.make_async_copy(held[i].at[:, cols], stores[i].at[:, cols], out_sems.at[3 * e + i])
                copy.start()
                sent.append(copy)
    for copy in sent:
        copy.wait()


def whole():
    return pl.BlockSpec(memory_space=pltpu.VMEM)


def afar():
    return pl.BlockSpec(memory_space=pl.ANY)


def expert_forward(x, part, far, gain, router, chosen, weights, save):
    out_specs = [whole()] * 2
    out_shape = [shape_of((512, D), f32), shape_of((512, D), bf16)]
    scratch = weight_buffers() + [pltpu.VMEM((512, D), f32)]
    if save:
        out_specs += [whole()] * 2 + [afar()] * 3
        out_shape += [shape_of((512, D), bf16), shape_of((512, ROW), f32)] + [shape_of((512, 2048), bf16)] * 3
        scratch += [pltpu.VMEM((512, 2048), bf16)] * 3 + [pltpu.SemaphoreType.DMA((3 * OWN,))]
    else:
        scratch += [pltpu.VMEM((512, D), bf16), pltpu.VMEM((512, ROW), f32)]
    return pl.pallas_call(
        functools.partial(expert_forward_kernel, save),
        in_specs=[whole()] * 6 + [afar()] * 10,
        out_specs=out_specs,
        out_shape=out_shape,
        scratch_shapes=scratch,
        compiler_params=params(),
        cost_estimate=pl.CostEstimate(flops=7 * 10**9, bytes_accessed=24 * 2**20, transcendentals=10**6),
        name="expert_forward",
    )(x, part, far, gain, router, chosen, *weights)


def expert_backward_kernel(*refs):
    grad_ref, total_ref, far_ref, gates_ref, router_ref, a_ref, b_ref = refs[:7]
    weights = refs[7:17]
    logit_ref, part_ref, *stores = refs[17:21]
    gate_ref, up_ref, down_ref, sems, acc_ref, slope_ref, a_in, b_in, a_out, b_out, row_sems = refs[21:]
    copies = weight_copies(weights, (gate_ref, up_ref, down_ref), sems)
    for e in range(OWN):
        cols = slice(FF * e, FF * (e + 1))
        copies[e].append(pltpu.make_async_copy(a_ref.at[:, cols], a_in.at[:, cols], row_sems.at[4 * e]))
        copies[e].append(pltpu.make_async_copy(b_ref.at[:, cols], b_in.at[:, cols], row_sems.at[4 * e + 1]))
        for copy in copies[e]:
            copy.start()
    inner = []
    for i in range(4):
        rows = slice(ROW * i, ROW * (i + 1))
        away = slice(ROW * ((i + 2) % 4), ROW * ((i + 2) % 4 + 1))
        moe = total_ref[rows].astype(f32) + far_ref[away].astype(f32)
        inner.append(jnp.sum(grad_ref[rows].astype(f32) * moe, -1, keepdims=True))
    inner = [jnp.concatenate(inner[2 * i : 2 * i + 2], 0) for i in range(2)]
    sent = []
    for e in range(OWN):
        for copy in copies[e]:
            copy.wait()
        cols = slice(FF * e, FF * (e + 1))
        for i in range(2):
            rows = slice(256 * i, 256 * (i + 1))
            mine = lanes(256) == e
            gate = jnp.sum(jnp.where(mine, gates_ref[rows], 0.0), -1, keepdims=True)
            wide = dot_t(grad_ref[rows], down_ref[e])
            a, b = a_in[rows, cols].astype(f32), b_in[rows, cols].astype(f32)
            sigma = lax.logistic(a)
            raised = wide * a * sigma
            slope = jnp.where(mine, gate * (jnp.sum(raised * b, -1, keepdims=True) - inner[i]), 0.0)
            a_out[rows, cols] = (gate * wide * b * sigma * (1.0 + a * (1.0 - sigma))).astype(bf16)
            b_out[rows, cols] = (gate * raised).astype(bf16)
            added = dot_t(a_out[rows, cols], gate_ref[e]) + dot_t(b_out[rows, cols], up_ref[e])
            if e == 0:
                slope_ref[rows] = slope
                acc_ref[rows] = added
            elif e < OWN - 1:
                slope_ref[rows] += slope
                acc_ref[rows] += added
            else:
                logit_ref[rows] = (slope_ref[rows] + slope).astype(bf16)
                added = added + dot_t(logit_ref[rows], router_ref[...])
                part_ref[rows] = (acc_ref[rows] + added).astype(bf16)
        for i, held in enumerate((a_out, b_out)):
            copy = pltpu.make_async_copy(held.at[:, cols], stores[i].at[:, cols], row_sems.at[4 * e + 2 + i])
            copy.start()
            sent.append(copy)
    for copy in sent:
        copy.wait()


def expert_backward(grad, total, far, gates, router, a, b, weights):
    return pl.pallas_call(
        expert_backward_kernel,
        in_specs=[whole()] * 5 + [afar()] * 12,
        out_specs=[whole()] * 2 + [afar()] * 2,
        out_shape=[shape_of((512, ROW), bf16), shape_of((512, D), bf16)] + [shape_of((512, 2048), bf16)] * 2,
        scratch_shapes=weight_buffers()
        + [pltpu.VMEM((512, D), f32), pltpu.VMEM((512, ROW), f32)]
        + [pltpu.VMEM((512, 2048), bf16)] * 4
        + [pltpu.SemaphoreType.DMA((4 * OWN,))],
        compiler_params=params(),
        cost_estimate=pl.CostEstimate(flops=7 * 10**9, bytes_accessed=24 * 2**20, transcendentals=10**6),
        name="expert_backward",
    )(grad, total, far, gates, router, a, b, *weights)


def spread_kernel(pair, pair_far, low, low_far, attn, attn_far, mix, mix_far, gate, up, down, query, key, value, out):
    first = lax.axis_index("core") == 0

    def sides(near, far):
        near, far = near.astype(f32), far.astype(f32)
        return jnp.where(first, near, far), jnp.where(first, far, near)

    for y in range(4):
        for c, side in enumerate(sides(pair[y], pair_far[y])):
            gate[:, 4 * c + y, :] = side[:, :FF]
            up[:, 4 * c + y, :] = side[:, FF:]
        for c, side in enumerate(sides(low[y], low_far[y])):
            down[4 * c + y] = side
    for c, side in enumerate(sides(mix[0], mix_far[0])):
        out[c] = side
    near, far = sides(attn[0], attn_far[0])
    below = lanes(64) < HEAD_DIM
    for s in range(4):
        query[:, 256 * s : 256 * s + ROW] = near[:, ROW * s : ROW * (s + 1)]
        query[:, 256 * s + ROW : 256 * (s + 1)] = far[:, ROW * s : ROW * (s + 1)]
    for to, base in ((key, 512), (value, 768)):
        for h in range(2):
            a = near[:, base + ROW * h : base + ROW * (h + 1)]
            b = far[:, base + ROW * h : base + ROW * (h + 1)]
            to[:, 256 * h : 256 * h + ROW] = jnp.where(below, a, pltpu.roll(b, HEAD_DIM, 1))
            to[:, 256 * h + ROW : 256 * (h + 1)] = jnp.where(below, pltpu.roll(a, HEAD_DIM, 1), b)


def spread(packed, theirs):
    specs = [
        spec((4, 64, D), lambda i: (0, i, 0)),
        spec((4, ROW, 256), lambda i: (0, 2, i)),
        spec((1, 64, D), lambda i: (i, 6, 0)),
        spec((1, 32, D), lambda i: (i, 14, 0)),
    ]
    return pl.pallas_call(
        spread_kernel,
        grid=(4,),
        in_specs=[item for item in specs for _ in range(2)],
        out_specs=[
            spec((64, 8, FF), lambda i: (i, 0, 0)),
            spec((64, 8, FF), lambda i: (i, 0, 0)),
            spec((8, ROW, 256), lambda i: (0, i, 0)),
            spec((64, D), lambda i: (i, 0)),
            spec((64, 512), lambda i: (i, 0)),
            spec((64, 512), lambda i: (i, 0)),
            spec((2, 32, D), lambda i: (0, i, 0)),
        ],
        out_shape=[
            shape_of(shape, f32)
            for shape in ((256, 8, FF), (256, 8, FF), (8, FF, 256), (256, D), (256, 512), (256, 512), (2, ROW, D))
        ],
        compiler_params=params(),
        cost_estimate=pl.CostEstimate(flops=10**6, bytes_accessed=24 * 2**20, transcendentals=0),
        name="spread",
    )(*[packed, theirs] * 4)


def norm_backward(grad_normed, value, gain):
    scale = inverse_root(value)
    scaled = grad_normed * gain
    change = scale * scaled - value * scale**3 * jnp.mean(value * scaled, -1, keepdims=True)
    return change, jnp.sum(grad_normed * value * scale, 0, keepdims=True)


def attention_backward_kernel(
    grad_ref, h_ref, near_ref, far_ref, gain_ref, *refs
):
    q_ref, k_ref, v_ref, cos_ref, sin_ref, bias_ref = refs[4:10]
    dh_ref, da_ref, dqkv_ref, part_ref, gain_grad_ref, do_ref, w_qkv, w_out, sems = refs[10:]
    bring_attention(refs[:4], w_qkv, w_out, sems)
    change, gain_grad = norm_backward(
        near_ref[...].astype(f32) + far_ref[...].astype(f32), h_ref[...], gain_ref[...]
    )

    @pl.when(pl.program_id(0) == 0)
    def _():
        gain_grad_ref[...] = gain_grad

    grad_hidden = grad_ref[...].astype(f32) + change
    dh_ref[...] = grad_hidden
    da_ref[...] = grad_hidden.astype(bf16)
    do_ref[...] = dot_t(da_ref[...], w_out[...]).astype(bf16)
    for r in range(2):
        rows = slice(ROW * r, ROW * (r + 1))
        bias = jnp.concatenate([bias_ref[r], bias_ref[r]], 0)
        cosine, sine = cos_ref[rows], -sin_ref[rows]
        key_grads, value_grads = [], []
        for g in range(GROUPS):
            cols = slice(ROW * g, ROW * (g + 1))
            query = split_heads(q_ref[rows, cols])
            keys = k_ref[rows, cols]
            prob = attend(query, keys, bias)
            grad_mixed = split_heads(do_ref[rows, cols])
            grad_prob = dot_t(grad_mixed, v_ref[rows, cols])
            value_grads.append(t_dot(prob.astype(bf16), grad_mixed))
            inner = jnp.sum(prob * grad_prob, -1, keepdims=True)
            grad_scores = (prob * (grad_prob - inner) * HEAD_DIM**-0.5).astype(bf16)
            dqkv_ref[rows, cols] = turn(join_heads(dot(grad_scores, keys)), cosine, sine).astype(bf16)
            key_grads.append(t_dot(grad_scores, query))
        for h in range(2):
            low = lanes(ROW) < HEAD_DIM
            pair = [v + pltpu.roll(v, HEAD_DIM, 1) for v in key_grads[2 * h : 2 * h + 2]]
            at = 512 + ROW * h
            dqkv_ref[rows, at : at + ROW] = turn(jnp.where(low, *pair), cosine, sine).astype(bf16)
            pair = [v + pltpu.roll(v, HEAD_DIM, 1) for v in value_grads[2 * h : 2 * h + 2]]
            at = 768 + ROW * h
            dqkv_ref[rows, at : at + ROW] = jnp.where(low, *pair).astype(bf16)
    part_ref[...] = dot_t(dqkv_ref[...], w_qkv[...]).astype(bf16)


def attention_backward(grad, hidden, near, far, gain, w_attn, query, keys, values, place):
    bias, cosine, sine = place
    return pl.pallas_call(
        attention_backward_kernel,
        grid=(2,),
        in_specs=[
            rows_spec(D), rows_spec(D), rows_spec(D), pl.BlockSpec((256, D), lambda i: (1 - i, 0)),
            fixed((1, D)), *[afar()] * 4,
            rows_spec(512), rows_spec(512), rows_spec(512), rows_spec(ROW), rows_spec(ROW),
            spec((2, ROW, ROW), lambda i: (i, 0, 0)),
        ],
        out_specs=[rows_spec(D)] * 4 + [fixed((1, D))],
        out_shape=[shape_of((512, D), f32)] + [shape_of((512, D), bf16)] * 3 + [shape_of((1, D), f32)],
        scratch_shapes=[pltpu.VMEM((256, 512), bf16)] + attention_buffers(),
        compiler_params=params(),
        cost_estimate=pl.CostEstimate(flops=9 * 10**9, bytes_accessed=16 * 2**20, transcendentals=10**6),
        name="attention_backward",
    )(grad, hidden, near, far, gain, *w_attn, query, keys, values, cosine, sine, bias)


def local(
    inputs, cotangent, lengths, expert_ids, gain_attn, w_query, w_key, w_value, w_out,
    gain_ffn, w_router, w_gate, w_up, w_down,
):
    section = lax.axis_index("section")
    x_at, y_at, core = lax.axis_index("x"), lax.axis_index("y"), lax.axis_index("core")

    expert = core * OWN + y_at
    pair = jnp.stack(
        [lax.dynamic_index_in_dim(w_gate[0], expert, 1, False), lax.dynamic_index_in_dim(w_up[0], expert, 1, False)], 0
    )
    pair = jnp.stack(ring3(pair, "x"), 1)
    q_own = lax.dynamic_index_in_dim(w_query[0].reshape(256, 4, 2, 128), core, 2, False).reshape(256, 512)
    k_own = lax.dynamic_index_in_dim(w_key[0].reshape(256, 4, 2, 64), core, 2, False).reshape(256, 256)
    v_own = lax.dynamic_index_in_dim(w_value[0].reshape(256, 4, 2, 64), core, 2, False).reshape(256, 256)
    out_own = lax.dynamic_slice_in_dim(w_out[0], core * 128, 128, 0)
    small = jnp.concatenate([gain_attn[0], gain_ffn[0], w_router[0].T.reshape(2048)])
    small = jnp.concatenate([small, jnp.zeros((16 * D - 2560,), bf16)]).reshape(16, D)
    attn_own = jnp.concatenate([jnp.concatenate([q_own, k_own, v_own], -1), out_own, small], 0)
    down_own = involute(lax.dynamic_slice_in_dim(w_down[0], core * OWN, OWN, 0), 0, y_at)
    attn_own, down_own, pair = lax.optimization_barrier((attn_own, down_own, pair))
    left, right = pp(pair, "y", 1), pp(pair, "y", -1)
    attn_all = ring3(attn_own, "x")
    down_left, down_right = pp(down_own, "x", 1), pp(down_own, "x", -1)
    far_gate, far_up = pp(left[:1], "y", 1), pp(right[1:], "y", -1)
    down_far, down_far_too = pp(down_left[:2], "x", 1), pp(down_right[2:], "x", -1)
    weights = (pair, left, far_gate, far_up, right, down_own, down_left, down_far, down_far_too, down_right)
    small_all = jnp.concatenate([v[384:387].reshape(12, 256) for v in attn_all], -1)
    small_all = involute(small_all, 1, x_at)
    gain_one = small_all[:1].astype(f32)
    gain_two = small_all[1:2].astype(f32)

    marks = jnp.concatenate(
        [expert_ids[0].reshape(256, 4), jnp.broadcast_to(lengths, (2, 128, 4)).reshape(256, 4)], -1
    )
    marks = both(marks)
    ids = marks[:, :4]
    place = layout(marks[:, 4:].reshape(4, 128, 4)[:, 0])
    near = core * OWN + (y_at - jnp.arange(OWN)) % OWN
    slots = jnp.concatenate([near, (near + OWN) % 8, jnp.full((ROW - 8,), -1)])
    chosen = jnp.sum((ids[:, :, None] == slots).astype(f32), 1)
    router = t_dot(small_all[2:10], (jnp.arange(8)[:, None] == slots).astype(bf16)).astype(bf16)

    start = both(inputs.reshape(256, D))
    x = start
    for phase in range(2):
        normed, query, keys, values, mixed, part = attention_forward(x, gain_one, attn_all, place)
        hidden, total, *record = expert_forward(
            x, part, other(part), gain_two, router, chosen, weights, phase == 1
        )
        total_far = other(total)
        moe = total[:256].astype(f32) + total_far[256:].astype(f32)
        own_out = (hidden[:256] + moe).astype(bf16)
        if phase == 0:
            received = lax.ppermute(own_out, "section", [(0, 1)])
            x = jnp.where(section == 0, start, both(received))

    normed_two, gates, gate_in, up_in, acted = record
    grad = both(cotangent.reshape(256, D))
    first = grad
    source = x[:256].astype(f32)
    for phase in range(2):
        logit_grad, part, gate_grad, up_grad = expert_backward(
            grad, total, total_far, gates, router, gate_in, up_in, weights
        )
        if phase == 1:
            down_grad = t_dot(acted, grad).astype(bf16).reshape(OWN, FF, D)
            gate_grad = t_dot(normed_two, gate_grad).astype(bf16)
            up_grad = t_dot(normed_two, up_grad).astype(bf16)
            part, gate_grad, up_grad, down_grad = lax.optimization_barrier(
                (part, gate_grad, up_grad, down_grad)
            )
            blocks = [
                jnp.concatenate([gate_grad[:, FF * e : FF * (e + 1)], up_grad[:, FF * e : FF * (e + 1)]], -1)
                for e in range(OWN)
            ]
            far_sent = (pp(blocks[2][:512], "y", 1), pp(blocks[2][512:], "y", -1))
            down_sum = lax.psum_scatter(down_grad, "x", scatter_dimension=2, tiled=True)
        grad_hidden, grad_attn, qkv_grad, part, gain_two_grad = attention_backward(
            grad, hidden, part, other(part), gain_two, attn_all, query, keys, values, place
        )
        if phase == 1:
            far_sent, part = lax.optimization_barrier((far_sent, part))
            ahead = jnp.concatenate([plus(blocks[3][:512], far_sent[0]), blocks[3][512:]], 0)
            behind = jnp.concatenate([blocks[1][:512], plus(blocks[1][512:], far_sent[1])], 0)
            ahead, behind = pp(ahead, "y", 1), pp(behind, "y", -1)
        far = other(part)
        grad_normed = part[:256].astype(f32) + far[256:].astype(f32)
        change, gain_one_grad = norm_backward(grad_normed, source, gain_one)
        own_grad = (grad_hidden[:256] + change).astype(bf16)
        if phase == 0:
            received = lax.ppermute(own_grad, "section", [(1, 0)])
            grad = jnp.where(section == 1, first, both(received))

    router_grad = t_dot(normed_two, logit_grad)[:, :OWN]
    qkv_grad = t_dot(normed, qkv_grad).astype(bf16)
    out_grad = t_dot(mixed, grad_attn).astype(bf16)
    placed = jnp.zeros((8, D), f32)
    placed = lax.dynamic_update_slice_in_dim(placed, involute(router_grad.T, 0, y_at), core * OWN, 0)
    small_grads = jnp.concatenate([gain_one_grad, gain_two_grad, placed], 0).astype(bf16)

    def block(s):
        small = small_grads[:, 256 * s : 256 * (s + 1)].reshape(2560)
        small = jnp.concatenate([small, jnp.zeros((32 * D - 2560,), bf16)]).reshape(32, D)
        return jnp.concatenate(
            [qkv_grad[256 * s : 256 * (s + 1)], out_grad[128 * s : 128 * (s + 1)], small], 0
        )

    attn_sum = lax.psum_scatter(jnp.stack([block(s) for s in range(4)], 0), "x", scatter_dimension=0)
    pair_sum = (blocks[0].astype(f32) + ahead.astype(f32) + behind.astype(f32)).astype(bf16)
    pair_sum = involute(pair_sum, 0, x_at)
    pair_sum = scatter3([pair_sum[256 * s : 256 * (s + 1)] for s in range(4)], "x")
    parts = [(attn_sum[:256], 64), (attn_sum[256:384], 32), (attn_sum[384:], 8)]
    parts = [(involute(part, 0, y_at), size) for part, size in parts]

    def rest(e):
        down = jnp.concatenate([down_sum[e, ROW * i : ROW * (i + 1)] for i in range(4)], -1)
        return jnp.concatenate([down] + [part[size * e : size * (e + 1)] for part, size in parts], 0)

    rest_sum = scatter3([rest(e) for e in range(OWN)], "y")

    packed = jnp.concatenate([pair_sum, rest_sum], 0)
    packed = plus(packed, pp(packed, "zh", 1))
    packed = lax.all_gather(packed, "y")
    theirs = other(packed)
    grad_gate, grad_up, grad_down, grad_query, grad_key, grad_value, grad_out = spread(packed, theirs)
    grad_out = grad_out.reshape(256, D)
    small_sum = (packed[0, 480:483].astype(f32) + theirs[0, 480:483].astype(f32)).reshape(12, 256)

    outputs = own_out.reshape(2, ROW, D)
    input_grads = own_grad.reshape(2, ROW, D)
    return (
        outputs[None],
        input_grads[None],
        small_sum[0][None],
        grad_query[None],
        grad_key[None],
        grad_value[None],
        grad_out[None],
        small_sum[1][None],
        small_sum[2:10].T[None],
        grad_gate[None],
        grad_up[None],
        grad_down[None],
    )


def solution(mesh):
    fine = Mesh(mesh.devices.reshape(2, 4, 2, 2, 4), ("section", "y", "zh", "core", "x"))
    rows = ("y", "zh", "core", "x")
    return jax.shard_map(
        local,
        mesh=fine,
        in_specs=(
            P(None, rows, None),
            P(None, rows, None),
            P(None, rows, None),
            P("section", None, rows, None),
            P("section", "x"),
            P("section", "x", None),
            P("section", "x", None),
            P("section", "x", None),
            P("section", "x", None),
            P("section", "x"),
            P("section", "x", None),
            P("section", "x", None, None),
            P("section", "x", None, None),
            P("section", None, None, "x"),
        ),
        out_specs=(
            P("section", None, rows, None),
            P("section", None, rows, None),
            P("section", "x"),
            P("section", "x", None),
            P("section", "x", None),
            P("section", "x", None),
            P("section", "x", None),
            P("section", "x"),
            P("section", "x", None),
            P("section", "x", None, None),
            P("section", "x", None, None),
            P("section", None, None, "x"),
        ),
        check_vma=False,
    )
```

time: 769 us -> 563 us (0.73)
  matrix products: 174 us -> 20 us
  Pallas kernels: 0 us -> 126 us
  starting transfers between devices: 160 us -> 55 us
  local copies, waits for them, and re-layouts: 143 us -> 62 us
  waiting for transfers between devices: 204 us -> 229 us
  other arithmetic: 67.5 us -> 47.1 us
  between operations: 5.4 us -> 15.3 us
    dot_general x66 -> x0, matrix products: 144 us -> none  [the longest x26 56.6 us: dot(): return jnp.dot(left, right, preferred_element_type=f32)]
    pallas_call x0 -> x9, Pallas kernels: none -> 126 us  [the longest x2 36.1 us: expert_backward(): pl.pallas_call(expert_backward_kernel, in_specs=[whole()] * 5 + [afar()]...]
    ppermute x104 -> x39, starting transfers between devices: 155 us -> 50 us  [pp(): lax.ppermute(value, axis, [(i, (i + step) % count) for i in range(count)])]
    all_gather x0 -> x1, waiting for transfers between devices: none -> 48.9 us  [local(): packed = lax.all_gather(packed, 'y')]
    unnamed x522 -> x162, local copies, waits for them, and re-layouts: 50.3 us -> 22.8 us
    ppermute x104 -> x39, waiting for transfers between devices: 179 us -> 155 us  [pp(): lax.ppermute(value, axis, [(i, (i + step) % count) for i in range(count)])]
    another operation x13 -> x2, local copies, waits for them, and re-layouts: 19.1 us -> 1.41 us  [the longest x1 1.41 us: local(): w_query[0].reshape(256, 4, 2, 128)]
    reshape x6 -> x15, local copies, waits for them, and re-layouts: 15.4 us -> 5.53 us  [the longest x4 3.21 us: block(): small = small_grads[:, 256 * s:256 * (s + 1)].reshape(2560)]
  transfers between devices with their start and end apart: 106 -> 44, of which waited for: 48 -> 24; matrix products, arithmetic and copies ran while one was open for 33% -> 16% of each run, Pallas kernels for 0% -> 5%
where the time goes in v2:
time: 563 us; the launch traced here: 554 us
  waiting for transfers between devices  229 us (41%)
  Pallas kernels  126 us (22%)
  local copies, waits for them, and re-layouts  62 us (11%)
  starting transfers between devices  55 us (10%)
  other arithmetic  47.1 us (8%)
  matrix products  20 us (4%)
  between operations  15.3 us (3%)
    ppermute x39, waiting for transfers between devices, pp(): lax.ppermute(value, axis, [(i, (i + step) % count) for i in range(count)])  155 us
    ppermute x39, starting transfers between devices, pp(): lax.ppermute(value, axis, [(i, (i + step) % count) for i in range(count)])  50 us
    all_gather x1, waiting for transfers between devices, local(): packed = lax.all_gather(packed, 'y')  48.9 us
    pallas_call x2, Pallas kernels, expert_backward(): pl.pallas_call(expert_backward_kernel, in_specs=[whole()] * 5 + [afar()]...  36.1 us
    pallas_call x2, Pallas kernels, attention_backward(): pl.pallas_call(attention_backward_kernel, grid=(2,), in_specs=[rows_spec(...  33 us
    pallas_call x2, Pallas kernels, expert_forward(): pl.pallas_call(functools.partial(expert_forward_kernel, save), in_specs=[...  28 us
    unnamed x162, local copies, waits for them, and re-layouts  22.8 us
    dot_general x7, matrix products, t_dot(): lax.dot_general(left, right, (((0,), (0,)), ((), ())), preferred_element_...  20 us
  transfers between devices with their start and end apart: 44, of which 24 were waited for; matrix products, arithmetic and copies ran while one was open for 16% of the time, Pallas kernels for 5%

profile of v2, /device:TPU:1, one launch (start us, length us, event | category | flops | bytes accessed | tf_op | source)
XLA Modules:
  0.0 553.7 jit_solution(8233457356301993952)
XLA Ops:
  7.3 3.4 constant_dynamic-slice_fusion.16
  32.5 6.7 %collective-permute-done.2 = bf16[2,256,512]{2,1,0:T(8,128)(2,1)} collective-permute-done((bf16[2,256,512]{2,1,0:T(8,128)(2,1)}, bf16[2,256,512]{2,1,0:T(8,128)(2,1)}, u32[]{:S(2)}, u32[]{:S(2)}) %collective-permute-start.2) | collective-permute-done | bytes 524320 | tf_op jit(solution)/shard_map/ppermute | solution.py:24
  40.8 2.9 collective-permute-start.4
  53.0 25.6 %collective-permute-done.4.refs_3_ = bf16[400,1024]{1,0:T(8,128)(2,1)} collective-permute-done((bf16[400,1024]{1,0:T(8,128)(2,1)}, bf16[400,1024]{1,0:T(8,128)(2,1)}, u32[]{:S(2)}, u32[]{:S(2)}) %collective-permute-start.4) | collective-permute-done | bytes 819232 | tf_op jit(solution)/shard_map/ppermute | solution.py:24
  79.3 3.8 collective-permute-start.15
  85.4 9.3 %attention_forward.2 = (bf16[512,1024]{1,0:T(8,128)(2,1)}, bf16[512,512]{1,0:T(8,128)(2,1)}, bf16[512,512]{1,0:T(8,128)(2,1)}, bf16[512,512]{1,0:T(8,128)(2,1)},...) custom-call(bf16[512,1024]{1,0:T(8,128)(2,1)} %pad_maximum_fusion.5.x_ref.refs_0_, ...), custom_call_target="tpu_custom_call" | custom-call | flops 6000000000 | bytes 10485760 | tf_op jit(solution)/shard_map/attention_forward/pallas_call | solution.py:206
  111.6 6.6 %collective-permute-done.14.refs_13_.refs_14_ = bf16[2,512,256]{2,1,0:T(8,128)(2,1)S(1)} collective-permute-done((bf16[2,512,256]{2,1,0:T(8,128)(2,1)S(1)}, bf16[2,512,256]{2,1,0:T(8,128)(2,1)S(1)}, u32[]{:S(2)}, u32[]{:S(2)}) %collective-permute-start.14) | collective-permute-done | bytes 524320 | tf_op jit(solution)/shard_map/ppermute | solution.py:24
  118.3 7.1 %collective-permute-done.10.refs_8_.refs_9_ = bf16[1,4,256,512]{3,2,1,0:T(8,128)(2,1)} collective-permute-done((bf16[1,4,256,512]{3,2,1,0:T(8,128)(2,1)}, bf16[1,4,256,512]{3,2,1,0:T(8,128)(2,1)}, u32[]{:S(2)}, u32[]{:S(2)}) %collective-permute-start.10) | collective-permute-done | bytes 1048608 | tf_op jit(solution)/shard_map/ppermute | solution.py:24
  126.1 13.1 %expert_forward.2 = (f32[512,1024]{1,0:T(8,128)}, bf16[512,1024]{1,0:T(8,128)(2,1)}) custom-call(bf16[512,1024]{1,0:T(8,128)(2,1)} %pad_maximum_fusion.5.x_ref.refs_0_, bf16[512,1024]{1,0:T(8,128)(2,1)} %get-tuple-element.58.refs_1_, bf16[512,1024]{1,0:T(8,128)(2,1)} %collective-permute-done.8.refs_2_, f32[1,1024]{1,0:T(1,128)} %get-tuple-element.159.refs_3_.gain_ref, ...), custom_call_target="tpu_custom_call" | custom-call | flops 7000000000 | bytes 25165824 | tf_op jit(solution)/shard_map/expert_forward/pallas_call | solution.py:325
  144.9 3.6 collective-permute-start.18
  148.4 10.9 %collective-permute-done.18 = bf16[256,1024]{1,0:T(8,128)(2,1)S(1)} collective-permute-done((bf16[256,1024]{1,0:T(8,128)(2,1)S(1)}, bf16[256,1024]{1,0:T(8,128)(2,1)S(1)}, u32[]{:S(2)}, u32[]{:S(2)}) %collective-permute-start.18) | collective-permute-done | bytes 524320 | tf_op jit(solution)/shard_map/ppermute | solution.py:592
  164.7 9.3 %attention_forward.3 = (bf16[512,1024]{1,0:T(8,128)(2,1)}, bf16[512,512]{1,0:T(8,128)(2,1)}, bf16[512,512]{1,0:T(8,128)(2,1)}, bf16[512,512]{1,0:T(8,128)(2,1)},...) custom-call(bf16[512,1024]{1,0:T(8,128)(2,1)} %maximum_select_fusion.x_ref.refs_0_, ...), custom_call_target="tpu_custom_call" | custom-call | flops 6000000000 | bytes 10485760 | tf_op jit(solution)/shard_map/attention_forward/pallas_call | solution.py:206
  178.0 14.9 %expert_forward.3 = (f32[512,1024]{1,0:T(8,128)}, bf16[512,1024]{1,0:T(8,128)(2,1)}, bf16[512,1024]{1,0:T(8,128)(2,1)}, f32[512,128]{1,0:T(8,128)}, bf16[512,204...) custom-call(bf16[512,1024]{1,0:T(8,128)(2,1)} %maximum_select_fusion.x_ref.refs_0_, ...), custom_call_target="tpu_custom_call" | custom-call | flops 7000000000 | bytes 25165824 | tf_op jit(solution)/shard_map/expert_forward/pallas_call | solution.py:325
  193.7 2.7 collective-permute-done.22
  198.5 18.0 %expert_backward.2 = (bf16[512,128]{1,0:T(8,128)(2,1)}, bf16[512,1024]{1,0:T(8,128)(2,1)}, bf16[512,2048]{1,0:T(8,128)(2,1)}, bf16[512,2048]{1,0:T(8,128)(2,1)}) custom-call(bf16[512,1024]{1,0:T(8,128)(2,1)} %pad_maximum_fusion.6.refs_0_.grad_ref, bf16[512,1024]{1,0:T(8,128)(2,1)} %get-tuple-element.65.refs_1_, bf16[512,1024]{1,0:T(8,128)(2,1)} %copy-done.26, ...), custom_call_target="tpu_custom_call" | custom-call | flops 7000000000 | bytes 25165824 | tf_op jit(solution)/shard_map/expert_backward/pallas_call | solution.py:392
  220.6 16.5 %attention_backward.2 = (f32[512,1024]{1,0:T(8,128)}, bf16[512,1024]{1,0:T(8,128)(2,1)}, bf16[512,1024]{1,0:T(8,128)(2,1)}, bf16[512,1024]{1,0:T(8,128)(2,1)}, f32[1,1024]{1,0:T(1,128)}) custom-call(bf16[512,1024]{1,0:T(8,128)(2,1)} %pad_maximum_fusion.6.refs_0_.grad_ref, f32[512,1024]{1,0:T(8,128)} %get-tuple-element.64.h_ref, ...), custom_call_target="tpu_custom_call" | custom-call | flops 8999999488 | bytes 16777216 | tf_op jit(solution)/shard_map/attention_backward/pallas_call | solution.py:520
  244.6 14.0 %collective-permute-done.25 = bf16[256,1024]{1,0:T(8,128)(2,1)S(1)} collective-permute-done((bf16[256,1024]{1,0:T(8,128)(2,1)S(1)}, bf16[256,1024]{1,0:T(8,128)(2,1)S(1)}, u32[]{:S(2)}, u32[]{:S(2)}) %collective-permute-start.25) | collective-permute-done | bytes 524320 | tf_op jit(solution)/shard_map/ppermute | solution.py:629
  262.0 4.4 convolution_convert_fusion
  266.4 18.1 %expert_backward.3 = (bf16[512,128]{1,0:T(8,128)(2,1)}, bf16[512,1024]{1,0:T(8,128)(2,1)}, bf16[512,2048]{1,0:T(8,128)(2,1)}, bf16[512,2048]{1,0:T(8,128)(2,1)}) custom-call(bf16[512,1024]{1,0:T(8,128)(2,1)} %copy-done.24, bf16[512,1024]{1,0:T(8,128)(2,1)} %get-tuple-element.65.refs_1_, bf16[512,1024]{1,0:T(8,128)(2,1)} %copy-done.26, ...), custom_call_target="tpu_custom_call" | custom-call | flops 7000000000 | bytes 25165824 | tf_op jit(solution)/shard_map/expert_backward/pallas_call | solution.py:392
  284.5 6.3 %convolution_convert_fusion.1 = bf16[1024,2048]{1,0:T(8,128)(2,1)} fusion(bf16[512,1024]{1,0:T(8,128)(2,1)S(1)} %copy-done.22, bf16[512,2048]{1,0:T(8,128)(2,1)} %get-tuple-element.78), kind=kOutput, calls=%fused_computation.5 | convolution fusion | flops 2149580800 | bytes 7340032 | tf_op jit(solution)/shard_map/dot_general | solution.py:71
  290.9 4.4 convolution_convert_fusion.2
  295.8 4.0 fusion.45
  306.4 16.5 %attention_backward.3 = (f32[512,1024]{1,0:T(8,128)}, bf16[512,1024]{1,0:T(8,128)(2,1)}, bf16[512,1024]{1,0:T(8,128)(2,1)}, bf16[512,1024]{1,0:T(8,128)(2,1)}, f32[1,1024]{1,0:T(1,128)}) custom-call(bf16[512,1024]{1,0:T(8,128)(2,1)} %copy-done.24, f32[512,1024]{1,0:T(8,128)} %get-tuple-element.64.h_ref, bf16[512,1024]{1,0:T(8,128)(2,1)} %get-tuple-element.80.near_ref, ...), custom_call_target="tpu_custom_call" | custom-call | flops 8999999488 | bytes 16777216 | tf_op jit(solution)/shard_map/attention_backward/pallas_call | solution.py:520
  322.9 6.5 %collective-permute-done.28 = bf16[512,1024]{1,0:T(8,128)(2,1)} collective-permute-done((bf16[512,1024]{1,0:T(8,128)(2,1)}, bf16[512,1024]{1,0:T(8,128)(2,1)}, u32[]{:S(2)}, u32[]{:S(2)}) %collective-permute-start.28) | collective-permute-done | bytes 1048608 | tf_op jit(solution)/shard_map/ppermute | solution.py:24
  361.9 42.9 %collective-permute-done.31 = bf16[1024,1024]{1,0:T(8,128)(2,1)} collective-permute-done((bf16[1024,1024]{1,0:T(8,128)(2,1)}, bf16[1024,1024]{1,0:T(8,128)(2,1)}, u32[]{:S(2)}, u32[]{:S(2)}) %collective-permute-start.31) | collective-permute-done | bytes 2097184 | tf_op jit(solution)/shard_map/ppermute | solution.py:24
  407.5 3.5 add_convert_fusion
  432.9 5.6 %collective-permute-done.35 = bf16[256,1024]{1,0:T(8,128)(2,1)} collective-permute-done((bf16[256,1024]{1,0:T(8,128)(2,1)S(1)}, bf16[256,1024]{1,0:T(8,128)(2,1)}, u32[]{:S(2)}, u32[]{:S(2)}) %collective-permute-start.35) | collective-permute-done | bytes 524320 | tf_op jit(solution)/shard_map/ppermute | solution.py:24
  440.6 11.1 %collective-permute-done.38 = bf16[232,1024]{1,0:T(8,128)(2,1)S(1)} collective-permute-done((bf16[232,1024]{1,0:T(8,128)(2,1)S(1)}, bf16[232,1024]{1,0:T(8,128)(2,1)S(1)}, u32[]{:S(2)}, u32[]{:S(2)}) %collective-permute-start.38) | collective-permute-done | bytes 475168 | tf_op jit(solution)/shard_map/ppermute | solution.py:24
  452.2 3.4 collective-permute-start.39
  455.5 19.7 %collective-permute-done.39 = bf16[488,1024]{1,0:T(8,128)(2,1)S(1)} collective-permute-done((bf16[488,1024]{1,0:T(8,128)(2,1)S(1)}, bf16[488,1024]{1,0:T(8,128)(2,1)S(1)}, u32[]{:S(2)}, u32[]{:S(2)}) %collective-permute-start.39) | collective-permute-done | bytes 999456 | tf_op jit(solution)/shard_map/ppermute | solution.py:24
  476.7 48.9 %all-gather.3.cloned.1.call-done = bf16[1952,1024]{1,0:T(8,128)(2,1)} async-done(((bf16[488,1024]{1,0:T(8,128)(2,1)}), bf16[1952,1024]{1,0:T(8,128)(2,1)}) %all-gather.3.cloned.1.call-update) | async-done | bytes 3997712 | tf_op jit(solution)/shard_map/all_gather | solution.py:661
  536.8 10.1 %spread.1 = (f32[256,8,512]{2,1,0:T(8,128)}, f32[256,8,512]{2,1,0:T(8,128)}, f32[8,512,256]{2,1,0:T(8,128)}, f32[256,1024]{1,0:T(8,128)}, f32[256,512]{1,0:T(8,1...) custom-call(bf16[4,488,1024]{2,1,0:T(8,128)(2,1)} %bitcast.207, bf16[4,488,1024]{2,1,0:T(8,128)(2,1)} %copy-done.2, ...), custom_call_target="tpu_custom_call" | custom-call | flops 1000000 | bytes 25165824 | tf_op jit(solution)/shard_map/spread/pallas_call | solution.py:442
  (359 shorter events, 164.5 us)
Async XLA Ops:
  7.2 409.1 %reduce-scatter.3.cloned.1.call-start = ((), (), s32[]{:S(2)}) async-start(), calls=%async_computation.2 | async-start | bytes 5242880 | tf_op jit(solution)/shard_map/reduce_scatter | solution.py:615
  11.8 20.7 %collective-permute-start.1 = (bf16[2,256,512]{2,1,0:T(8,128)(2,1)}, bf16[2,256,512]{2,1,0:T(8,128)(2,1)}, u32[]{:S(2)}, u32[]{:S(2)}) collective-permute-start(bf16[2,256,512]{2,1,0:T(8,128)(2,1)} %get-tuple-element.150), channel_id=1, source_target_pairs={{0,1},{1,2},{2,3},{3,0},{4,5},{5,6},{6,7},{7,4},{8,9},{9,10},{10,1... | collective-permute-start | bytes 1572872 | tf_op jit(solution)/shard_map/ppermute | solution.py:24
  13.8 25.3 %collective-permute-start.2 = (bf16[2,256,512]{2,1,0:T(8,128)(2,1)}, bf16[2,256,512]{2,1,0:T(8,128)(2,1)}, u32[]{:S(2)}, u32[]{:S(2)}) collective-permute-start(bf16[2,256,512]{2,1,0:T(8,128)(2,1)} %get-tuple-element.150), channel_id=1, source_target_pairs={{0,2},{1,3},{2,0},{3,1},{4,6},{5,7},{6,4},{7,5},{8,10},{9,11},{10,... | collective-permute-start | bytes 1572872 | tf_op jit(solution)/shard_map/ppermute | solution.py:24
  16.3 22.9 %collective-permute-start.3 = (bf16[2,256,512]{2,1,0:T(8,128)(2,1)}, bf16[2,256,512]{2,1,0:T(8,128)(2,1)}, u32[]{:S(2)}, u32[]{:S(2)}) collective-permute-start(bf16[2,256,512]{2,1,0:T(8,128)(2,1)} %get-tuple-element.150), channel_id=1, source_target_pairs={{0,3},{1,0},{2,1},{3,2},{4,7},{5,4},{6,5},{7,6},{8,11},{9,8},{10,9... | collective-permute-start | bytes 1572872 | tf_op jit(solution)/shard_map/ppermute | solution.py:24
  17.6 14.1 %collective-permute-start.7 = (s32[256,8]{0,1:T(8,128)S(1)}, s32[256,8]{0,1:T(8,128)S(1)}, u32[]{:S(2)}, u32[]{:S(2)}) collective-permute-start(s32[256,8]{0,1:T(8,128)S(1)} %pad_add_fusion.1), channel_id=1, source_target_pairs={{0,4},{4,0},{1,5},{5,1},{2,6},{6,2},{3,7},{7,3},{8,12},{12,8},{9,1... | collective-permute-start | bytes 24584 | tf_op jit(solution)/shard_map/ppermute | solution.py:24
  19.2 26.7 %collective-permute-start = (bf16[256,1024]{1,0:T(8,128)(2,1)}, bf16[256,1024]{1,0:T(8,128)(2,1)}, u32[]{:S(2)}, u32[]{:S(2)}) collective-permute-start(bf16[256,1024]{1,0:T(8,128)(2,1)} %bitcast), channel_id=1, source_target_pairs={{0,4},{4,0},{1,5},{5,1},{2,6},{6,2},{3,7},{7,3},{8,12},{12,8},{9,1... | collective-permute-start | bytes 1572872 | tf_op jit(solution)/shard_map/ppermute | solution.py:24
  40.8 37.8 %collective-permute-start.4 = (bf16[400,1024]{1,0:T(8,128)(2,1)}, bf16[400,1024]{1,0:T(8,128)(2,1)}, u32[]{:S(2)}, u32[]{:S(2)}) collective-permute-start(bf16[400,1024]{1,0:T(8,128)(2,1)} %pad_maximum_fusion.8.refs_0_), channel_id=1, source_target_pairs={{0,3},{1,0},{2,1},{3,2},{4,7},{5,4},{6,5},{7,6},{8,11},{9,8},{10,9... | collective-permute-start | bytes 2457608 | tf_op jit(solution)/shard_map/ppermute | solution.py:24
  43.7 35.6 %collective-permute-start.5 = (bf16[400,1024]{1,0:T(8,128)(2,1)}, bf16[400,1024]{1,0:T(8,128)(2,1)}, u32[]{:S(2)}, u32[]{:S(2)}) collective-permute-start(bf16[400,1024]{1,0:T(8,128)(2,1)} %pad_maximum_fusion.8.refs_0_), channel_id=1, source_target_pairs={{0,2},{1,3},{2,0},{3,1},{4,6},{5,7},{6,4},{7,5},{8,10},{9,11},{10,... | collective-permute-start | bytes 2457608 | tf_op jit(solution)/shard_map/ppermute | solution.py:24
  43.7 40.2 %collective-permute-start.6 = (bf16[400,1024]{1,0:T(8,128)(2,1)}, bf16[400,1024]{1,0:T(8,128)(2,1)}, u32[]{:S(2)}, u32[]{:S(2)}) collective-permute-start(bf16[400,1024]{1,0:T(8,128)(2,1)} %pad_maximum_fusion.8.refs_0_), channel_id=1, source_target_pairs={{0,1},{1,2},{2,3},{3,0},{4,5},{5,6},{6,7},{7,4},{8,9},{9,10},{10,1... | collective-permute-start | bytes 2457608 | tf_op jit(solution)/shard_map/ppermute | solution.py:24
  44.4 52.0 %collective-permute-start.9 = (bf16[2,4,256,512]{3,2,1,0:T(8,128)(2,1)S(1)}, bf16[2,4,256,512]{3,2,1,0:T(8,128)(2,1)}, u32[]{:S(2)}, u32[]{:S(2)}) collective-permute-start(bf16[2,4,256,512]{3,2,1,0:T(8,128)(2,1)S(1)} %pad_maximum_fusion.1.refs_6_.refs_7_), channel_id=1, source_target_pairs={{0,16},{16,32},{32,48},{48,0},{1,17},{17,33},{33,49},{49,1},{2,18}... | collective-permute-start | bytes 6291464 | tf_op jit(solution)/shard_map/ppermute | solution.py:24
  45.9 54.3 %collective-permute-start.11 = (bf16[2,4,256,512]{3,2,1,0:T(8,128)(2,1)S(1)}, bf16[2,4,256,512]{3,2,1,0:T(8,128)(2,1)}, u32[]{:S(2)}, u32[]{:S(2)}) collective-permute-start(bf16[2,4,256,512]{3,2,1,0:T(8,128)(2,1)S(1)} %pad_maximum_fusion.1.refs_6_.refs_7_), channel_id=1, source_target_pairs={{0,48},{16,0},{32,16},{48,32},{1,49},{17,1},{33,17},{49,33},{2,50}... | collective-permute-start | bytes 6291464 | tf_op jit(solution)/shard_map/ppermute | solution.py:24
  78.6 25.8 %collective-permute-start.13 = (bf16[4,512,256]{2,1,0:T(8,128)(2,1)S(1)}, bf16[4,512,256]{2,1,0:T(8,128)(2,1)}, u32[]{:S(2)}, u32[]{:S(2)}) collective-permute-start(bf16[4,512,256]{2,1,0:T(8,128)(2,1)S(1)} %copy-done.21), channel_id=1, source_target_pairs={{0,1},{1,2},{2,3},{3,0},{4,5},{5,6},{6,7},{7,4},{8,9},{9,10},{10,1... | collective-permute-start | bytes 3145736 | tf_op jit(solution)/shard_map/ppermute | solution.py:24
  79.3 26.2 %collective-permute-start.15 = (bf16[4,512,256]{2,1,0:T(8,128)(2,1)S(1)}, bf16[4,512,256]{2,1,0:T(8,128)(2,1)}, u32[]{:S(2)}, u32[]{:S(2)}) collective-permute-start(bf16[4,512,256]{2,1,0:T(8,128)(2,1)S(1)} %copy-done.21), channel_id=1, source_target_pairs={{0,3},{1,0},{2,1},{3,2},{4,7},{5,4},{6,5},{7,6},{8,11},{9,8},{10,9... | collective-permute-start | bytes 3145736 | tf_op jit(solution)/shard_map/ppermute | solution.py:24
  94.7 23.6 %collective-permute-start.8 = (bf16[512,1024]{1,0:T(8,128)(2,1)}, bf16[512,1024]{1,0:T(8,128)(2,1)}, u32[]{:S(2)}, u32[]{:S(2)}) collective-permute-start(bf16[512,1024]{1,0:T(8,128)(2,1)} %get-tuple-element.58.refs_1_), channel_id=1, source_target_pairs={{0,4},{4,0},{1,5},{5,1},{2,6},{6,2},{3,7},{7,3},{8,12},{12,8},{9,1... | collective-permute-start | bytes 3145736 | tf_op jit(solution)/shard_map/ppermute | solution.py:24
  98.6 26.7 %collective-permute-start.10 = (bf16[1,4,256,512]{3,2,1,0:T(8,128)(2,1)}, bf16[1,4,256,512]{3,2,1,0:T(8,128)(2,1)}, u32[]{:S(2)}, u32[]{:S(2)}) collective-permute-start(bf16[1,4,256,512]{3,2,1,0:T(8,128)(2,1)} %slice.550), channel_id=1, source_target_pairs={{0,16},{16,32},{32,48},{48,0},{1,17},{17,33},{33,49},{49,1},{2,18}... | collective-permute-start | bytes 3145736 | tf_op jit(solution)/shard_map/ppermute | solution.py:24
  101.4 24.6 %collective-permute-start.12 = (bf16[1,4,256,512]{3,2,1,0:T(8,128)(2,1)S(1)}, bf16[1,4,256,512]{3,2,1,0:T(8,128)(2,1)}, u32[]{:S(2)}, u32[]{:S(2)}) collective-permute-start(bf16[1,4,256,512]{3,2,1,0:T(8,128)(2,1)S(1)} %slice.551), channel_id=1, source_target_pairs={{0,48},{16,0},{32,16},{48,32},{1,49},{17,1},{33,17},{49,33},{2,50}... | collective-permute-start | bytes 3145736 | tf_op jit(solution)/shard_map/ppermute | solution.py:24
  105.4 12.8 %collective-permute-start.14 = (bf16[2,512,256]{2,1,0:T(8,128)(2,1)S(1)}, bf16[2,512,256]{2,1,0:T(8,128)(2,1)S(1)}, u32[]{:S(2)}, u32[]{:S(2)}) collective-permute-start(bf16[2,512,256]{2,1,0:T(8,128)(2,1)S(1)} %slice.552), channel_id=1, source_target_pairs={{0,1},{1,2},{2,3},{3,0},{4,5},{5,6},{6,7},{7,4},{8,9},{9,10},{10,1... | collective-permute-start | bytes 1572872 | tf_op jit(solution)/shard_map/ppermute | solution.py:24
  106.6 11.7 %collective-permute-start.16 = (bf16[2,512,256]{2,1,0:T(8,128)(2,1)S(1)}, bf16[2,512,256]{2,1,0:T(8,128)(2,1)}, u32[]{:S(2)}, u32[]{:S(2)}) collective-permute-start(bf16[2,512,256]{2,1,0:T(8,128)(2,1)S(1)} %slice.553), channel_id=1, source_target_pairs={{0,3},{1,0},{2,1},{3,2},{4,7},{5,4},{6,5},{7,6},{8,11},{9,8},{10,9... | collective-permute-start | bytes 1572872 | tf_op jit(solution)/shard_map/ppermute | solution.py:24
  144.9 14.5 %collective-permute-start.18 = (bf16[256,1024]{1,0:T(8,128)(2,1)S(1)}, bf16[256,1024]{1,0:T(8,128)(2,1)S(1)}, u32[]{:S(2)}, u32[]{:S(2)}) collective-permute-start(bf16[256,1024]{1,0:T(8,128)(2,1)S(1)} %add_convert_fusion.6), channel_id=1, source_target_pairs={{0,64},{1,65},{2,66},{3,67},{4,68},{5,69},{6,70},{7,71},{8,72},{9,... | collective-permute-start | bytes 1572872 | tf_op jit(solution)/shard_map/ppermute | solution.py:592
  243.3 15.3 %collective-permute-start.25 = (bf16[256,1024]{1,0:T(8,128)(2,1)S(1)}, bf16[256,1024]{1,0:T(8,128)(2,1)S(1)}, u32[]{:S(2)}, u32[]{:S(2)}) collective-permute-start(bf16[256,1024]{1,0:T(8,128)(2,1)S(1)} %fusion.8), channel_id=1, source_target_pairs={{64,0},{65,1},{66,2},{67,3},{68,4},{69,5},{70,6},{71,7},{72,8},{73... | collective-permute-start | bytes 1572872 | tf_op jit(solution)/shard_map/ppermute | solution.py:629
  295.3 123.0 %reduce-scatter.5.cloned.1.call-start = ((), (), s32[]{:S(2)}) async-start(), calls=%async_computation.3 | async-start | bytes 4259840 | tf_op jit(solution)/shard_map/reduce_scatter | solution.py:646
  303.2 26.1 %collective-permute-start.28 = (bf16[512,1024]{1,0:T(8,128)(2,1)}, bf16[512,1024]{1,0:T(8,128)(2,1)}, u32[]{:S(2)}, u32[]{:S(2)}) collective-permute-start(bf16[512,1024]{1,0:T(8,128)(2,1)} %get-tuple-element.124), channel_id=1, source_target_pairs={{0,16},{16,32},{32,48},{48,0},{1,17},{17,33},{33,49},{49,1},{2,18}... | collective-permute-start | bytes 3145736 | tf_op jit(solution)/shard_map/ppermute | solution.py:24
  304.5 24.9 %collective-permute-start.29 = (bf16[512,1024]{1,0:T(8,128)(2,1)}, bf16[512,1024]{1,0:T(8,128)(2,1)}, u32[]{:S(2)}, u32[]{:S(2)}) collective-permute-start(bf16[512,1024]{1,0:T(8,128)(2,1)} %get-tuple-element.123), channel_id=1, source_target_pairs={{0,48},{16,0},{32,16},{48,32},{1,49},{17,1},{33,17},{49,33},{2,50}... | collective-permute-start | bytes 3145736 | tf_op jit(solution)/shard_map/ppermute | solution.py:24
  351.3 174.3 %all-gather.3.cloned.1.call-start = ((), (), s32[]{:S(2)}) async-start(), calls=%async_computation.4 | async-start | bytes 4997120 | tf_op jit(solution)/shard_map/all_gather | solution.py:661
  356.1 48.8 %collective-permute-start.31 = (bf16[1024,1024]{1,0:T(8,128)(2,1)}, bf16[1024,1024]{1,0:T(8,128)(2,1)}, u32[]{:S(2)}, u32[]{:S(2)}) collective-permute-start(bf16[1024,1024]{1,0:T(8,128)(2,1)} %fusion.3), channel_id=1, source_target_pairs={{0,16},{16,32},{32,48},{48,0},{1,17},{17,33},{33,49},{49,1},{2,18}... | collective-permute-start | bytes 6291464 | tf_op jit(solution)/shard_map/ppermute | solution.py:24
  360.2 47.3 %collective-permute-start.32 = (bf16[1024,1024]{1,0:T(8,128)(2,1)}, bf16[1024,1024]{1,0:T(8,128)(2,1)}, u32[]{:S(2)}, u32[]{:S(2)}) collective-permute-start(bf16[1024,1024]{1,0:T(8,128)(2,1)} %pad_maximum_fusion.2), channel_id=1, source_target_pairs={{0,48},{16,0},{32,16},{48,32},{1,49},{17,1},{33,17},{49,33},{2,50}... | collective-permute-start | bytes 6291464 | tf_op jit(solution)/shard_map/ppermute | solution.py:24
  413.2 18.3 %collective-permute-start.33 = (bf16[256,1024]{1,0:T(8,128)(2,1)S(1)}, bf16[256,1024]{1,0:T(8,128)(2,1)S(1)}, u32[]{:S(2)}, u32[]{:S(2)}) collective-permute-start(bf16[256,1024]{1,0:T(8,128)(2,1)S(1)} %get-tuple-element.116), channel_id=1, source_target_pairs={{0,1},{1,2},{2,3},{3,0},{4,5},{5,6},{6,7},{7,4},{8,9},{9,10},{10,1... | collective-permute-start | bytes 1572872 | tf_op jit(solution)/shard_map/ppermute | solution.py:24
  413.3 19.6 %collective-permute-start.34 = (bf16[256,1024]{1,0:T(8,128)(2,1)S(1)}, bf16[256,1024]{1,0:T(8,128)(2,1)}, u32[]{:S(2)}, u32[]{:S(2)}) collective-permute-start(bf16[256,1024]{1,0:T(8,128)(2,1)S(1)} %get-tuple-element.117), channel_id=1, source_target_pairs={{0,3},{1,0},{2,1},{3,2},{4,7},{5,4},{6,5},{7,6},{8,11},{9,8},{10,9... | collective-permute-start | bytes 1572872 | tf_op jit(solution)/shard_map/ppermute | solution.py:24
  416.0 22.5 %collective-permute-start.35 = (bf16[256,1024]{1,0:T(8,128)(2,1)S(1)}, bf16[256,1024]{1,0:T(8,128)(2,1)}, u32[]{:S(2)}, u32[]{:S(2)}) collective-permute-start(bf16[256,1024]{1,0:T(8,128)(2,1)S(1)} %get-tuple-element.118), channel_id=1, source_target_pairs={{0,2},{1,3},{2,0},{3,1},{4,6},{5,7},{6,4},{7,5},{8,10},{9,11},{10,... | collective-permute-start | bytes 1572872 | tf_op jit(solution)/shard_map/ppermute | solution.py:24
  428.4 12.3 %collective-permute-start.36 = (bf16[232,1024]{1,0:T(8,128)(2,1)S(1)}, bf16[232,1024]{1,0:T(8,128)(2,1)S(1)}, u32[]{:S(2)}, u32[]{:S(2)}) collective-permute-start(bf16[232,1024]{1,0:T(8,128)(2,1)S(1)} %pad_maximum_fusion.10), channel_id=1, source_target_pairs={{0,16},{16,32},{32,48},{48,0},{1,17},{17,33},{33,49},{49,1},{2,18}... | collective-permute-start | bytes 1425416 | tf_op jit(solution)/shard_map/ppermute | solution.py:24
  431.5 20.3 %collective-permute-start.38 = (bf16[232,1024]{1,0:T(8,128)(2,1)S(1)}, bf16[232,1024]{1,0:T(8,128)(2,1)S(1)}, u32[]{:S(2)}, u32[]{:S(2)}) collective-permute-start(bf16[232,1024]{1,0:T(8,128)(2,1)S(1)} %pad_maximum_fusion.12), channel_id=1, source_target_pairs={{0,32},{16,48},{32,0},{48,16},{1,33},{17,49},{33,1},{49,17},{2,34}... | collective-permute-start | bytes 1425416 | tf_op jit(solution)/shard_map/ppermute | solution.py:24
  452.2 23.1 %collective-permute-start.39 = (bf16[488,1024]{1,0:T(8,128)(2,1)S(1)}, bf16[488,1024]{1,0:T(8,128)(2,1)S(1)}, u32[]{:S(2)}, u32[]{:S(2)}) collective-permute-start(bf16[488,1024]{1,0:T(8,128)(2,1)S(1)} %pad_maximum_fusion.7), channel_id=1, source_target_pairs={{0,8},{8,0},{1,9},{9,1},{2,10},{10,2},{3,11},{11,3},{4,12},{12,4},... | collective-permute-start | bytes 2998280 | tf_op jit(solution)/shard_map/ppermute | solution.py:24
  (71 other events, 804.2 us)
Sparse Core Ops, SparseCore 0:
  295.4 47.1 reduce-scatter.2
  351.4 40.4 reduce-scatter.4
  476.8 48.7 all-gather.2

commit v3 on v2

--- a/solution.py
+++ b/solution.py
@@ -33,6 +33,10 @@
 
 def plus(first, second):
     return (first.astype(f32) + second.astype(f32)).astype(bf16)
+
+
+def after(value, *others):
+    return lax.optimization_barrier((value, *others))[0]
 
 
 def ring3(value, axis):
@@ -214,7 +218,7 @@
         out_shape=[shape_of((512, w), bf16) for w in (D, 512, 512, 512, 512, D)],
         scratch_shapes=attention_buffers(),
         compiler_params=params(),
-        cost_estimate=pl.CostEstimate(flops=6 * 10**9, bytes_accessed=10 * 2**20, transcendentals=10**6),
+        cost_estimate=pl.CostEstimate(flops=1, bytes_accessed=1, transcendentals=0),
         name="attention_forward",
     )(x, gain, *w_attn, cosine, sine, bias)
 
@@ -329,7 +333,7 @@
         out_shape=out_shape,
         scratch_shapes=scratch,
         compiler_params=params(),
-        cost_estimate=pl.CostEstimate(flops=7 * 10**9, bytes_accessed=24 * 2**20, transcendentals=10**6),
+        cost_estimate=pl.CostEstimate(flops=1, bytes_accessed=1, transcendentals=0),
         name="expert_forward",
     )(x, part, far, gain, router, chosen, *weights)
 
@@ -399,22 +403,98 @@
         + [pltpu.VMEM((512, 2048), bf16)] * 4
         + [pltpu.SemaphoreType.DMA((4 * OWN,))],
         compiler_params=params(),
-        cost_estimate=pl.CostEstimate(flops=7 * 10**9, bytes_accessed=24 * 2**20, transcendentals=10**6),
+        cost_estimate=pl.CostEstimate(flops=1, bytes_accessed=1, transcendentals=0),
         name="expert_backward",
     )(grad, total, far, gates, router, a, b, *weights)
 
 
-def spread_kernel(pair, pair_far, low, low_far, attn, attn_far, mix, mix_far, gate, up, down, query, key, value, out):
+def expert_grads_kernel(n_ref, a_ref, b_ref, *refs):
+    *outs, turned_ref = refs
+
+    @pl.when(pl.program_id(0) == 0)
+    def _():
+        turned_ref[...] = n_ref[...].T
+
+    for i in range(4):
+        rows = slice(256 * i, 256 * (i + 1))
+        if len(outs) == 1:
+            out, at = outs[0].at[0], rows
+        else:
+            out, at = outs[i // 2], slice(256 * (i % 2), 256 * (i % 2 + 1))
+        out[at, :FF] = dot(turned_ref[rows], a_ref[...]).astype(bf16)
+        out[at, FF:] = dot(turned_ref[rows], b_ref[...]).astype(bf16)
+
+
+def expert_grads(normed, gate_grad, up_grad, far):
+    if far:
+        slots = spec((512, FF), lambda e: (0, 2))
+        out_specs, out_shape = [fixed((512, D))] * 2, [shape_of((512, D), bf16)] * 2
+    else:
+        slots = spec((512, FF), lambda e: (0, e + e // 2))
+        out_specs, out_shape = spec((1, D, D), lambda e: (e, 0, 0)), shape_of((3, D, D), bf16)
+    return pl.pallas_call(
+        expert_grads_kernel,
+        grid=(1 if far else 3,),
+        in_specs=[fixed((512, D)), slots, slots],
+        out_specs=out_specs,
+        out_shape=out_shape,
+        scratch_shapes=[pltpu.VMEM((D, 512), bf16)],
+        compiler_params=params(),
+        cost_estimate=pl.CostEstimate(flops=1, bytes_accessed=1, transcendentals=0),
+        name="expert_grads",
+    )(normed, gate_grad, up_grad)
+
+
+def attention_grads_kernel(n_ref, qkv_ref, o_ref, a_ref, small_ref, out_ref):
+    out_ref[0, :256] = t_dot(n_ref[...], qkv_ref[...]).astype(bf16)
+    out_ref[0, 256:384] = t_dot(o_ref[...], a_ref[...]).astype(bf16)
+    out_ref[0, 384:] = jnp.concatenate([small_ref[...], jnp.zeros((32, D - 256), bf16)], -1)
+
+
+def attention_grads(normed, qkv_grad, mixed, grad_attn, small):
+    return pl.pallas_call(
+        attention_grads_kernel,
+        grid=(4,),
+        in_specs=[
+            spec((512, 256), lambda s: (0, s)), fixed((512, D)), spec((512, ROW), lambda s: (0, s)),
+            fixed((512, D)), spec((32, 256), lambda s: (0, s)),
+        ],
+        out_specs=spec((1, 416, D), lambda s: (s, 0, 0)),
+        out_shape=shape_of((4, 416, D), bf16),
+        compiler_params=params(),
+        cost_estimate=pl.CostEstimate(flops=1, bytes_accessed=1, transcendentals=0),
+        name="attention_grads",
+    )(normed, qkv_grad, mixed, grad_attn, small)
+
+
+def sides(near, far):
     first = lax.axis_index("core") == 0
-
-    def sides(near, far):
-        near, far = near.astype(f32), far.astype(f32)
-        return jnp.where(first, near, far), jnp.where(first, far, near)
-
+    near, far = near.astype(f32), far.astype(f32)
+    return jnp.where(first, near, far), jnp.where(first, far, near)
+
+
+def spread_pair_kernel(pair, pair_far, gate, up):
     for y in range(4):
         for c, side in enumerate(sides(pair[y], pair_far[y])):
             gate[:, 4 * c + y, :] = side[:, :FF]
             up[:, 4 * c + y, :] = side[:, FF:]
+
+
+def spread_pair(packed, theirs):
+    return pl.pallas_call(
+        spread_pair_kernel,
+        grid=(4,),
+        in_specs=[spec((4, 64, D), lambda i: (0, i, 0))] * 2,
+        out_specs=[spec((64, 8, FF), lambda i: (i, 0, 0))] * 2,
+        out_shape=[shape_of((256, 8, FF), f32)] * 2,
+        compiler_params=params(),
+        cost_estimate=pl.CostEstimate(flops=1, bytes_accessed=1, transcendentals=0),
+        name="spread_pair",
+    )(packed, theirs)
+
+
+def spread_rest_kernel(low, low_far, attn, attn_far, mix, mix_far, down, query, key, value, out):
+    for y in range(4):
         for c, side in enumerate(sides(low[y], low_far[y])):
             down[4 * c + y] = side
     for c, side in enumerate(sides(mix[0], mix_far[0])):
@@ -432,20 +512,17 @@
             to[:, 256 * h + ROW : 256 * (h + 1)] = jnp.where(below, pltpu.roll(a, HEAD_DIM, 1), b)
 
 
-def spread(packed, theirs):
+def spread_rest(packed, theirs):
     specs = [
-        spec((4, 64, D), lambda i: (0, i, 0)),
-        spec((4, ROW, 256), lambda i: (0, 2, i)),
-        spec((1, 64, D), lambda i: (i, 6, 0)),
-        spec((1, 32, D), lambda i: (i, 14, 0)),
+        spec((4, ROW, 256), lambda i: (0, 0, i)),
+        spec((1, 64, D), lambda i: (i, 2, 0)),
+        spec((1, 32, D), lambda i: (i, 6, 0)),
     ]
     return pl.pallas_call(
-        spread_kernel,
+        spread_rest_kernel,
         grid=(4,),
         in_specs=[item for item in specs for _ in range(2)],
         out_specs=[
-            spec((64, 8, FF), lambda i: (i, 0, 0)),
-            spec((64, 8, FF), lambda i: (i, 0, 0)),
             spec((8, ROW, 256), lambda i: (0, i, 0)),
             spec((64, D), lambda i: (i, 0)),
             spec((64, 512), lambda i: (i, 0)),
@@ -453,13 +530,12 @@
             spec((2, 32, D), lambda i: (0, i, 0)),
         ],
         out_shape=[
-            shape_of(shape, f32)
-            for shape in ((256, 8, FF), (256, 8, FF), (8, FF, 256), (256, D), (256, 512), (256, 512), (2, ROW, D))
+            shape_of(shape, f32) for shape in ((8, FF, 256), (256, D), (256, 512), (256, 512), (2, ROW, D))
         ],
         compiler_params=params(),
-        cost_estimate=pl.CostEstimate(flops=10**6, bytes_accessed=24 * 2**20, transcendentals=0),
-        name="spread",
-    )(*[packed, theirs] * 4)
+        cost_estimate=pl.CostEstimate(flops=1, bytes_accessed=1, transcendentals=0),
+        name="spread_rest",
+    )(*[packed, theirs] * 3)
 
 
 def norm_backward(grad_normed, value, gain):
@@ -530,7 +606,7 @@
         out_shape=[shape_of((512, D), f32)] + [shape_of((512, D), bf16)] * 3 + [shape_of((1, D), f32)],
         scratch_shapes=[pltpu.VMEM((256, 512), bf16)] + attention_buffers(),
         compiler_params=params(),
-        cost_estimate=pl.CostEstimate(flops=9 * 10**9, bytes_accessed=16 * 2**20, transcendentals=10**6),
+        cost_estimate=pl.CostEstimate(flops=1, bytes_accessed=1, transcendentals=0),
         name="attention_backward",
     )(grad, hidden, near, far, gain, *w_attn, query, keys, values, cosine, sine, bias)
 
@@ -551,8 +627,8 @@
     k_own = lax.dynamic_index_in_dim(w_key[0].reshape(256, 4, 2, 64), core, 2, False).reshape(256, 256)
     v_own = lax.dynamic_index_in_dim(w_value[0].reshape(256, 4, 2, 64), core, 2, False).reshape(256, 256)
     out_own = lax.dynamic_slice_in_dim(w_out[0], core * 128, 128, 0)
-    small = jnp.concatenate([gain_attn[0], gain_ffn[0], w_router[0].T.reshape(2048)])
-    small = jnp.concatenate([small, jnp.zeros((16 * D - 2560,), bf16)]).reshape(16, D)
+    small = jnp.concatenate([gain_attn[0][None], gain_ffn[0][None], w_router[0].T], 0)
+    small = jnp.pad(small, ((0, 6), (0, D - 256)))
     attn_own = jnp.concatenate([jnp.concatenate([q_own, k_own, v_own], -1), out_own, small], 0)
     down_own = involute(lax.dynamic_slice_in_dim(w_down[0], core * OWN, OWN, 0), 0, y_at)
     attn_own, down_own, pair = lax.optimization_barrier((attn_own, down_own, pair))
@@ -560,10 +636,10 @@
     attn_all = ring3(attn_own, "x")
     down_left, down_right = pp(down_own, "x", 1), pp(down_own, "x", -1)
     far_gate, far_up = pp(left[:1], "y", 1), pp(right[1:], "y", -1)
+    start = both(inputs.reshape(256, D))
     down_far, down_far_too = pp(down_left[:2], "x", 1), pp(down_right[2:], "x", -1)
     weights = (pair, left, far_gate, far_up, right, down_own, down_left, down_far, down_far_too, down_right)
-    small_all = jnp.concatenate([v[384:387].reshape(12, 256) for v in attn_all], -1)
-    small_all = involute(small_all, 1, x_at)
+    small_all = involute(jnp.concatenate([v[384:394, :256] for v in attn_all], -1), 1, x_at)
     gain_one = small_all[:1].astype(f32)
     gain_two = small_all[1:2].astype(f32)
 
@@ -578,7 +654,6 @@
     chosen = jnp.sum((ids[:, :, None] == slots).astype(f32), 1)
     router = t_dot(small_all[2:10], (jnp.arange(8)[:, None] == slots).astype(bf16)).astype(bf16)
 
-    start = both(inputs.reshape(256, D))
     x = start
     for phase in range(2):
         normed, query, keys, values, mixed, part = attention_forward(x, gain_one, attn_all, place)
@@ -601,25 +676,19 @@
             grad, total, total_far, gates, router, gate_in, up_in, weights
         )
         if phase == 1:
-            down_grad = t_dot(acted, grad).astype(bf16).reshape(OWN, FF, D)
-            gate_grad = t_dot(normed_two, gate_grad).astype(bf16)
-            up_grad = t_dot(normed_two, up_grad).astype(bf16)
-            part, gate_grad, up_grad, down_grad = lax.optimization_barrier(
-                (part, gate_grad, up_grad, down_grad)
-            )
-            blocks = [
-                jnp.concatenate([gate_grad[:, FF * e : FF * (e + 1)], up_grad[:, FF * e : FF * (e + 1)]], -1)
-                for e in range(OWN)
-            ]
-            far_sent = (pp(blocks[2][:512], "y", 1), pp(blocks[2][512:], "y", -1))
-            down_sum = lax.psum_scatter(down_grad, "x", scatter_dimension=2, tiled=True)
+            far_grads = expert_grads(normed_two, gate_grad, up_grad, True)
+            far_sent = (pp(far_grads[0], "y", 1), pp(far_grads[1], "y", -1))
+            near_grads = expert_grads(after(normed_two, *far_grads), gate_grad, up_grad, False)
+            part = after(part, near_grads)
         grad_hidden, grad_attn, qkv_grad, part, gain_two_grad = attention_backward(
             grad, hidden, part, other(part), gain_two, attn_all, query, keys, values, place
         )
         if phase == 1:
-            far_sent, part = lax.optimization_barrier((far_sent, part))
-            ahead = jnp.concatenate([plus(blocks[3][:512], far_sent[0]), blocks[3][512:]], 0)
-            behind = jnp.concatenate([blocks[1][:512], plus(blocks[1][512:], far_sent[1])], 0)
+            far_sent = (after(far_sent[0], part), after(far_sent[1], part))
+            ahead = jnp.concatenate([plus(near_grads[2, :512], far_sent[0]), near_grads[2, 512:]], 0)
+            behind = jnp.concatenate([near_grads[1, :512], plus(near_grads[1, 512:], far_sent[1])], 0)
+            part = after(part, ahead, behind)
+            qkv_grad = after(qkv_grad, ahead, behind)
             ahead, behind = pp(ahead, "y", 1), pp(behind, "y", -1)
         far = other(part)
         grad_normed = part[:256].astype(f32) + far[256:].astype(f32)
@@ -629,24 +698,22 @@
             received = lax.ppermute(own_grad, "section", [(1, 0)])
             grad = jnp.where(section == 1, first, both(received))
 
+    down_grad = t_dot(after(acted, *far_grads), grad).astype(bf16).reshape(OWN, FF, D)
+    down_sum = lax.psum_scatter(down_grad, "x", scatter_dimension=2, tiled=True)
     router_grad = t_dot(normed_two, logit_grad)[:, :OWN]
-    qkv_grad = t_dot(normed, qkv_grad).astype(bf16)
-    out_grad = t_dot(mixed, grad_attn).astype(bf16)
     placed = jnp.zeros((8, D), f32)
     placed = lax.dynamic_update_slice_in_dim(placed, involute(router_grad.T, 0, y_at), core * OWN, 0)
-    small_grads = jnp.concatenate([gain_one_grad, gain_two_grad, placed], 0).astype(bf16)
-
-    def block(s):
-        small = small_grads[:, 256 * s : 256 * (s + 1)].reshape(2560)
-        small = jnp.concatenate([small, jnp.zeros((32 * D - 2560,), bf16)]).reshape(32, D)
-        return jnp.concatenate(
-            [qkv_grad[256 * s : 256 * (s + 1)], out_grad[128 * s : 128 * (s + 1)], small], 0
-        )
-
-    attn_sum = lax.psum_scatter(jnp.stack([block(s) for s in range(4)], 0), "x", scatter_dimension=0)
-    pair_sum = (blocks[0].astype(f32) + ahead.astype(f32) + behind.astype(f32)).astype(bf16)
-    pair_sum = involute(pair_sum, 0, x_at)
-    pair_sum = scatter3([pair_sum[256 * s : 256 * (s + 1)] for s in range(4)], "x")
+    small_grads = jnp.concatenate([gain_one_grad, gain_two_grad, placed, jnp.zeros((22, D), f32)], 0)
+    attn_grads = attention_grads(normed, qkv_grad, mixed, grad_attn, small_grads.astype(bf16))
+    attn_sum = lax.psum_scatter(attn_grads, "x", scatter_dimension=0)
+    down_sum = after(down_sum, attn_grads)
+    down_sum = plus(down_sum, pp(down_sum, "zh", 1))
+
+    ahead, behind = after(ahead, down_sum), after(behind, down_sum)
+    pair_sum = (near_grads[0].astype(f32) + ahead.astype(f32) + behind.astype(f32)).astype(bf16)
+    pair_sum = lax.psum_scatter(pair_sum.reshape(4, 256, D), "x", scatter_dimension=0)
+    attn_sum = plus(attn_sum, pp(attn_sum, "zh", 1))
+
     parts = [(attn_sum[:256], 64), (attn_sum[256:384], 32), (attn_sum[384:], 8)]
     parts = [(involute(part, 0, y_at), size) for part, size in parts]
 
@@ -654,15 +721,18 @@
         down = jnp.concatenate([down_sum[e, ROW * i : ROW * (i + 1)] for i in range(4)], -1)
         return jnp.concatenate([down] + [part[size * e : size * (e + 1)] for part, size in parts], 0)
 
-    rest_sum = scatter3([rest(e) for e in range(OWN)], "y")
-
-    packed = jnp.concatenate([pair_sum, rest_sum], 0)
-    packed = plus(packed, pp(packed, "zh", 1))
-    packed = lax.all_gather(packed, "y")
-    theirs = other(packed)
-    grad_gate, grad_up, grad_down, grad_query, grad_key, grad_value, grad_out = spread(packed, theirs)
+    rest_blocks = [rest(e) for e in range(OWN)]
+    rest_sum = scatter3(rest_blocks, "y")
+    pair_sum = plus(pair_sum, pp(pair_sum, "zh", 1))
+    pair_all = lax.all_gather(pair_sum, "y")
+    rest_all = lax.all_gather(rest_sum, "y")
+    rest_far = other(rest_all)
+    pair_far = other(pair_all)
+    grad_gate, grad_up = spread_pair(pair_all, pair_far)
+    grad_down, grad_query, grad_key, grad_value, grad_out = spread_rest(rest_all, rest_far)
     grad_out = grad_out.reshape(256, D)
-    small_sum = (packed[0, 480:483].astype(f32) + theirs[0, 480:483].astype(f32)).reshape(12, 256)
+    small_sum = rest_all[:2, 224:, :256].astype(f32) + rest_far[:2, 224:, :256].astype(f32)
+    small_sum = small_sum.reshape(16, 256)
 
     outputs = own_out.reshape(2, ROW, D)
     input_grads = own_grad.reshape(2, ROW, D)

time: 563 us -> 526 us (0.934)
  local copies, waits for them, and re-layouts: 62 us -> 27.9 us
  Pallas kernels: 126 us -> 146 us
  matrix products: 20 us -> 6.02 us
  waiting for transfers between devices: 229 us -> 219 us
    ppermute x39, waiting for transfers between devices: 155 us -> 112 us  [pp(): lax.ppermute(value, axis, [(i, (i + step) % count) for i in range(count)])]
    reduce_scatter x1 -> x2, waiting for transfers between devices: 0.01 us -> 34.8 us  [the longest x1 34.8 us: local(): attn_sum = lax.psum_scatter(attn_grads, 'x', scatter_dimension=0)]
    pallas_call x1 -> x5, Pallas kernels: 10.1 us -> 30.3 us  [the longest x2 11.8 us: expert_grads(): pl.pallas_call(expert_grads_kernel, grid=(1 if far else 3,), in_specs=[fi...]
    dot_general x7 -> x3, matrix products: 20 us -> 6.02 us  [t_dot(): lax.dot_general(left, right, (((0,), (0,)), ((), ())), preferred_element_...]
    slice x10 -> x0, local copies, waits for them, and re-layouts: 11.6 us -> none  [the longest x1 4.04 us: local(): gate_grad[:, FF * e:FF * (e + 1)]]
    unnamed x162 -> x119, local copies, waits for them, and re-layouts: 22.8 us -> 12.2 us
    all_gather x1 -> x2, waiting for transfers between devices: 48.9 us -> 47.7 us  [the longest x1 32.3 us: local(): pair_all = lax.all_gather(pair_sum, 'y')]
  transfers between devices with their start and end apart: 44 -> 46, of which waited for: 24 -> 26; matrix products, arithmetic and copies ran while one was open for 16% -> 11% of each run, Pallas kernels for 5% -> 9%
where the time goes in v3:
time: 526 us; the launch traced here: 518 us
  waiting for transfers between devices  219 us (42%)
  Pallas kernels  146 us (28%)
  starting transfers between devices  58 us (11%)
  other arithmetic  45.5 us (9%)
  local copies, waits for them, and re-layouts  27.9 us (5%)
  between operations  14.9 us (3%)
  matrix products  6.02 us (1%)
    ppermute x39, waiting for transfers between devices, pp(): lax.ppermute(value, axis, [(i, (i + step) % count) for i in range(count)])  112 us
    ppermute x39, starting transfers between devices, pp(): lax.ppermute(value, axis, [(i, (i + step) % count) for i in range(count)])  53 us
    pallas_call x2, Pallas kernels, expert_backward(): pl.pallas_call(expert_backward_kernel, in_specs=[whole()] * 5 + [afar()]...  36.1 us
    reduce_scatter x1, waiting for transfers between devices, local(): attn_sum = lax.psum_scatter(attn_grads, 'x', scatter_dimension=0)  34.8 us
    pallas_call x2, Pallas kernels, attention_backward(): pl.pallas_call(attention_backward_kernel, grid=(2,), in_specs=[rows_spec(...  33.1 us
    all_gather x1, waiting for transfers between devices, local(): pair_all = lax.all_gather(pair_sum, 'y')  32.3 us
    pallas_call x2, Pallas kernels, expert_forward(): pl.pallas_call(functools.partial(expert_forward_kernel, save), in_specs=[...  28.1 us
    pallas_call x2, Pallas kernels, attention_forward(): pl.pallas_call(attention_forward_kernel, grid=(2,), in_specs=[rows_spec(D...  18.6 us
  transfers between devices with their start and end apart: 46, of which 26 were waited for; matrix products, arithmetic and copies ran while one was open for 11% of the time, Pallas kernels for 9%

profile of v3, /device:TPU:1, one launch (start us, length us, event | category | flops | bytes accessed | tf_op | source)
XLA Modules:
  0.0 517.7 jit_solution(4070169589800129733)
XLA Ops:
  31.4 7.7 %collective-permute-done.2 = bf16[2,256,512]{2,1,0:T(8,128)(2,1)} collective-permute-done((bf16[2,256,512]{2,1,0:T(8,128)(2,1)}, bf16[2,256,512]{2,1,0:T(8,128)(2,1)}, u32[]{:S(2)}, u32[]{:S(2)}) %collective-permute-start.2) | collective-permute-done | bytes 524320 | tf_op jit(solution)/shard_map/ppermute | solution.py:24
  52.5 26.0 %collective-permute-done.4.refs_3_ = bf16[400,1024]{1,0:T(8,128)(2,1)S(1)} collective-permute-done((bf16[400,1024]{1,0:T(8,128)(2,1)S(1)}, bf16[400,1024]{1,0:T(8,128)(2,1)S(1)}, u32[]{:S(2)}, u32[]{:S(2)}) %collective-permute-start.4) | collective-permute-done | bytes 819232 | tf_op jit(solution)/shard_map/ppermute | solution.py:24
  78.5 3.8 collective-permute-start.15
  84.1 9.3 %attention_forward.2 = (bf16[512,1024]{1,0:T(8,128)(2,1)}, bf16[512,512]{1,0:T(8,128)(2,1)}, bf16[512,512]{1,0:T(8,128)(2,1)}, bf16[512,512]{1,0:T(8,128)(2,1)},...) custom-call(bf16[512,1024]{1,0:T(8,128)(2,1)} %pad_maximum_fusion.3.x_ref.refs_0_, ...), custom_call_target="tpu_custom_call" | custom-call | flops 1 | bytes 1 | tf_op jit(solution)/shard_map/attention_forward/pallas_call | solution.py:210
  100.1 4.2 collective-permute-done.13.refs_12_.refs_13_
  111.5 6.6 %collective-permute-done.14.refs_13_.refs_14_ = bf16[2,512,256]{2,1,0:T(8,128)(2,1)S(1)} collective-permute-done((bf16[2,512,256]{2,1,0:T(8,128)(2,1)S(1)}, bf16[2,512,256]{2,1,0:T(8,128)(2,1)S(1)}, u32[]{:S(2)}, u32[]{:S(2)}) %collective-permute-start.14) | collective-permute-done | bytes 524320 | tf_op jit(solution)/shard_map/ppermute | solution.py:24
  118.2 4.5 collective-permute-done.10.refs_8_.refs_9_
  124.2 13.1 %expert_forward.2 = (f32[512,1024]{1,0:T(8,128)}, bf16[512,1024]{1,0:T(8,128)(2,1)}) custom-call(bf16[512,1024]{1,0:T(8,128)(2,1)} %pad_maximum_fusion.3.x_ref.refs_0_, bf16[512,1024]{1,0:T(8,128)(2,1)} %get-tuple-element.63.refs_1_, bf16[512,1024]{1,0:T(8,128)(2,1)} %collective-permute-done.8.refs_2_, f32[1,1024]{1,0:T(1,128)} %get-tuple-element.152.refs_3_.gain_ref, ...), custom_call_target="tpu_custom_call" | custom-call | flops 1 | bytes 1 | tf_op jit(solution)/shard_map/expert_forward/pallas_call | solution.py:329
  143.1 3.5 collective-permute-start.18
  146.7 10.9 %collective-permute-done.18 = bf16[256,1024]{1,0:T(8,128)(2,1)S(1)} collective-permute-done((bf16[256,1024]{1,0:T(8,128)(2,1)S(1)}, bf16[256,1024]{1,0:T(8,128)(2,1)S(1)}, u32[]{:S(2)}, u32[]{:S(2)}) %collective-permute-start.18) | collective-permute-done | bytes 524320 | tf_op jit(solution)/shard_map/ppermute | solution.py:667
  162.9 9.3 %attention_forward.3 = (bf16[512,1024]{1,0:T(8,128)(2,1)}, bf16[512,512]{1,0:T(8,128)(2,1)}, bf16[512,512]{1,0:T(8,128)(2,1)}, bf16[512,512]{1,0:T(8,128)(2,1)},...) custom-call(bf16[512,1024]{1,0:T(8,128)(2,1)} %maximum_select_fusion.x_ref.refs_0_, ...), custom_call_target="tpu_custom_call" | custom-call | flops 1 | bytes 1 | tf_op jit(solution)/shard_map/attention_forward/pallas_call | solution.py:210
  176.2 15.0 %expert_forward.3 = (f32[512,1024]{1,0:T(8,128)}, bf16[512,1024]{1,0:T(8,128)(2,1)}, bf16[512,1024]{1,0:T(8,128)(2,1)}, f32[512,128]{1,0:T(8,128)}, bf16[512,204...) custom-call(bf16[512,1024]{1,0:T(8,128)(2,1)} %maximum_select_fusion.x_ref.refs_0_, ...), custom_call_target="tpu_custom_call" | custom-call | flops 1 | bytes 1 | tf_op jit(solution)/shard_map/expert_forward/pallas_call | solution.py:329
  195.8 18.1 %expert_backward.2 = (bf16[512,128]{1,0:T(8,128)(2,1)}, bf16[512,1024]{1,0:T(8,128)(2,1)}, bf16[512,2048]{1,0:T(8,128)(2,1)}, bf16[512,2048]{1,0:T(8,128)(2,1)}) custom-call(bf16[512,1024]{1,0:T(8,128)(2,1)} %pad_maximum_fusion.4.refs_0_.grad_ref, bf16[512,1024]{1,0:T(8,128)(2,1)} %get-tuple-element.70.refs_1_, ...), custom_call_target="tpu_custom_call" | custom-call | flops 1 | bytes 1 | tf_op jit(solution)/shard_map/expert_backward/pallas_call | solution.py:396
  217.8 16.6 %attention_backward.2 = (f32[512,1024]{1,0:T(8,128)}, bf16[512,1024]{1,0:T(8,128)(2,1)}, bf16[512,1024]{1,0:T(8,128)(2,1)}, bf16[512,1024]{1,0:T(8,128)(2,1)}, f32[1,1024]{1,0:T(1,128)}) custom-call(bf16[512,1024]{1,0:T(8,128)(2,1)} %pad_maximum_fusion.4.refs_0_.grad_ref, f32[512,1024]{1,0:T(8,128)} %get-tuple-element.69.h_ref, ...), custom_call_target="tpu_custom_call" | custom-call | flops 1 | bytes 1 | tf_op jit(solution)/shard_map/attention_backward/pallas_call | solution.py:596
  241.9 14.0 %collective-permute-done.25 = bf16[256,1024]{1,0:T(8,128)(2,1)S(1)} collective-permute-done((bf16[256,1024]{1,0:T(8,128)(2,1)S(1)}, bf16[256,1024]{1,0:T(8,128)(2,1)S(1)}, u32[]{:S(2)}, u32[]{:S(2)}) %collective-permute-start.25) | collective-permute-done | bytes 524320 | tf_op jit(solution)/shard_map/ppermute | solution.py:698
  260.3 18.1 %expert_backward.3 = (bf16[512,128]{1,0:T(8,128)(2,1)}, bf16[512,1024]{1,0:T(8,128)(2,1)}, bf16[512,2048]{1,0:T(8,128)(2,1)}, bf16[512,2048]{1,0:T(8,128)(2,1)}) custom-call(bf16[512,1024]{1,0:T(8,128)(2,1)} %maximum_select_fusion.1.refs_0_.grad_ref, bf16[512,1024]{1,0:T(8,128)(2,1)} %get-tuple-element.70.refs_1_, ...), custom_call_target="tpu_custom_call" | custom-call | flops 1 | bytes 1 | tf_op jit(solution)/shard_map/expert_backward/pallas_call | solution.py:396
  278.4 3.9 expert_grads.2
  282.3 4.6 convolution_convert_fusion
  287.0 7.9 %expert_grads.3 = bf16[3,1024,1024]{2,1,0:T(8,128)(2,1)} custom-call(bf16[512,1024]{1,0:T(8,128)(2,1)} %get-tuple-element.86.n_ref, bf16[512,2048]{1,0:T(8,128)(2,1)} %get-tuple-element.82.a_ref, bf16[512,2048]{1,0:T(8,128)(2,1)} %get-tuple-element.83.b_ref), custom_call_target="tpu_custom_call" | custom-call | flops 1 | bytes 1 | tf_op jit(solution)/shard_map/expert_grads/pallas_call | solution.py:435
  300.7 16.5 %attention_backward.3 = (f32[512,1024]{1,0:T(8,128)}, bf16[512,1024]{1,0:T(8,128)(2,1)}, bf16[512,1024]{1,0:T(8,128)(2,1)}, bf16[512,1024]{1,0:T(8,128)(2,1)}, f32[1,1024]{1,0:T(1,128)}) custom-call(bf16[512,1024]{1,0:T(8,128)(2,1)} %maximum_select_fusion.1.refs_0_.grad_ref, f32[512,1024]{1,0:T(8,128)} %get-tuple-element.69.h_ref, ...), custom_call_target="tpu_custom_call" | custom-call | flops 1 | bytes 1 | tf_op jit(solution)/shard_map/attention_backward/pallas_call | solution.py:596
  317.2 4.4 collective-permute-done.28
  331.7 5.9 %attention_grads.1 = bf16[4,416,1024]{2,1,0:T(8,128)(2,1)} custom-call(bf16[512,1024]{1,0:T(8,128)(2,1)} %get-tuple-element.95.n_ref, bf16[512,1024]{1,0:T(8,128)(2,1)} %get-tuple-element.97.qkv_ref, bf16[512,512]{1,0:T(8,128)(2,1)} %get-tuple-element.98.o_ref, bf16[512,1024]{1,0:T(8,128)(2,1)} %get-tuple-element.99.a_ref, ...), custom_call_target="tpu_custom_call" | custom-call | flops 1 | bytes 1 | tf_op jit(solution)/shard_map/attention_grads/pallas_call | solution.py:455
  343.7 34.8 %reduce-scatter.6.cloned.1.call-done = bf16[1,416,1024]{2,1,0:T(8,128)(2,1)} async-done(((bf16[4,416,1024]{2,1,0:T(8,128)(2,1)}), bf16[1,416,1024]{2,1,0:T(8,128)(2,1)}) %reduce-scatter.6.cloned.1.call-update) | async-done | bytes 851984 | tf_op jit(solution)/shard_map/reduce_scatter | solution.py:708
  386.1 5.6 %fusion.1 = bf16[1024,1024]{1,0:T(8,128)(2,1)} fusion(bf16[1024,1024]{1,0:T(8,128)(2,1)} %collective-permute-done.38, bf16[1024,1024]{1,0:T(8,128)(2,1)} %collective-permute-done.37, bf16[3,1024,1024]{2,1,0:T(8,128)(2,1)} %expert_grads.3), kind=kLoop, calls=%fused_computation.2 | loop fusion | flops 6291456 | bytes 8388608 | tf_op jit(solution)/shard_map/convert_element_type | solution.py:713
  391.9 8.5 %collective-permute-done.32 = bf16[416,1024]{1,0:T(8,128)(2,1)} collective-permute-done((bf16[416,1024]{1,0:T(8,128)(2,1)}, bf16[416,1024]{1,0:T(8,128)(2,1)}, u32[]{:S(2)}, u32[]{:S(2)}) %collective-permute-start.32) | collective-permute-done | bytes 852000 | tf_op jit(solution)/shard_map/ppermute | solution.py:24
  406.9 7.6 %collective-permute-done.33 = bf16[232,1024]{1,0:T(8,128)(2,1)S(1)} collective-permute-done((bf16[232,1024]{1,0:T(8,128)(2,1)S(1)}, bf16[232,1024]{1,0:T(8,128)(2,1)S(1)}, u32[]{:S(2)}, u32[]{:S(2)}) %collective-permute-start.33) | collective-permute-done | bytes 475168 | tf_op jit(solution)/shard_map/ppermute | solution.py:24
  414.5 11.0 %collective-permute-done.35 = bf16[232,1024]{1,0:T(8,128)(2,1)S(1)} collective-permute-done((bf16[232,1024]{1,0:T(8,128)(2,1)S(1)}, bf16[232,1024]{1,0:T(8,128)(2,1)S(1)}, u32[]{:S(2)}, u32[]{:S(2)}) %collective-permute-start.35) | collective-permute-done | bytes 475168 | tf_op jit(solution)/shard_map/ppermute | solution.py:24
  429.6 9.7 %collective-permute-done.39 = bf16[256,1024]{1,0:T(8,128)(2,1)S(1)} collective-permute-done((bf16[256,1024]{1,0:T(8,128)(2,1)}, bf16[256,1024]{1,0:T(8,128)(2,1)S(1)}, u32[]{:S(2)}, u32[]{:S(2)}) %collective-permute-start.39) | collective-permute-done | bytes 524320 | tf_op jit(solution)/shard_map/ppermute | solution.py:24
  441.3 15.5 %all-gather.5.cloned.1.call-done = bf16[928,1024]{1,0:T(8,128)(2,1)} async-done(((bf16[232,1024]{1,0:T(8,128)(2,1)}), bf16[928,1024]{1,0:T(8,128)(2,1)}) %all-gather.5.cloned.1.call-update) | async-done | bytes 1900560 | tf_op jit(solution)/shard_map/all_gather | solution.py:728
  457.5 32.3 %all-gather.7.cloned.1.call-done = bf16[1024,1024]{1,0:T(8,128)(2,1)} async-done(((bf16[256,1024]{1,0:T(8,128)(2,1)}), bf16[1024,1024]{1,0:T(8,128)(2,1)}) %all-gather.7.cloned.1.call-update) | async-done | bytes 2097168 | tf_op jit(solution)/shard_map/all_gather | solution.py:727
  495.0 5.6 %spread_rest.1 = (f32[8,512,256]{2,1,0:T(8,128)}, f32[256,1024]{1,0:T(8,128)}, f32[256,512]{1,0:T(8,128)}, f32[256,512]{1,0:T(8,128)}, f32[2,128,1024]{2,1,0:T(8,128)}) custom-call(bf16[4,232,1024]{2,1,0:T(8,128)(2,1)} %bitcast.149, bf16[4,232,1024]{2,1,0:T(8,128)(2,1)} %collective-permute-done.36.low_far.attn_far.mix_far, bf16[4,232,1024]{2,1,0:T(8,128)(2,1)} %bitcast.150, ...), custom_call_target="tpu_custom_call" | custom-call | flops 1 | bytes 1 | tf_op jit(solution)/shard_map/spread_rest/pallas_call | solution.py:521
  503.9 7.0 %spread_pair.1 = (f32[256,8,512]{2,1,0:T(8,128)}, f32[256,8,512]{2,1,0:T(8,128)}) custom-call(bf16[4,256,1024]{2,1,0:T(8,128)(2,1)} %bitcast.156, bf16[4,256,1024]{2,1,0:T(8,128)(2,1)} %copy-done.17), custom_call_target="tpu_custom_call" | custom-call | flops 1 | bytes 1 | tf_op jit(solution)/shard_map/spread_pair/pallas_call | solution.py:484
  (285 shorter events, 141.4 us)
Async XLA Ops:
  7.2 333.2 %reduce-scatter.4.cloned.1.call-start = ((), (), s32[]{:S(2)}) async-start(), calls=%async_computation.3 | async-start | bytes 5242880 | tf_op jit(solution)/shard_map/reduce_scatter | solution.py:702
  11.8 19.7 %collective-permute-start.1 = (bf16[2,256,512]{2,1,0:T(8,128)(2,1)}, bf16[2,256,512]{2,1,0:T(8,128)(2,1)}, u32[]{:S(2)}, u32[]{:S(2)}) collective-permute-start(bf16[2,256,512]{2,1,0:T(8,128)(2,1)} %get-tuple-element.143), channel_id=1, source_target_pairs={{0,1},{1,2},{2,3},{3,0},{4,5},{5,6},{6,7},{7,4},{8,9},{9,10},{10,1... | collective-permute-start | bytes 1572872 | tf_op jit(solution)/shard_map/ppermute | solution.py:24
  13.8 25.3 %collective-permute-start.2 = (bf16[2,256,512]{2,1,0:T(8,128)(2,1)}, bf16[2,256,512]{2,1,0:T(8,128)(2,1)}, u32[]{:S(2)}, u32[]{:S(2)}) collective-permute-start(bf16[2,256,512]{2,1,0:T(8,128)(2,1)} %get-tuple-element.143), channel_id=1, source_target_pairs={{0,2},{1,3},{2,0},{3,1},{4,6},{5,7},{6,4},{7,5},{8,10},{9,11},{10,... | collective-permute-start | bytes 1572872 | tf_op jit(solution)/shard_map/ppermute | solution.py:24
  16.3 22.9 %collective-permute-start.3 = (bf16[2,256,512]{2,1,0:T(8,128)(2,1)}, bf16[2,256,512]{2,1,0:T(8,128)(2,1)}, u32[]{:S(2)}, u32[]{:S(2)}) collective-permute-start(bf16[2,256,512]{2,1,0:T(8,128)(2,1)} %get-tuple-element.143), channel_id=1, source_target_pairs={{0,3},{1,0},{2,1},{3,2},{4,7},{5,4},{6,5},{7,6},{8,11},{9,8},{10,9... | collective-permute-start | bytes 1572872 | tf_op jit(solution)/shard_map/ppermute | solution.py:24
  17.6 13.0 %collective-permute-start.7 = (s32[256,8]{0,1:T(8,128)S(1)}, s32[256,8]{0,1:T(8,128)S(1)}, u32[]{:S(2)}, u32[]{:S(2)}) collective-permute-start(s32[256,8]{0,1:T(8,128)S(1)} %pad_add_fusion.1), channel_id=1, source_target_pairs={{0,4},{4,0},{1,5},{5,1},{2,6},{6,2},{3,7},{7,3},{8,12},{12,8},{9,1... | collective-permute-start | bytes 24584 | tf_op jit(solution)/shard_map/ppermute | solution.py:24
  19.2 26.9 %collective-permute-start = (bf16[256,1024]{1,0:T(8,128)(2,1)}, bf16[256,1024]{1,0:T(8,128)(2,1)}, u32[]{:S(2)}, u32[]{:S(2)}) collective-permute-start(bf16[256,1024]{1,0:T(8,128)(2,1)} %bitcast), channel_id=1, source_target_pairs={{0,4},{4,0},{1,5},{5,1},{2,6},{6,2},{3,7},{7,3},{8,12},{12,8},{9,1... | collective-permute-start | bytes 1572872 | tf_op jit(solution)/shard_map/ppermute | solution.py:24
  41.0 37.4 %collective-permute-start.4 = (bf16[400,1024]{1,0:T(8,128)(2,1)S(1)}, bf16[400,1024]{1,0:T(8,128)(2,1)S(1)}, u32[]{:S(2)}, u32[]{:S(2)}) collective-permute-start(bf16[400,1024]{1,0:T(8,128)(2,1)S(1)} %copy-done.7), channel_id=1, source_target_pairs={{0,3},{1,0},{2,1},{3,2},{4,7},{5,4},{6,5},{7,6},{8,11},{9,8},{10,9... | collective-permute-start | bytes 2457608 | tf_op jit(solution)/shard_map/ppermute | solution.py:24
  43.9 34.5 %collective-permute-start.5 = (bf16[400,1024]{1,0:T(8,128)(2,1)S(1)}, bf16[400,1024]{1,0:T(8,128)(2,1)S(1)}, u32[]{:S(2)}, u32[]{:S(2)}) collective-permute-start(bf16[400,1024]{1,0:T(8,128)(2,1)S(1)} %copy-done.7), channel_id=1, source_target_pairs={{0,2},{1,3},{2,0},{3,1},{4,6},{5,7},{6,4},{7,5},{8,10},{9,11},{10,... | collective-permute-start | bytes 2457608 | tf_op jit(solution)/shard_map/ppermute | solution.py:24
  43.9 38.6 %collective-permute-start.6 = (bf16[400,1024]{1,0:T(8,128)(2,1)S(1)}, bf16[400,1024]{1,0:T(8,128)(2,1)S(1)}, u32[]{:S(2)}, u32[]{:S(2)}) collective-permute-start(bf16[400,1024]{1,0:T(8,128)(2,1)S(1)} %copy-done.7), channel_id=1, source_target_pairs={{0,1},{1,2},{2,3},{3,0},{4,5},{5,6},{6,7},{7,4},{8,9},{9,10},{10,1... | collective-permute-start | bytes 2457608 | tf_op jit(solution)/shard_map/ppermute | solution.py:24
  44.6 50.3 %collective-permute-start.9 = (bf16[2,4,256,512]{3,2,1,0:T(8,128)(2,1)S(1)}, bf16[2,4,256,512]{3,2,1,0:T(8,128)(2,1)S(1)}, u32[]{:S(2)}, u32[]{:S(2)}) collective-permute-start(bf16[2,4,256,512]{3,2,1,0:T(8,128)(2,1)S(1)} %pad_maximum_fusion.refs_6_.refs_7_), channel_id=1, source_target_pairs={{0,16},{16,32},{32,48},{48,0},{1,17},{17,33},{33,49},{49,1},{2,18}... | collective-permute-start | bytes 6291464 | tf_op jit(solution)/shard_map/ppermute | solution.py:24
  46.1 51.4 %collective-permute-start.11 = (bf16[2,4,256,512]{3,2,1,0:T(8,128)(2,1)S(1)}, bf16[2,4,256,512]{3,2,1,0:T(8,128)(2,1)S(1)}, u32[]{:S(2)}, u32[]{:S(2)}) collective-permute-start(bf16[2,4,256,512]{3,2,1,0:T(8,128)(2,1)S(1)} %pad_maximum_fusion.refs_6_.refs_7_), channel_id=1, source_target_pairs={{0,48},{16,0},{32,16},{48,32},{1,49},{17,1},{33,17},{49,33},{2,50}... | collective-permute-start | bytes 6291464 | tf_op jit(solution)/shard_map/ppermute | solution.py:24
  78.5 25.8 %collective-permute-start.13 = (bf16[4,512,256]{2,1,0:T(8,128)(2,1)S(1)}, bf16[4,512,256]{2,1,0:T(8,128)(2,1)}, u32[]{:S(2)}, u32[]{:S(2)}) collective-permute-start(bf16[4,512,256]{2,1,0:T(8,128)(2,1)S(1)} %constant_dynamic-slice_fusion.15.refs_11_.refs_12_), channel_id=1, source_target_pairs={{0,1},{1,2},{2,3},{3,0},{4,5},{5,6},{6,7},{7,4},{8,9},{9,10},{10,1... | collective-permute-start | bytes 3145736 | tf_op jit(solution)/shard_map/ppermute | solution.py:24
  78.5 26.9 %collective-permute-start.15 = (bf16[4,512,256]{2,1,0:T(8,128)(2,1)S(1)}, bf16[4,512,256]{2,1,0:T(8,128)(2,1)}, u32[]{:S(2)}, u32[]{:S(2)}) collective-permute-start(bf16[4,512,256]{2,1,0:T(8,128)(2,1)S(1)} %constant_dynamic-slice_fusion.15.refs_11_.refs_12_), channel_id=1, source_target_pairs={{0,3},{1,0},{2,1},{3,2},{4,7},{5,4},{6,5},{7,6},{8,11},{9,8},{10,9... | collective-permute-start | bytes 3145736 | tf_op jit(solution)/shard_map/ppermute | solution.py:24
  93.4 24.8 %collective-permute-start.8 = (bf16[512,1024]{1,0:T(8,128)(2,1)}, bf16[512,1024]{1,0:T(8,128)(2,1)}, u32[]{:S(2)}, u32[]{:S(2)}) collective-permute-start(bf16[512,1024]{1,0:T(8,128)(2,1)} %get-tuple-element.63.refs_1_), channel_id=1, source_target_pairs={{0,4},{4,0},{1,5},{5,1},{2,6},{6,2},{3,7},{7,3},{8,12},{12,8},{9,1... | collective-permute-start | bytes 3145736 | tf_op jit(solution)/shard_map/ppermute | solution.py:24
  96.0 26.7 %collective-permute-start.10 = (bf16[1,4,256,512]{3,2,1,0:T(8,128)(2,1)}, bf16[1,4,256,512]{3,2,1,0:T(8,128)(2,1)}, u32[]{:S(2)}, u32[]{:S(2)}) collective-permute-start(bf16[1,4,256,512]{3,2,1,0:T(8,128)(2,1)} %slice.383), channel_id=1, source_target_pairs={{0,16},{16,32},{32,48},{48,0},{1,17},{17,33},{33,49},{49,1},{2,18}... | collective-permute-start | bytes 3145736 | tf_op jit(solution)/shard_map/ppermute | solution.py:24
  98.6 24.6 %collective-permute-start.12 = (bf16[1,4,256,512]{3,2,1,0:T(8,128)(2,1)}, bf16[1,4,256,512]{3,2,1,0:T(8,128)(2,1)S(1)}, u32[]{:S(2)}, u32[]{:S(2)}) collective-permute-start(bf16[1,4,256,512]{3,2,1,0:T(8,128)(2,1)} %slice.384), channel_id=1, source_target_pairs={{0,48},{16,0},{32,16},{48,32},{1,49},{17,1},{33,17},{49,33},{2,50}... | collective-permute-start | bytes 3145736 | tf_op jit(solution)/shard_map/ppermute | solution.py:24
  105.3 12.8 %collective-permute-start.14 = (bf16[2,512,256]{2,1,0:T(8,128)(2,1)S(1)}, bf16[2,512,256]{2,1,0:T(8,128)(2,1)S(1)}, u32[]{:S(2)}, u32[]{:S(2)}) collective-permute-start(bf16[2,512,256]{2,1,0:T(8,128)(2,1)S(1)} %slice.385), channel_id=1, source_target_pairs={{0,1},{1,2},{2,3},{3,0},{4,5},{5,6},{6,7},{7,4},{8,9},{9,10},{10,1... | collective-permute-start | bytes 1572872 | tf_op jit(solution)/shard_map/ppermute | solution.py:24
  143.1 14.4 %collective-permute-start.18 = (bf16[256,1024]{1,0:T(8,128)(2,1)S(1)}, bf16[256,1024]{1,0:T(8,128)(2,1)S(1)}, u32[]{:S(2)}, u32[]{:S(2)}) collective-permute-start(bf16[256,1024]{1,0:T(8,128)(2,1)S(1)} %add_convert_fusion.4), channel_id=1, source_target_pairs={{0,64},{1,65},{2,66},{3,67},{4,68},{5,69},{6,70},{7,71},{8,72},{9,... | collective-permute-start | bytes 1572872 | tf_op jit(solution)/shard_map/ppermute | solution.py:667
  240.6 15.3 %collective-permute-start.25 = (bf16[256,1024]{1,0:T(8,128)(2,1)S(1)}, bf16[256,1024]{1,0:T(8,128)(2,1)S(1)}, u32[]{:S(2)}, u32[]{:S(2)}) collective-permute-start(bf16[256,1024]{1,0:T(8,128)(2,1)S(1)} %fusion.8), channel_id=1, source_target_pairs={{64,0},{65,1},{66,2},{67,3},{68,4},{69,5},{70,6},{71,7},{72,8},{73... | collective-permute-start | bytes 1572872 | tf_op jit(solution)/shard_map/ppermute | solution.py:698
  286.9 91.6 %reduce-scatter.6.cloned.1.call-start = ((), (), s32[]{:S(2)}) async-start(), calls=%async_computation.4 | async-start | bytes 4259840 | tf_op jit(solution)/shard_map/reduce_scatter | solution.py:708
  295.3 26.3 %collective-permute-start.28 = (bf16[512,1024]{1,0:T(8,128)(2,1)}, bf16[512,1024]{1,0:T(8,128)(2,1)S(1)}, u32[]{:S(2)}, u32[]{:S(2)}) collective-permute-start(bf16[512,1024]{1,0:T(8,128)(2,1)} %get-tuple-element.84), channel_id=1, source_target_pairs={{0,16},{16,32},{32,48},{48,0},{1,17},{17,33},{33,49},{49,1},{2,18}... | collective-permute-start | bytes 3145736 | tf_op jit(solution)/shard_map/ppermute | solution.py:24
  296.6 25.0 %collective-permute-start.29 = (bf16[512,1024]{1,0:T(8,128)(2,1)S(1)}, bf16[512,1024]{1,0:T(8,128)(2,1)}, u32[]{:S(2)}, u32[]{:S(2)}) collective-permute-start(bf16[512,1024]{1,0:T(8,128)(2,1)S(1)} %copy-done.40), channel_id=1, source_target_pairs={{0,48},{16,0},{32,16},{48,32},{1,49},{17,1},{33,17},{49,33},{2,50}... | collective-permute-start | bytes 3145736 | tf_op jit(solution)/shard_map/ppermute | solution.py:24
  337.6 89.0 %reduce-scatter.8.cloned.1.call-start = ((), (), s32[]{:S(2)}) async-start(), calls=%async_computation.5 | async-start | bytes 2621440 | tf_op jit(solution)/shard_map/reduce_scatter | solution.py:714
  337.7 48.4 %collective-permute-start.37 = (bf16[1024,1024]{1,0:T(8,128)(2,1)}, bf16[1024,1024]{1,0:T(8,128)(2,1)}, u32[]{:S(2)}, u32[]{:S(2)}) collective-permute-start(bf16[1024,1024]{1,0:T(8,128)(2,1)} %pad_maximum_fusion.1), channel_id=1, source_target_pairs={{0,16},{16,32},{32,48},{48,0},{1,17},{17,33},{33,49},{49,1},{2,18}... | collective-permute-start | bytes 6291464 | tf_op jit(solution)/shard_map/ppermute | solution.py:24
  338.7 47.4 %collective-permute-start.38 = (bf16[1024,1024]{1,0:T(8,128)(2,1)}, bf16[1024,1024]{1,0:T(8,128)(2,1)}, u32[]{:S(2)}, u32[]{:S(2)}) collective-permute-start(bf16[1024,1024]{1,0:T(8,128)(2,1)} %pad_maximum_fusion.2), channel_id=1, source_target_pairs={{0,48},{16,0},{32,16},{48,32},{1,49},{17,1},{33,17},{49,33},{2,50}... | collective-permute-start | bytes 6291464 | tf_op jit(solution)/shard_map/ppermute | solution.py:24
  340.4 41.1 %collective-permute-start.31 = (bf16[4,512,256]{2,1,0:T(8,128)(2,1)}, bf16[4,512,256]{2,1,0:T(8,128)(2,1)S(1)}, u32[]{:S(2)}, u32[]{:S(2)}) collective-permute-start(bf16[4,512,256]{2,1,0:T(8,128)(2,1)} %reduce-scatter.4.cloned.1.call-done), channel_id=1, source_target_pairs={{0,8},{8,0},{1,9},{9,1},{2,10},{10,2},{3,11},{11,3},{4,12},{12,4},... | collective-permute-start | bytes 3145736 | tf_op jit(solution)/shard_map/ppermute | solution.py:24
  378.5 21.9 %collective-permute-start.32 = (bf16[416,1024]{1,0:T(8,128)(2,1)}, bf16[416,1024]{1,0:T(8,128)(2,1)}, u32[]{:S(2)}, u32[]{:S(2)}) collective-permute-start(bf16[416,1024]{1,0:T(8,128)(2,1)} %bitcast.164), channel_id=1, source_target_pairs={{0,8},{8,0},{1,9},{9,1},{2,10},{10,2},{3,11},{11,3},{4,12},{12,4},... | collective-permute-start | bytes 2555912 | tf_op jit(solution)/shard_map/ppermute | solution.py:24
  391.8 65.0 %all-gather.5.cloned.1.call-start = ((), (), s32[]{:S(2)}) async-start(), calls=%async_computation.6 | async-start | bytes 2375680 | tf_op jit(solution)/shard_map/all_gather | solution.py:728
  405.3 20.2 %collective-permute-start.35 = (bf16[232,1024]{1,0:T(8,128)(2,1)S(1)}, bf16[232,1024]{1,0:T(8,128)(2,1)S(1)}, u32[]{:S(2)}, u32[]{:S(2)}) collective-permute-start(bf16[232,1024]{1,0:T(8,128)(2,1)S(1)} %pad_maximum_fusion.9), channel_id=1, source_target_pairs={{0,32},{16,48},{32,0},{48,16},{1,33},{17,49},{33,1},{49,17},{2,34}... | collective-permute-start | bytes 1425416 | tf_op jit(solution)/shard_map/ppermute | solution.py:24
  426.6 63.1 %all-gather.7.cloned.1.call-start = ((), (), s32[]{:S(2)}) async-start(), calls=%async_computation.7 | async-start | bytes 2621440 | tf_op jit(solution)/shard_map/all_gather | solution.py:727
  456.8 38.3 %collective-permute-start.36 = (bf16[4,232,1024]{2,1,0:T(8,128)(2,1)}, bf16[4,232,1024]{2,1,0:T(8,128)(2,1)}, u32[]{:S(2)}, u32[]{:S(2)}) collective-permute-start(bf16[4,232,1024]{2,1,0:T(8,128)(2,1)} %bitcast.148), channel_id=1, source_target_pairs={{0,4},{4,0},{1,5},{5,1},{2,6},{6,2},{3,7},{7,3},{8,12},{12,8},{9,1... | collective-permute-start | bytes 5701640 | tf_op jit(solution)/shard_map/ppermute | solution.py:24
  489.7 12.8 %collective-permute-start.40 = (bf16[4,256,1024]{2,1,0:T(8,128)(2,1)}, bf16[4,256,1024]{2,1,0:T(8,128)(2,1)S(1)}, u32[]{:S(2)}, u32[]{:S(2)}) collective-permute-start(bf16[4,256,1024]{2,1,0:T(8,128)(2,1)} %bitcast.155), channel_id=1, source_target_pairs={{0,4},{4,0},{1,5},{5,1},{2,6},{6,2},{3,7},{7,3},{8,12},{12,8},{9,1... | collective-permute-start | bytes 6291464 | tf_op jit(solution)/shard_map/ppermute | solution.py:24
  (55 other events, 481.9 us)
Sparse Core Ops, SparseCore 0:
  287.1 47.1 reduce-scatter.3
  337.8 40.7 reduce-scatter.5
  391.9 30.9 reduce-scatter.7
  426.7 30.0 all-gather.4
  458.9 30.8 all-gather.6

commit v4 on v3

--- a/solution.py
+++ b/solution.py
@@ -724,9 +724,10 @@
     rest_blocks = [rest(e) for e in range(OWN)]
     rest_sum = scatter3(rest_blocks, "y")
     pair_sum = plus(pair_sum, pp(pair_sum, "zh", 1))
-    pair_all = lax.all_gather(pair_sum, "y")
+    pair_all = ring3(pair_sum, "y")
     rest_all = lax.all_gather(rest_sum, "y")
     rest_far = other(rest_all)
+    pair_all = involute(jnp.stack(pair_all, 0), 0, y_at)
     pair_far = other(pair_all)
     grad_gate, grad_up = spread_pair(pair_all, pair_far)
     grad_down, grad_query, grad_key, grad_value, grad_out = spread_rest(rest_all, rest_far)

time: 526 us -> 517 us (0.983)
  waiting for transfers between devices: 219 us -> 206 us
    all_gather x1 -> x0, waiting for transfers between devices: 32.3 us -> none  [local(): pair_all = lax.all_gather(pair_sum, 'y')]
    all_gather x1, waiting for transfers between devices: 15.5 us -> 34.3 us  [local(): rest_all = lax.all_gather(rest_sum, 'y')]
    ppermute x39 -> x42, starting transfers between devices: 53 us -> 56.3 us  [pp(): lax.ppermute(value, axis, [(i, (i + step) % count) for i in range(count)])]
    unnamed x119 -> x135, local copies, waits for them, and re-layouts: 12.2 us -> 15.1 us
    ppermute x39 -> x42, waiting for transfers between devices: 112 us -> 112 us  [pp(): lax.ppermute(value, axis, [(i, (i + step) % count) for i in range(count)])]
  transfers between devices with their start and end apart: 46 -> 48, of which waited for: 26 -> 25; matrix products, arithmetic and copies ran while one was open for 11% -> 10% of each run, Pallas kernels for 9% -> 9%
where the time goes in v4:
time: 517 us; the launch traced here: 508 us
  waiting for transfers between devices  206 us (40%)
  Pallas kernels  146 us (28%)
  starting transfers between devices  61.3 us (12%)
  other arithmetic  42.2 us (8%)
  local copies, waits for them, and re-layouts  31.1 us (6%)
  between operations  15.1 us (3%)
  matrix products  6.02 us (1%)
    ppermute x42, waiting for transfers between devices, pp(): lax.ppermute(value, axis, [(i, (i + step) % count) for i in range(count)])  112 us
    ppermute x42, starting transfers between devices, pp(): lax.ppermute(value, axis, [(i, (i + step) % count) for i in range(count)])  56.3 us
    pallas_call x2, Pallas kernels, expert_backward(): pl.pallas_call(expert_backward_kernel, in_specs=[whole()] * 5 + [afar()]...  36.1 us
    reduce_scatter x1, waiting for transfers between devices, local(): attn_sum = lax.psum_scatter(attn_grads, 'x', scatter_dimension=0)  34.8 us
    all_gather x1, waiting for transfers between devices, local(): rest_all = lax.all_gather(rest_sum, 'y')  34.3 us
    pallas_call x2, Pallas kernels, attention_backward(): pl.pallas_call(attention_backward_kernel, grid=(2,), in_specs=[rows_spec(...  33 us
    pallas_call x2, Pallas kernels, expert_forward(): pl.pallas_call(functools.partial(expert_forward_kernel, save), in_specs=[...  28.2 us
    pallas_call x2, Pallas kernels, attention_forward(): pl.pallas_call(attention_forward_kernel, grid=(2,), in_specs=[rows_spec(D...  18.6 us
  transfers between devices with their start and end apart: 48, of which 25 were waited for; matrix products, arithmetic and copies ran while one was open for 10% of the time, Pallas kernels for 9%

profile of v4, /device:TPU:1, one launch (start us, length us, event | category | flops | bytes accessed | tf_op | source)
XLA Modules:
  0.0 507.6 jit_solution(7219718301596872724)
XLA Ops:
  7.3 3.4 constant_dynamic-slice_fusion.14
  31.4 7.7 %collective-permute-done.2 = bf16[2,256,512]{2,1,0:T(8,128)(2,1)} collective-permute-done((bf16[2,256,512]{2,1,0:T(8,128)(2,1)}, bf16[2,256,512]{2,1,0:T(8,128)(2,1)}, u32[]{:S(2)}, u32[]{:S(2)}) %collective-permute-start.2) | collective-permute-done | bytes 524320 | tf_op jit(solution)/shard_map/ppermute | solution.py:24
  52.4 26.0 %collective-permute-done.4.refs_3_ = bf16[400,1024]{1,0:T(8,128)(2,1)S(1)} collective-permute-done((bf16[400,1024]{1,0:T(8,128)(2,1)S(1)}, bf16[400,1024]{1,0:T(8,128)(2,1)S(1)}, u32[]{:S(2)}, u32[]{:S(2)}) %collective-permute-start.4) | collective-permute-done | bytes 819232 | tf_op jit(solution)/shard_map/ppermute | solution.py:24
  78.5 3.8 collective-permute-start.15
  84.1 9.3 %attention_forward.2 = (bf16[512,1024]{1,0:T(8,128)(2,1)}, bf16[512,512]{1,0:T(8,128)(2,1)}, bf16[512,512]{1,0:T(8,128)(2,1)}, bf16[512,512]{1,0:T(8,128)(2,1)},...) custom-call(bf16[512,1024]{1,0:T(8,128)(2,1)} %pad_maximum_fusion.3.x_ref.refs_0_, ...), custom_call_target="tpu_custom_call" | custom-call | flops 1 | bytes 1 | tf_op jit(solution)/shard_map/attention_forward/pallas_call | solution.py:210
  100.1 4.1 collective-permute-done.13.refs_12_.refs_13_
  111.5 6.6 %collective-permute-done.14.refs_13_.refs_14_ = bf16[2,512,256]{2,1,0:T(8,128)(2,1)S(1)} collective-permute-done((bf16[2,512,256]{2,1,0:T(8,128)(2,1)S(1)}, bf16[2,512,256]{2,1,0:T(8,128)(2,1)S(1)}, u32[]{:S(2)}, u32[]{:S(2)}) %collective-permute-start.14) | collective-permute-done | bytes 524320 | tf_op jit(solution)/shard_map/ppermute | solution.py:24
  118.2 4.6 collective-permute-done.10.refs_8_.refs_9_
  124.3 13.1 %expert_forward.2 = (f32[512,1024]{1,0:T(8,128)}, bf16[512,1024]{1,0:T(8,128)(2,1)}) custom-call(bf16[512,1024]{1,0:T(8,128)(2,1)} %pad_maximum_fusion.3.x_ref.refs_0_, bf16[512,1024]{1,0:T(8,128)(2,1)} %get-tuple-element.63.refs_1_, bf16[512,1024]{1,0:T(8,128)(2,1)} %collective-permute-done.8.refs_2_, f32[1,1024]{1,0:T(1,128)} %get-tuple-element.152.refs_3_.gain_ref, ...), custom_call_target="tpu_custom_call" | custom-call | flops 1 | bytes 1 | tf_op jit(solution)/shard_map/expert_forward/pallas_call | solution.py:329
  143.1 3.6 collective-permute-start.18
  146.7 10.9 %collective-permute-done.18 = bf16[256,1024]{1,0:T(8,128)(2,1)S(1)} collective-permute-done((bf16[256,1024]{1,0:T(8,128)(2,1)S(1)}, bf16[256,1024]{1,0:T(8,128)(2,1)S(1)}, u32[]{:S(2)}, u32[]{:S(2)}) %collective-permute-start.18) | collective-permute-done | bytes 524320 | tf_op jit(solution)/shard_map/ppermute | solution.py:667
  162.9 9.3 %attention_forward.3 = (bf16[512,1024]{1,0:T(8,128)(2,1)}, bf16[512,512]{1,0:T(8,128)(2,1)}, bf16[512,512]{1,0:T(8,128)(2,1)}, bf16[512,512]{1,0:T(8,128)(2,1)},...) custom-call(bf16[512,1024]{1,0:T(8,128)(2,1)} %maximum_select_fusion.x_ref.refs_0_, ...), custom_call_target="tpu_custom_call" | custom-call | flops 1 | bytes 1 | tf_op jit(solution)/shard_map/attention_forward/pallas_call | solution.py:210
  176.2 15.1 %expert_forward.3 = (f32[512,1024]{1,0:T(8,128)}, bf16[512,1024]{1,0:T(8,128)(2,1)}, bf16[512,1024]{1,0:T(8,128)(2,1)}, f32[512,128]{1,0:T(8,128)}, bf16[512,204...) custom-call(bf16[512,1024]{1,0:T(8,128)(2,1)} %maximum_select_fusion.x_ref.refs_0_, ...), custom_call_target="tpu_custom_call" | custom-call | flops 1 | bytes 1 | tf_op jit(solution)/shard_map/expert_forward/pallas_call | solution.py:329
  196.8 18.1 %expert_backward.2 = (bf16[512,128]{1,0:T(8,128)(2,1)}, bf16[512,1024]{1,0:T(8,128)(2,1)}, bf16[512,2048]{1,0:T(8,128)(2,1)}, bf16[512,2048]{1,0:T(8,128)(2,1)}) custom-call(bf16[512,1024]{1,0:T(8,128)(2,1)} %pad_maximum_fusion.4.refs_0_.grad_ref, bf16[512,1024]{1,0:T(8,128)(2,1)} %get-tuple-element.70.refs_1_, bf16[512,1024]{1,0:T(8,128)(2,1)} %copy-done.19, ...), custom_call_target="tpu_custom_call" | custom-call | flops 1 | bytes 1 | tf_op jit(solution)/shard_map/expert_backward/pallas_call | solution.py:396
  218.9 16.6 %attention_backward.2 = (f32[512,1024]{1,0:T(8,128)}, bf16[512,1024]{1,0:T(8,128)(2,1)}, bf16[512,1024]{1,0:T(8,128)(2,1)}, bf16[512,1024]{1,0:T(8,128)(2,1)}, f32[1,1024]{1,0:T(1,128)}) custom-call(bf16[512,1024]{1,0:T(8,128)(2,1)} %pad_maximum_fusion.4.refs_0_.grad_ref, f32[512,1024]{1,0:T(8,128)} %get-tuple-element.69.h_ref, ...), custom_call_target="tpu_custom_call" | custom-call | flops 1 | bytes 1 | tf_op jit(solution)/shard_map/attention_backward/pallas_call | solution.py:596
  242.9 14.0 %collective-permute-done.25 = bf16[256,1024]{1,0:T(8,128)(2,1)S(1)} collective-permute-done((bf16[256,1024]{1,0:T(8,128)(2,1)S(1)}, bf16[256,1024]{1,0:T(8,128)(2,1)S(1)}, u32[]{:S(2)}, u32[]{:S(2)}) %collective-permute-start.25) | collective-permute-done | bytes 524320 | tf_op jit(solution)/shard_map/ppermute | solution.py:698
  261.3 18.1 %expert_backward.3 = (bf16[512,128]{1,0:T(8,128)(2,1)}, bf16[512,1024]{1,0:T(8,128)(2,1)}, bf16[512,2048]{1,0:T(8,128)(2,1)}, bf16[512,2048]{1,0:T(8,128)(2,1)}) custom-call(bf16[512,1024]{1,0:T(8,128)(2,1)} %maximum_select_fusion.1.refs_0_.grad_ref, bf16[512,1024]{1,0:T(8,128)(2,1)} %get-tuple-element.70.refs_1_, bf16[512,1024]{1,0:T(8,128)(2,1)} %copy-done.19, ...), custom_call_target="tpu_custom_call" | custom-call | flops 1 | bytes 1 | tf_op jit(solution)/shard_map/expert_backward/pallas_call | solution.py:396
  279.4 3.9 expert_grads.2
  283.4 4.6 convolution_convert_fusion
  288.1 7.9 %expert_grads.3 = bf16[3,1024,1024]{2,1,0:T(8,128)(2,1)} custom-call(bf16[512,1024]{1,0:T(8,128)(2,1)} %get-tuple-element.86.n_ref, bf16[512,2048]{1,0:T(8,128)(2,1)} %get-tuple-element.82.a_ref, bf16[512,2048]{1,0:T(8,128)(2,1)} %get-tuple-element.83.b_ref), custom_call_target="tpu_custom_call" | custom-call | flops 1 | bytes 1 | tf_op jit(solution)/shard_map/expert_grads/pallas_call | solution.py:435
  301.7 16.5 %attention_backward.3 = (f32[512,1024]{1,0:T(8,128)}, bf16[512,1024]{1,0:T(8,128)(2,1)}, bf16[512,1024]{1,0:T(8,128)(2,1)}, bf16[512,1024]{1,0:T(8,128)(2,1)}, f32[1,1024]{1,0:T(1,128)}) custom-call(bf16[512,1024]{1,0:T(8,128)(2,1)} %maximum_select_fusion.1.refs_0_.grad_ref, f32[512,1024]{1,0:T(8,128)} %get-tuple-element.69.h_ref, ...), custom_call_target="tpu_custom_call" | custom-call | flops 1 | bytes 1 | tf_op jit(solution)/shard_map/attention_backward/pallas_call | solution.py:596
  318.2 4.3 collective-permute-done.28
  332.7 5.9 %attention_grads.1 = bf16[4,416,1024]{2,1,0:T(8,128)(2,1)} custom-call(bf16[512,1024]{1,0:T(8,128)(2,1)} %get-tuple-element.95.n_ref, bf16[512,1024]{1,0:T(8,128)(2,1)} %get-tuple-element.97.qkv_ref, bf16[512,512]{1,0:T(8,128)(2,1)} %get-tuple-element.98.o_ref, bf16[512,1024]{1,0:T(8,128)(2,1)} %get-tuple-element.99.a_ref, ...), custom_call_target="tpu_custom_call" | custom-call | flops 1 | bytes 1 | tf_op jit(solution)/shard_map/attention_grads/pallas_call | solution.py:455
  344.7 34.8 %reduce-scatter.6.cloned.1.call-done = bf16[1,416,1024]{2,1,0:T(8,128)(2,1)} async-done(((bf16[4,416,1024]{2,1,0:T(8,128)(2,1)}), bf16[1,416,1024]{2,1,0:T(8,128)(2,1)}) %reduce-scatter.6.cloned.1.call-update) | async-done | bytes 851984 | tf_op jit(solution)/shard_map/reduce_scatter | solution.py:708
  387.1 5.6 %fusion.1 = bf16[1024,1024]{1,0:T(8,128)(2,1)} fusion(bf16[1024,1024]{1,0:T(8,128)(2,1)} %collective-permute-done.38, bf16[1024,1024]{1,0:T(8,128)(2,1)} %collective-permute-done.37, bf16[3,1024,1024]{2,1,0:T(8,128)(2,1)} %expert_grads.3), kind=kLoop, calls=%fused_computation.2 | loop fusion | flops 6291456 | bytes 8388608 | tf_op jit(solution)/shard_map/convert_element_type | solution.py:713
  392.9 8.5 %collective-permute-done.32 = bf16[416,1024]{1,0:T(8,128)(2,1)} collective-permute-done((bf16[416,1024]{1,0:T(8,128)(2,1)}, bf16[416,1024]{1,0:T(8,128)(2,1)}, u32[]{:S(2)}, u32[]{:S(2)}) %collective-permute-start.32) | collective-permute-done | bytes 852000 | tf_op jit(solution)/shard_map/ppermute | solution.py:24
  407.9 7.6 %collective-permute-done.33 = bf16[232,1024]{1,0:T(8,128)(2,1)S(1)} collective-permute-done((bf16[232,1024]{1,0:T(8,128)(2,1)S(1)}, bf16[232,1024]{1,0:T(8,128)(2,1)S(1)}, u32[]{:S(2)}, u32[]{:S(2)}) %collective-permute-start.33) | collective-permute-done | bytes 475168 | tf_op jit(solution)/shard_map/ppermute | solution.py:24
  415.5 11.0 %collective-permute-done.35 = bf16[232,1024]{1,0:T(8,128)(2,1)S(1)} collective-permute-done((bf16[232,1024]{1,0:T(8,128)(2,1)S(1)}, bf16[232,1024]{1,0:T(8,128)(2,1)S(1)}, u32[]{:S(2)}, u32[]{:S(2)}) %collective-permute-start.35) | collective-permute-done | bytes 475168 | tf_op jit(solution)/shard_map/ppermute | solution.py:24
  430.6 9.7 %collective-permute-done.39 = bf16[256,1024]{1,0:T(8,128)(2,1)S(1)} collective-permute-done((bf16[256,1024]{1,0:T(8,128)(2,1)}, bf16[256,1024]{1,0:T(8,128)(2,1)S(1)}, u32[]{:S(2)}, u32[]{:S(2)}) %collective-permute-start.39) | collective-permute-done | bytes 524320 | tf_op jit(solution)/shard_map/ppermute | solution.py:24
  443.8 34.3 %all-gather.3.cloned.1.call-done = bf16[928,1024]{1,0:T(8,128)(2,1)} async-done(((bf16[232,1024]{1,0:T(8,128)(2,1)}), bf16[928,1024]{1,0:T(8,128)(2,1)}) %all-gather.3.cloned.1.call-update) | async-done | bytes 1900560 | tf_op jit(solution)/shard_map/all_gather | solution.py:728
  485.0 5.6 %spread_rest.1 = (f32[8,512,256]{2,1,0:T(8,128)}, f32[256,1024]{1,0:T(8,128)}, f32[256,512]{1,0:T(8,128)}, f32[256,512]{1,0:T(8,128)}, f32[2,128,1024]{2,1,0:T(8,128)}) custom-call(bf16[4,232,1024]{2,1,0:T(8,128)(2,1)} %bitcast.159, bf16[4,232,1024]{2,1,0:T(8,128)(2,1)} %collective-permute-done.36.low_far.attn_far.mix_far, bf16[4,232,1024]{2,1,0:T(8,128)(2,1)} %bitcast.160, ...), custom_call_target="tpu_custom_call" | custom-call | flops 1 | bytes 1 | tf_op jit(solution)/shard_map/spread_rest/pallas_call | solution.py:521
  493.9 7.0 %spread_pair.1 = (f32[256,8,512]{2,1,0:T(8,128)}, f32[256,8,512]{2,1,0:T(8,128)}) custom-call(bf16[4,256,1024]{2,1,0:T(8,128)(2,1)} %copy-done.17, bf16[4,256,1024]{2,1,0:T(8,128)(2,1)} %copy-done.21), custom_call_target="tpu_custom_call" | custom-call | flops 1 | bytes 1 | tf_op jit(solution)/shard_map/spread_pair/pallas_call | solution.py:484
  (306 shorter events, 141.2 us)
Async XLA Ops:
  7.2 334.2 %reduce-scatter.4.cloned.1.call-start = ((), (), s32[]{:S(2)}) async-start(), calls=%async_computation.3 | async-start | bytes 5242880 | tf_op jit(solution)/shard_map/reduce_scatter | solution.py:702
  11.8 19.6 %collective-permute-start.1 = (bf16[2,256,512]{2,1,0:T(8,128)(2,1)}, bf16[2,256,512]{2,1,0:T(8,128)(2,1)}, u32[]{:S(2)}, u32[]{:S(2)}) collective-permute-start(bf16[2,256,512]{2,1,0:T(8,128)(2,1)} %get-tuple-element.143), channel_id=1, source_target_pairs={{0,1},{1,2},{2,3},{3,0},{4,5},{5,6},{6,7},{7,4},{8,9},{9,10},{10,1... | collective-permute-start | bytes 1572872 | tf_op jit(solution)/shard_map/ppermute | solution.py:24
  13.8 25.3 %collective-permute-start.2 = (bf16[2,256,512]{2,1,0:T(8,128)(2,1)}, bf16[2,256,512]{2,1,0:T(8,128)(2,1)}, u32[]{:S(2)}, u32[]{:S(2)}) collective-permute-start(bf16[2,256,512]{2,1,0:T(8,128)(2,1)} %get-tuple-element.143), channel_id=1, source_target_pairs={{0,2},{1,3},{2,0},{3,1},{4,6},{5,7},{6,4},{7,5},{8,10},{9,11},{10,... | collective-permute-start | bytes 1572872 | tf_op jit(solution)/shard_map/ppermute | solution.py:24
  16.3 22.9 %collective-permute-start.3 = (bf16[2,256,512]{2,1,0:T(8,128)(2,1)}, bf16[2,256,512]{2,1,0:T(8,128)(2,1)}, u32[]{:S(2)}, u32[]{:S(2)}) collective-permute-start(bf16[2,256,512]{2,1,0:T(8,128)(2,1)} %get-tuple-element.143), channel_id=1, source_target_pairs={{0,3},{1,0},{2,1},{3,2},{4,7},{5,4},{6,5},{7,6},{8,11},{9,8},{10,9... | collective-permute-start | bytes 1572872 | tf_op jit(solution)/shard_map/ppermute | solution.py:24
  17.6 13.0 %collective-permute-start.7 = (s32[256,8]{0,1:T(8,128)S(1)}, s32[256,8]{0,1:T(8,128)S(1)}, u32[]{:S(2)}, u32[]{:S(2)}) collective-permute-start(s32[256,8]{0,1:T(8,128)S(1)} %pad_add_fusion.1), channel_id=1, source_target_pairs={{0,4},{4,0},{1,5},{5,1},{2,6},{6,2},{3,7},{7,3},{8,12},{12,8},{9,1... | collective-permute-start | bytes 24584 | tf_op jit(solution)/shard_map/ppermute | solution.py:24
  19.2 26.9 %collective-permute-start = (bf16[256,1024]{1,0:T(8,128)(2,1)}, bf16[256,1024]{1,0:T(8,128)(2,1)}, u32[]{:S(2)}, u32[]{:S(2)}) collective-permute-start(bf16[256,1024]{1,0:T(8,128)(2,1)} %bitcast), channel_id=1, source_target_pairs={{0,4},{4,0},{1,5},{5,1},{2,6},{6,2},{3,7},{7,3},{8,12},{12,8},{9,1... | collective-permute-start | bytes 1572872 | tf_op jit(solution)/shard_map/ppermute | solution.py:24
  41.0 37.4 %collective-permute-start.4 = (bf16[400,1024]{1,0:T(8,128)(2,1)S(1)}, bf16[400,1024]{1,0:T(8,128)(2,1)S(1)}, u32[]{:S(2)}, u32[]{:S(2)}) collective-permute-start(bf16[400,1024]{1,0:T(8,128)(2,1)S(1)} %copy-done.7), channel_id=1, source_target_pairs={{0,3},{1,0},{2,1},{3,2},{4,7},{5,4},{6,5},{7,6},{8,11},{9,8},{10,9... | collective-permute-start | bytes 2457608 | tf_op jit(solution)/shard_map/ppermute | solution.py:24
  43.9 34.5 %collective-permute-start.5 = (bf16[400,1024]{1,0:T(8,128)(2,1)S(1)}, bf16[400,1024]{1,0:T(8,128)(2,1)S(1)}, u32[]{:S(2)}, u32[]{:S(2)}) collective-permute-start(bf16[400,1024]{1,0:T(8,128)(2,1)S(1)} %copy-done.7), channel_id=1, source_target_pairs={{0,2},{1,3},{2,0},{3,1},{4,6},{5,7},{6,4},{7,5},{8,10},{9,11},{10,... | collective-permute-start | bytes 2457608 | tf_op jit(solution)/shard_map/ppermute | solution.py:24
  43.9 38.6 %collective-permute-start.6 = (bf16[400,1024]{1,0:T(8,128)(2,1)S(1)}, bf16[400,1024]{1,0:T(8,128)(2,1)S(1)}, u32[]{:S(2)}, u32[]{:S(2)}) collective-permute-start(bf16[400,1024]{1,0:T(8,128)(2,1)S(1)} %copy-done.7), channel_id=1, source_target_pairs={{0,1},{1,2},{2,3},{3,0},{4,5},{5,6},{6,7},{7,4},{8,9},{9,10},{10,1... | collective-permute-start | bytes 2457608 | tf_op jit(solution)/shard_map/ppermute | solution.py:24
  44.6 50.3 %collective-permute-start.9 = (bf16[2,4,256,512]{3,2,1,0:T(8,128)(2,1)S(1)}, bf16[2,4,256,512]{3,2,1,0:T(8,128)(2,1)S(1)}, u32[]{:S(2)}, u32[]{:S(2)}) collective-permute-start(bf16[2,4,256,512]{3,2,1,0:T(8,128)(2,1)S(1)} %pad_maximum_fusion.refs_6_.refs_7_), channel_id=1, source_target_pairs={{0,16},{16,32},{32,48},{48,0},{1,17},{17,33},{33,49},{49,1},{2,18}... | collective-permute-start | bytes 6291464 | tf_op jit(solution)/shard_map/ppermute | solution.py:24
  46.1 51.4 %collective-permute-start.11 = (bf16[2,4,256,512]{3,2,1,0:T(8,128)(2,1)S(1)}, bf16[2,4,256,512]{3,2,1,0:T(8,128)(2,1)S(1)}, u32[]{:S(2)}, u32[]{:S(2)}) collective-permute-start(bf16[2,4,256,512]{3,2,1,0:T(8,128)(2,1)S(1)} %pad_maximum_fusion.refs_6_.refs_7_), channel_id=1, source_target_pairs={{0,48},{16,0},{32,16},{48,32},{1,49},{17,1},{33,17},{49,33},{2,50}... | collective-permute-start | bytes 6291464 | tf_op jit(solution)/shard_map/ppermute | solution.py:24
  78.5 25.8 %collective-permute-start.13 = (bf16[4,512,256]{2,1,0:T(8,128)(2,1)S(1)}, bf16[4,512,256]{2,1,0:T(8,128)(2,1)}, u32[]{:S(2)}, u32[]{:S(2)}) collective-permute-start(bf16[4,512,256]{2,1,0:T(8,128)(2,1)S(1)} %constant_dynamic-slice_fusion.16.refs_11_.refs_12_), channel_id=1, source_target_pairs={{0,1},{1,2},{2,3},{3,0},{4,5},{5,6},{6,7},{7,4},{8,9},{9,10},{10,1... | collective-permute-start | bytes 3145736 | tf_op jit(solution)/shard_map/ppermute | solution.py:24
  78.5 26.9 %collective-permute-start.15 = (bf16[4,512,256]{2,1,0:T(8,128)(2,1)S(1)}, bf16[4,512,256]{2,1,0:T(8,128)(2,1)}, u32[]{:S(2)}, u32[]{:S(2)}) collective-permute-start(bf16[4,512,256]{2,1,0:T(8,128)(2,1)S(1)} %constant_dynamic-slice_fusion.16.refs_11_.refs_12_), channel_id=1, source_target_pairs={{0,3},{1,0},{2,1},{3,2},{4,7},{5,4},{6,5},{7,6},{8,11},{9,8},{10,9... | collective-permute-start | bytes 3145736 | tf_op jit(solution)/shard_map/ppermute | solution.py:24
  93.4 24.8 %collective-permute-start.8 = (bf16[512,1024]{1,0:T(8,128)(2,1)}, bf16[512,1024]{1,0:T(8,128)(2,1)}, u32[]{:S(2)}, u32[]{:S(2)}) collective-permute-start(bf16[512,1024]{1,0:T(8,128)(2,1)} %get-tuple-element.63.refs_1_), channel_id=1, source_target_pairs={{0,4},{4,0},{1,5},{5,1},{2,6},{6,2},{3,7},{7,3},{8,12},{12,8},{9,1... | collective-permute-start | bytes 3145736 | tf_op jit(solution)/shard_map/ppermute | solution.py:24
  96.0 26.7 %collective-permute-start.10 = (bf16[1,4,256,512]{3,2,1,0:T(8,128)(2,1)}, bf16[1,4,256,512]{3,2,1,0:T(8,128)(2,1)}, u32[]{:S(2)}, u32[]{:S(2)}) collective-permute-start(bf16[1,4,256,512]{3,2,1,0:T(8,128)(2,1)} %slice.383), channel_id=1, source_target_pairs={{0,16},{16,32},{32,48},{48,0},{1,17},{17,33},{33,49},{49,1},{2,18}... | collective-permute-start | bytes 3145736 | tf_op jit(solution)/shard_map/ppermute | solution.py:24
  98.7 24.6 %collective-permute-start.12 = (bf16[1,4,256,512]{3,2,1,0:T(8,128)(2,1)}, bf16[1,4,256,512]{3,2,1,0:T(8,128)(2,1)S(1)}, u32[]{:S(2)}, u32[]{:S(2)}) collective-permute-start(bf16[1,4,256,512]{3,2,1,0:T(8,128)(2,1)} %slice.384), channel_id=1, source_target_pairs={{0,48},{16,0},{32,16},{48,32},{1,49},{17,1},{33,17},{49,33},{2,50}... | collective-permute-start | bytes 3145736 | tf_op jit(solution)/shard_map/ppermute | solution.py:24
  105.3 12.8 %collective-permute-start.14 = (bf16[2,512,256]{2,1,0:T(8,128)(2,1)S(1)}, bf16[2,512,256]{2,1,0:T(8,128)(2,1)S(1)}, u32[]{:S(2)}, u32[]{:S(2)}) collective-permute-start(bf16[2,512,256]{2,1,0:T(8,128)(2,1)S(1)} %slice.385), channel_id=1, source_target_pairs={{0,1},{1,2},{2,3},{3,0},{4,5},{5,6},{6,7},{7,4},{8,9},{9,10},{10,1... | collective-permute-start | bytes 1572872 | tf_op jit(solution)/shard_map/ppermute | solution.py:24
  143.1 14.5 %collective-permute-start.18 = (bf16[256,1024]{1,0:T(8,128)(2,1)S(1)}, bf16[256,1024]{1,0:T(8,128)(2,1)S(1)}, u32[]{:S(2)}, u32[]{:S(2)}) collective-permute-start(bf16[256,1024]{1,0:T(8,128)(2,1)S(1)} %add_convert_fusion.4), channel_id=1, source_target_pairs={{0,64},{1,65},{2,66},{3,67},{4,68},{5,69},{6,70},{7,71},{8,72},{9,... | collective-permute-start | bytes 1572872 | tf_op jit(solution)/shard_map/ppermute | solution.py:667
  241.6 15.3 %collective-permute-start.25 = (bf16[256,1024]{1,0:T(8,128)(2,1)S(1)}, bf16[256,1024]{1,0:T(8,128)(2,1)S(1)}, u32[]{:S(2)}, u32[]{:S(2)}) collective-permute-start(bf16[256,1024]{1,0:T(8,128)(2,1)S(1)} %fusion.8), channel_id=1, source_target_pairs={{64,0},{65,1},{66,2},{67,3},{68,4},{69,5},{70,6},{71,7},{72,8},{73... | collective-permute-start | bytes 1572872 | tf_op jit(solution)/shard_map/ppermute | solution.py:698
  288.0 91.5 %reduce-scatter.6.cloned.1.call-start = ((), (), s32[]{:S(2)}) async-start(), calls=%async_computation.4 | async-start | bytes 4259840 | tf_op jit(solution)/shard_map/reduce_scatter | solution.py:708
  296.3 26.2 %collective-permute-start.28 = (bf16[512,1024]{1,0:T(8,128)(2,1)}, bf16[512,1024]{1,0:T(8,128)(2,1)S(1)}, u32[]{:S(2)}, u32[]{:S(2)}) collective-permute-start(bf16[512,1024]{1,0:T(8,128)(2,1)} %get-tuple-element.84), channel_id=1, source_target_pairs={{0,16},{16,32},{32,48},{48,0},{1,17},{17,33},{33,49},{49,1},{2,18}... | collective-permute-start | bytes 3145736 | tf_op jit(solution)/shard_map/ppermute | solution.py:24
  297.6 24.9 %collective-permute-start.29 = (bf16[512,1024]{1,0:T(8,128)(2,1)S(1)}, bf16[512,1024]{1,0:T(8,128)(2,1)}, u32[]{:S(2)}, u32[]{:S(2)}) collective-permute-start(bf16[512,1024]{1,0:T(8,128)(2,1)S(1)} %copy-done.45), channel_id=1, source_target_pairs={{0,48},{16,0},{32,16},{48,32},{1,49},{17,1},{33,17},{49,33},{2,50}... | collective-permute-start | bytes 3145736 | tf_op jit(solution)/shard_map/ppermute | solution.py:24
  338.6 89.0 %reduce-scatter.8.cloned.1.call-start = ((), (), s32[]{:S(2)}) async-start(), calls=%async_computation.5 | async-start | bytes 2621440 | tf_op jit(solution)/shard_map/reduce_scatter | solution.py:714
  338.6 48.4 %collective-permute-start.37 = (bf16[1024,1024]{1,0:T(8,128)(2,1)}, bf16[1024,1024]{1,0:T(8,128)(2,1)}, u32[]{:S(2)}, u32[]{:S(2)}) collective-permute-start(bf16[1024,1024]{1,0:T(8,128)(2,1)} %pad_maximum_fusion.1), channel_id=1, source_target_pairs={{0,16},{16,32},{32,48},{48,0},{1,17},{17,33},{33,49},{49,1},{2,18}... | collective-permute-start | bytes 6291464 | tf_op jit(solution)/shard_map/ppermute | solution.py:24
  339.7 47.4 %collective-permute-start.38 = (bf16[1024,1024]{1,0:T(8,128)(2,1)}, bf16[1024,1024]{1,0:T(8,128)(2,1)}, u32[]{:S(2)}, u32[]{:S(2)}) collective-permute-start(bf16[1024,1024]{1,0:T(8,128)(2,1)} %pad_maximum_fusion.2), channel_id=1, source_target_pairs={{0,48},{16,0},{32,16},{48,32},{1,49},{17,1},{33,17},{49,33},{2,50}... | collective-permute-start | bytes 6291464 | tf_op jit(solution)/shard_map/ppermute | solution.py:24
  341.4 41.2 %collective-permute-start.31 = (bf16[4,512,256]{2,1,0:T(8,128)(2,1)}, bf16[4,512,256]{2,1,0:T(8,128)(2,1)S(1)}, u32[]{:S(2)}, u32[]{:S(2)}) collective-permute-start(bf16[4,512,256]{2,1,0:T(8,128)(2,1)} %reduce-scatter.4.cloned.1.call-done), channel_id=1, source_target_pairs={{0,8},{8,0},{1,9},{9,1},{2,10},{10,2},{3,11},{11,3},{4,12},{12,4},... | collective-permute-start | bytes 3145736 | tf_op jit(solution)/shard_map/ppermute | solution.py:24
  379.5 21.9 %collective-permute-start.32 = (bf16[416,1024]{1,0:T(8,128)(2,1)}, bf16[416,1024]{1,0:T(8,128)(2,1)}, u32[]{:S(2)}, u32[]{:S(2)}) collective-permute-start(bf16[416,1024]{1,0:T(8,128)(2,1)} %bitcast.172), channel_id=1, source_target_pairs={{0,8},{8,0},{1,9},{9,1},{2,10},{10,2},{3,11},{11,3},{4,12},{12,4},... | collective-permute-start | bytes 2555912 | tf_op jit(solution)/shard_map/ppermute | solution.py:24
  392.7 85.4 %all-gather.3.cloned.1.call-start = ((), (), s32[]{:S(2)}) async-start(), calls=%async_computation.6 | async-start | bytes 2375680 | tf_op jit(solution)/shard_map/all_gather | solution.py:728
  406.3 20.2 %collective-permute-start.35 = (bf16[232,1024]{1,0:T(8,128)(2,1)S(1)}, bf16[232,1024]{1,0:T(8,128)(2,1)S(1)}, u32[]{:S(2)}, u32[]{:S(2)}) collective-permute-start(bf16[232,1024]{1,0:T(8,128)(2,1)S(1)} %pad_maximum_fusion.9), channel_id=1, source_target_pairs={{0,32},{16,48},{32,0},{48,16},{1,33},{17,49},{33,1},{49,17},{2,34}... | collective-permute-start | bytes 1425416 | tf_op jit(solution)/shard_map/ppermute | solution.py:24
  441.5 37.8 %collective-permute-start.40 = (bf16[256,1024]{1,0:T(8,128)(2,1)S(1)}, bf16[256,1024]{1,0:T(8,128)(2,1)S(1)}, u32[]{:S(2)}, u32[]{:S(2)}) collective-permute-start(bf16[256,1024]{1,0:T(8,128)(2,1)S(1)} %add_convert_fusion.2), channel_id=1, source_target_pairs={{0,48},{16,0},{32,16},{48,32},{1,49},{17,1},{33,17},{49,33},{2,50}... | collective-permute-start | bytes 1572872 | tf_op jit(solution)/shard_map/ppermute | solution.py:24
  442.3 37.0 %collective-permute-start.41 = (bf16[256,1024]{1,0:T(8,128)(2,1)S(1)}, bf16[256,1024]{1,0:T(8,128)(2,1)S(1)}, u32[]{:S(2)}, u32[]{:S(2)}) collective-permute-start(bf16[256,1024]{1,0:T(8,128)(2,1)S(1)} %add_convert_fusion.2), channel_id=1, source_target_pairs={{0,32},{16,48},{32,0},{48,16},{1,33},{17,49},{33,1},{49,17},{2,34}... | collective-permute-start | bytes 1572872 | tf_op jit(solution)/shard_map/ppermute | solution.py:24
  443.8 35.6 %collective-permute-start.42 = (bf16[256,1024]{1,0:T(8,128)(2,1)S(1)}, bf16[256,1024]{1,0:T(8,128)(2,1)S(1)}, u32[]{:S(2)}, u32[]{:S(2)}) collective-permute-start(bf16[256,1024]{1,0:T(8,128)(2,1)S(1)} %add_convert_fusion.2), channel_id=1, source_target_pairs={{0,16},{16,32},{32,48},{48,0},{1,17},{17,33},{33,49},{49,1},{2,18}... | collective-permute-start | bytes 1572872 | tf_op jit(solution)/shard_map/ppermute | solution.py:24
  (62 other events, 457.3 us)
Sparse Core Ops, SparseCore 0:
  288.1 47.1 reduce-scatter.3
  338.7 40.7 reduce-scatter.5
  392.9 31.0 reduce-scatter.7
  427.7 50.3 all-gather.2
